TPU v7x, 256 devices: a whole 4x4x8 slice. The times are simulated.
256 devices in a mesh: member: 8 (over z_hi, core), grid: 32 (over y, z_lo, x).
Axes of the slice: x: 4, y: 4, z: 8 (z_hi: 4, z_lo: 2; z = z_hi * 2 + z_lo), core: 2. Of those that a mesh axis runs over, the one named last changes fastest.
Arguments:
- inputs: bfloat16 [8, 8192, 1024], P('member', 'grid'), may hold values from -6 to 6
- norm_gain: float32 [1024], replicated, may hold values from 0.25 to 1.75
- w_query: bfloat16 [1024, 1024], replicated, may hold values from -0.1875 to 0.1875
- w_key: bfloat16 [1024, 1024], replicated, may hold values from -0.1875 to 0.1875
- w_value: bfloat16 [1024, 1024], replicated, may hold values from -0.1875 to 0.1875
- w_out: bfloat16 [1024, 1024], replicated, may hold values from -0.1875 to 0.1875
- w_decode: bfloat16 [1024, 128], replicated, may hold values from -0.1875 to 0.1875
- point_node: int32 [32768], P('grid'), may hold values from 0 to 8191, as said below
- truth: float32 [128, 32768], P(None, 'grid'), may hold values from -6 to 6
Outputs:
- crps_terms: float32 [8, 128, 32768], P('member', None, 'grid')
- grad_value: float32 [1024, 1024], P('grid', 'member')
Inputs may be any that keep to these rules, and one draw needn't show every extreme that they name: `point_node`: the grid points of the r-th block of 1024 read nodes of the r-th band r * 256 to (r + 1) * 256 - 1.
All inputs are finite; a program needn't handle non-finite values.
Results may differ from a plain program's by a relative error of at most 0.035.
Values may be sent and summed in bfloat16 or wider, within the bound.
No kernel may reach another device: no remote copies, remote signals or barrier semaphores. Data moves between devices by JAX's collectives and lax.ppermute only.
A program may use at most 64 MiB of HBM per device.

v0:
```python
import jax
import jax.numpy as jnp
from jax import lax
from jax.sharding import PartitionSpec as P

HD = 64


def extended(value, sides, width):
    for axis, dim in sides:
        size, length = (lax.axis_size(axis), value.shape[dim])
        up = [(i, (i + 1) % size) for i in range(size - 1)]
        down = [(j, i) for i, j in up]
        last = lax.slice_in_dim(value, length - width, length, axis=dim)
        initial = lax.slice_in_dim(value, 0, width, axis=dim)
        before = lax.ppermute(last, axis, up)
        after = lax.ppermute(initial, axis, down)
        value = jnp.concatenate([before, value, after], axis=dim)
    return value


def rms_normed(states, norm_gain):
    floats = states.astype(jnp.float32)
    meansq = jnp.mean(floats * floats, axis=-1, keepdims=True) + 1e-05
    return (floats * lax.rsqrt(meansq) * norm_gain).astype(jnp.bfloat16)


def smooth_abs(values):
    return jnp.sqrt(values * values + 0.25)


def smooth_slope(values):
    return values / jnp.sqrt(values * values + 0.25)


def project(normed, weight):
    return jnp.dot(normed, weight, preferred_element_type=jnp.float32).astype(jnp.bfloat16)


def body(inputs, norm_gain, w_query, w_key, w_value, w_out, w_decode, point_node, truth):
    states = inputs[0]
    node_rows = states.shape[0]
    width = states.shape[1]
    reach = node_rows // 2
    head_size = HD
    heads = width // head_size
    band_index = lax.axis_index("grid")
    node_count = node_rows * lax.axis_size("grid")
    normed = rms_normed(states, norm_gain)
    queries = project(normed, w_query)
    stacked = jnp.stack([project(normed, w_key), project(normed, w_value)])
    widened = extended(stacked, (("grid", 1),), reach)
    key_rows = widened[0]
    value_rows = widened[1]
    span = node_rows + 2 * reach
    scores = (
        jnp.einsum(
            "qhd,khd->hqk",
            queries.reshape(node_rows, heads, head_size),
            key_rows.reshape(span, heads, head_size),
            preferred_element_type=jnp.float32,
        )
        * 0.125
    )
    query_pos = jnp.arange(node_rows)[:, None]
    key_pos = jnp.arange(span)[None, :]
    global_pos = band_index * node_rows + key_pos - reach
    valid = (
        (jnp.abs(key_pos - query_pos - reach) <= reach)
        & (global_pos >= 0)
        & (global_pos < node_count)
    )
    scores = jnp.where(valid[None], scores, -1e30)
    row_max = jnp.max(scores, axis=-1, keepdims=True)
    weights = jnp.exp(scores - row_max)
    weights = (weights / jnp.sum(weights, axis=-1, keepdims=True)).astype(jnp.bfloat16)
    mixed = jnp.einsum(
        "hqk,khd->qhd",
        weights,
        value_rows.reshape(span, heads, head_size),
        preferred_element_type=jnp.float32,
    )
    mixed = mixed.reshape(node_rows, width).astype(jnp.bfloat16)
    projected = jnp.dot(mixed, w_out, preferred_element_type=jnp.float32)
    hidden = (states.astype(jnp.float32) + projected).astype(jnp.bfloat16)
    decoded = jnp.dot(hidden, w_decode, preferred_element_type=jnp.float32)
    local_node = point_node - band_index * node_rows
    selector = (local_node[:, None] == jnp.arange(node_rows)[None, :]).astype(jnp.float32)
    pred = jnp.dot(decoded.T, selector.T, precision=lax.Precision.HIGHEST)
    differ = pred[None] - lax.all_gather(pred[None], "member", axis=0, tiled=True)
    spread = jnp.sum(smooth_abs(differ), axis=0)
    slope_total = jnp.sum(smooth_slope(differ), axis=0)
    member_count = lax.axis_size("member")
    error_value = pred - truth
    crps_terms = smooth_abs(error_value) - spread / (2.0 * (member_count - 1))
    loss_grad = (smooth_slope(error_value) - slope_total / (member_count - 1)) / member_count
    node_grad = jnp.dot(loss_grad, selector, precision=lax.Precision.HIGHEST)
    hidden_grad = jnp.dot(
        node_grad.T, w_decode.astype(jnp.float32).T, precision=lax.Precision.HIGHEST
    ).astype(jnp.bfloat16)
    mixed_grad = jnp.dot(hidden_grad, w_out.T, preferred_element_type=jnp.float32).astype(
        jnp.bfloat16
    )
    contrib = jnp.einsum(
        "hqk,qhd->khd",
        weights,
        mixed_grad.reshape(node_rows, heads, head_size),
        preferred_element_type=jnp.float32,
    )
    contrib = contrib.reshape(span, width)
    centre = contrib[reach : reach + node_rows]
    outward = jnp.concatenate([contrib[:reach], contrib[reach + node_rows :]], axis=0)
    received = extended(outward.astype(jnp.bfloat16), (("grid", 0),), reach).astype(outward.dtype)
    incoming = jnp.concatenate([received[:reach], received[reach + node_rows :]], axis=0)
    value_grad = (centre + incoming).astype(jnp.bfloat16)
    contract = (((0,), (0,)), ((), ()))
    product = lax.dot_general(normed, value_grad, contract, preferred_element_type=jnp.float32)
    partial_sum = lax.psum_scatter(
        product.astype(jnp.bfloat16), "member", scatter_dimension=1, tiled=True
    )
    grad_value = lax.psum_scatter(partial_sum, "grid", scatter_dimension=0, tiled=True).astype(
        jnp.float32
    )
    return (crps_terms[None], grad_value)


def solution(mesh):
    return jax.shard_map(
        body,
        mesh=mesh,
        in_specs=(
            P("member", "grid", None),
            P(),
            P(),
            P(),
            P(),
            P(),
            P(),
            P("grid"),
            P(None, "grid"),
        ),
        out_specs=(P("member", None, "grid"), P("grid", "member")),
        check_vma=False,
    )
```

profile of v0, /device:TPU:64, one launch (start us, length us, event | category | flops | bytes accessed | tf_op | source)
XLA Modules:
  0.0 365.6 jit_solution(9238538961133781223)
XLA Ops:
  7.2 0.0 copy-start
  7.2 0.0 all-gather.3.cloned.1.call-start
  7.2 1.4 fusion.14
  8.6 0.0 copy-start.4
  8.6 0.0 copy-start.10
  8.6 2.6 fusion.11
  11.2 2.5 fusion.12
  13.8 0.0 copy-start.6
  13.8 0.8 copy-done.6
  14.6 1.0 fusion.24
  15.6 1.3 collective-permute-start.1
  16.9 5.4 %collective-permute-start = (bf16[2,128,1024]{2,1,0:T(8,128)(2,1)}, bf16[2,128,1024]{2,1,0:T(8,128)(2,1)}, u32[]{:S(2)}, u32[]{:S(2)}) collective-permute-start(bf16[2,128,1024]{2,1,0:T(8,128)(2,1)} %get-tuple-element.10), channel_id=1, source_target_pairs={{0,1},{1,2},{2,3},{3,4},{4,5},{5,6},{6,7},{7,8},{8,9},{9,10},{10,1... | collective-permute-start | bytes 1572872 | tf_op jit(solution)/shard_map/ppermute | solution.py:16
  22.3 0.0 copy-done.4
  22.3 0.0 copy-done.10
  22.3 3.2 convolution_convert_fusion.4
  25.4 2.1 copy.20
  27.5 0.0 copy-done.11
  27.5 0.2 fusion.36
  27.7 3.8 %collective-permute-done.1 = bf16[2,128,1024]{2,1,0:T(8,128)(2,1)} collective-permute-done((bf16[2,128,1024]{2,1,0:T(8,128)(2,1)}, bf16[2,128,1024]{2,1,0:T(8,128)(2,1)}, u32[]{:S(2)}, u32[]{:S(2)}) %collective-permute-start.1) | collective-permute-done | bytes 524320 | tf_op jit(solution)/shard_map/ppermute | solution.py:17
  31.5 1.2 collective-permute-done
  32.7 1.5 pad_maximum_fusion
  34.2 0.0 copy-start.7
  34.2 1.5 fusion.52
  35.7 2.3 copy.19
  38.0 2.3 copy.21
  40.3 0.0 copy-done.7
  40.3 7.4 %fusion.54 = (f32[16,256]{1,0:T(8,128)S(1)}, f32[16,256,512]{2,1,0:T(8,128)}) fusion(pred[256,512]{1,0:T(8,128)(4,1)S(1)} %fusion.36, bf16[256,16,64]{0,2,1:T(8,128)(2,1)S(1)} %bitcast.79, bf16[512,16,64]{0,2,1:T(8,128)(2,1)} %bitcast.74), kind=kOutput, calls=%fused_computation.80 | convolution fusion | flops 276824576 | bytes 10108928 | tf_op jit(solution)/shard_map/sub | solution.py:75
  47.7 3.9 %divide_convert_fusion = bf16[16,256,512]{2,1,0:T(8,128)(2,1)S(1)} fusion(f32[16,256,512]{2,1,0:T(8,128)} %get-tuple-element.13, f32[16,256]{1,0:T(8,128)S(1)} %get-tuple-element.12), kind=kLoop, calls=%fused_computation.1 | loop fusion | flops 4194304 | bytes 12599296 | tf_op jit(solution)/shard_map/convert_element_type | solution.py:76
  51.6 0.0 copy-start.1
  51.6 0.0 copy-start.9
  51.6 1.9 copy-done.1
  53.6 0.0 copy-done.3
  53.6 1.4 convolution_convert_fusion.1
  55.0 0.0 copy-done
  55.0 0.0 copy-done.9
  55.0 0.9 fusion.13
  55.9 1.6 fusion.21
  57.4 0.0 all-gather.3.cloned.1.call-update
  57.5 0.2 reduce-scatter.7.cloned.1.call-start
  57.7 59.2 %all-gather.3.cloned.1.call-done = f32[1024,1024]{1,0:T(8,128)} async-done(((f32[128,1024]{1,0:T(8,128)}), f32[1024,1024]{1,0:T(8,128)}) %all-gather.3.cloned.1.call-update) | async-done | bytes 4194320 | tf_op jit(solution)/shard_map/all_gather | solution.py:90
  116.9 5.6 %fusion.6 = (f32[128,1024]{1,0:T(8,128)S(1)}, f32[128,1024]{1,0:T(8,128)}) fusion(f32[8,128,1024]{2,1,0:T(8,128)} %bitcast.68, f32[128,1024]{1,0:T(8,128)} %fusion.21), kind=kLoop, calls=%fused_computation.10 | loop fusion | flops 6029312 | bytes 5767168 | tf_op jit(solution)/shard_map/reduce_sum | solution.py:92
  122.5 0.0 copy-done.8
  122.5 0.9 fusion.20
  123.4 0.6 convolution_convert_fusion.3
  124.0 1.5 convolution_convert_fusion.2
  125.5 2.0 copy.22
  127.6 3.2 fusion.55
  130.8 0.1 fusion.53
  130.9 1.3 collective-permute-start.3
  132.2 4.6 %collective-permute-start.2 = (bf16[128,1024]{0,1:T(8,128)(2,1)S(1)}, bf16[128,1024]{0,1:T(8,128)(2,1)S(1)}, u32[]{:S(2)}, u32[]{:S(2)}) collective-permute-start(bf16[128,1024]{0,1:T(8,128)(2,1)S(1)} %bitcast.75), channel_id=1, source_target_pairs={{0,1},{1,2},{2,3},{3,4},{4,5},{5,6},{6,7},{7,8},{8,9},{9,10},{10,1... | collective-permute-start | bytes 786440 | tf_op jit(solution)/shard_map/ppermute | solution.py:16
  136.8 4.5 %collective-permute-done.3 = bf16[128,1024]{0,1:T(8,128)(2,1)S(1)} collective-permute-done((bf16[128,1024]{0,1:T(8,128)(2,1)S(1)}, bf16[128,1024]{0,1:T(8,128)(2,1)S(1)}, u32[]{:S(2)}, u32[]{:S(2)}) %collective-permute-start.3) | collective-permute-done | bytes 262176 | tf_op jit(solution)/shard_map/ppermute | solution.py:17
  141.3 1.2 collective-permute-done.2
  142.5 0.1 maximum_convert_fusion
  142.5 0.3 fusion.19
  142.8 2.2 convolution_convert_fusion
  145.0 4.0 %copy.23 = bf16[1024,1024]{0,1:T(8,128)(2,1)} copy(bf16[1024,1024]{1,0:T(8,128)(2,1)} %convolution_convert_fusion) | data formatting | bytes 4194304
  149.0 0.0 reduce-scatter.7.cloned.1.call-update
  149.0 0.0 reduce-scatter.5.cloned.1.call-start
  149.1 40.9 %reduce-scatter.7.cloned.1.call-done = bf16[128,1024]{1,0:T(8,128)(2,1)} async-done(((bf16[1024,1024]{1,0:T(8,128)(2,1)}), bf16[128,1024]{1,0:T(8,128)(2,1)}) %reduce-scatter.7.cloned.1.call-update) | async-done | bytes 262160
  190.0 1.8 copy.24
  191.8 0.0 reduce-scatter.5.cloned.1.call-update
  191.8 2.0 subtract_bitcast_fusion
  193.9 163.9 %reduce-scatter.5.cloned.1.call-done = bf16[32,128]{1,0:T(8,128)(2,1)} async-done(((bf16[1024,128]{1,0:T(8,128)(2,1)}), bf16[32,128]{1,0:T(8,128)(2,1)}) %reduce-scatter.5.cloned.1.call-update) | async-done | bytes 8208 | tf_op jit(solution)/shard_map/reduce_scatter | solution.py:121
  357.8 1.3 convert_element_type.86
  (10 shorter events, 0.0 us)
Async XLA Ops:
  7.2 47.8 %copy-start = (bf16[1024,1024]{1,0:T(8,128)(2,1)S(1)}, bf16[1024,1024]{1,0:T(8,128)(2,1)}, u32[]{:S(2)}) copy-start(bf16[1024,1024]{1,0:T(8,128)(2,1)} %param.14) | copy-start | bytes 6291460
  7.2 109.7 %all-gather.3.cloned.1.call-start = ((), (), s32[]{:S(2)}) async-start(), calls=%async_computation.3 | async-start | bytes 4718592 | tf_op jit(solution)/shard_map/all_gather | solution.py:90
  8.6 13.7 %copy-start.4 = (bf16[1,256,1024]{2,1,0:T(8,128)(2,1)S(1)}, bf16[1,256,1024]{2,1,0:T(8,128)(2,1)}, u32[]{:S(2)}) copy-start(bf16[1,256,1024]{2,1,0:T(8,128)(2,1)} %param.9) | copy-start | bytes 1572868
  8.6 13.7 %copy-start.10 = (f32[1024]{0:T(1024)S(1)}, f32[1024]{0:T(1024)}, u32[]{:S(2)}) copy-start(f32[1024]{0:T(1024)} %param.10) | copy-start | bytes 12292
  13.8 0.8 copy-start.6
  14.6 12.9 %copy-start.11 = (s32[1024]{0:T(1024)S(1)}, s32[1024]{0:T(1024)}, u32[]{:S(2)}) copy-start(s32[1024]{0:T(1024)} %param.16) | copy-start | bytes 12292
  15.6 15.9 %collective-permute-start.1 = (bf16[2,128,1024]{2,1,0:T(8,128)(2,1)}, bf16[2,128,1024]{2,1,0:T(8,128)(2,1)}, u32[]{:S(2)}, u32[]{:S(2)}) collective-permute-start(bf16[2,128,1024]{2,1,0:T(8,128)(2,1)} %get-tuple-element.11), channel_id=1, source_target_pairs={{1,0},{2,1},{3,2},{4,3},{5,4},{6,5},{7,6},{8,7},{9,8},{10,9},{11,1... | collective-permute-start | bytes 1572872 | tf_op jit(solution)/shard_map/ppermute | solution.py:17
  16.9 15.7 %collective-permute-start = (bf16[2,128,1024]{2,1,0:T(8,128)(2,1)}, bf16[2,128,1024]{2,1,0:T(8,128)(2,1)}, u32[]{:S(2)}, u32[]{:S(2)}) collective-permute-start(bf16[2,128,1024]{2,1,0:T(8,128)(2,1)} %get-tuple-element.10), channel_id=1, source_target_pairs={{0,1},{1,2},{2,3},{3,4},{4,5},{5,6},{6,7},{7,8},{8,9},{9,10},{10,1... | collective-permute-start | bytes 1572872 | tf_op jit(solution)/shard_map/ppermute | solution.py:16
  34.2 6.1 %copy-start.7 = (bf16[256,1024]{0,1:T(8,128)(2,1)S(1)}, bf16[256,1024]{0,1:T(8,128)(2,1)}, u32[]{:S(2)}) copy-start(bf16[256,1024]{0,1:T(8,128)(2,1)} %copy.20) | copy-start | bytes 1572868
  47.7 5.9 %copy-start.3 = (bf16[1,512,1024]{1,2,0:T(8,128)(2,1)S(1)}, bf16[1,512,1024]{1,2,0:T(8,128)(2,1)}, u32[]{:S(2)}) copy-start(bf16[1,512,1024]{1,2,0:T(8,128)(2,1)} %copy.19) | copy-start | bytes 3145732
  51.6 2.0 copy-start.1
  51.6 3.3 copy-start.9
  57.4 65.1 %copy-start.2 = (f32[128,1024]{1,0:T(8,128)S(1)}, f32[128,1024]{1,0:T(8,128)}, u32[]{:S(2)}) copy-start(f32[128,1024]{1,0:T(8,128)} %fusion.21) | copy-start | bytes 1572868
  57.5 132.5 %reduce-scatter.7.cloned.1.call-start = ((), (), s32[]{:S(2)}) async-start(), calls=%async_computation.4 | async-start | bytes 2359296
  116.9 5.6 %copy-start.8 = (f32[128,1024]{1,0:T(8,128)S(1)}, f32[128,1024]{1,0:T(8,128)}, u32[]{:S(2)}) copy-start(f32[128,1024]{1,0:T(8,128)} %param.17) | copy-start | bytes 1572868
  130.9 10.3 %collective-permute-start.3 = (bf16[128,1024]{0,1:T(8,128)(2,1)S(1)}, bf16[128,1024]{0,1:T(8,128)(2,1)S(1)}, u32[]{:S(2)}, u32[]{:S(2)}) collective-permute-start(bf16[128,1024]{0,1:T(8,128)(2,1)S(1)} %bitcast.77), channel_id=1, source_target_pairs={{1,0},{2,1},{3,2},{4,3},{5,4},{6,5},{7,6},{8,7},{9,8},{10,9},{11,1... | collective-permute-start | bytes 786440 | tf_op jit(solution)/shard_map/ppermute | solution.py:17
  132.2 10.2 %collective-permute-start.2 = (bf16[128,1024]{0,1:T(8,128)(2,1)S(1)}, bf16[128,1024]{0,1:T(8,128)(2,1)S(1)}, u32[]{:S(2)}, u32[]{:S(2)}) collective-permute-start(bf16[128,1024]{0,1:T(8,128)(2,1)S(1)} %bitcast.75), channel_id=1, source_target_pairs={{0,1},{1,2},{2,3},{3,4},{4,5},{5,6},{6,7},{7,8},{8,9},{9,10},{10,1... | collective-permute-start | bytes 786440 | tf_op jit(solution)/shard_map/ppermute | solution.py:16
  145.0 46.8 %copy-start.5 = (f32[128,1024]{1,0:T(8,128)S(1)}, f32[128,1024]{1,0:T(8,128)}, u32[]{:S(2)}) copy-start(f32[128,1024]{1,0:T(8,128)} %get-tuple-element.3) | copy-start | bytes 1572868
  149.0 208.8 %reduce-scatter.5.cloned.1.call-start = ((), (), s32[]{:S(2)}) async-start(), calls=%async_computation.2 | async-start | bytes 270336 | tf_op jit(solution)/shard_map/reduce_scatter | solution.py:121
Sparse Core Ops, SparseCore 0:
  57.6 59.2 all-gather.2
  149.1 40.8 reduce-scatter.6
  192.5 165.2 reduce-scatter.4
where the time goes:
time: 366 us
  waiting for transfers between devices  275 us (75%)
  matrix products  27.9 us (8%)
  local copies, waits for them, and re-layouts  18.9 us (5%)
  other arithmetic  17.3 us (5%)
  between operations  13.9 us (4%)
  starting transfers between devices  12.8 us (3%)
    reduce_scatter x1, waiting for transfers between devices, body(): lax.psum_scatter(partial_sum, 'grid', scatter_dimension=0, tiled=True)  164 us
    all_gather x1, waiting for transfers between devices, body(): lax.all_gather(pred[None], 'member', axis=0, tiled=True)  59.2 us
    unnamed x4, waiting for transfers between devices  41 us
    ppermute x2, starting transfers between devices, extended(): before = lax.ppermute(last, axis, up)  9.93 us
    unnamed x26, local copies, waits for them, and re-layouts  8.58 us
    dot_general x3, matrix products, project(): jnp.dot(normed, weight, preferred_element_type=jnp.float32)  8.28 us
    ppermute x2, waiting for transfers between devices, extended(): after = lax.ppermute(initial, axis, down)  8.27 us
    sub x1, matrix products, body(): weights = jnp.exp(scores - row_max)  7.38 us
  transfers between devices with their start and end apart: 7, of which 7 were waited for; matrix products, arithmetic and copies ran while one was open for 2% of the time, Pallas kernels for 0%

commit v1 on v0

v1 whole, which is shorter than its diff:
```python
import jax
import jax.numpy as jnp
from jax import lax
from jax.experimental import pallas as pl
from jax.experimental.pallas import tpu as pltpu
from jax.sharding import Mesh, PartitionSpec as P

F32 = jnp.float32
BF16 = jnp.bfloat16
ROWS = 256
REACH = 128
D = 1024
PAIRS = 8
PTS = 1024
CH = 128
MEMBERS = 8
MASKED = -1e30
GRID = ("y", "zl", "x")

NT = (((1,), (1,)), ((), ()))


def mm(a, b):
    return jnp.dot(a, b, preferred_element_type=F32)


def mm_nt(a, b):
    return lax.dot_general(a, b, NT, preferred_element_type=F32)


def rms(states, gain):
    floats = states.astype(F32)
    meansq = jnp.mean(floats * floats, axis=-1, keepdims=True) + 1e-05
    return (floats * lax.rsqrt(meansq) * gain).astype(BF16)


def thirds(values):
    first = values.astype(BF16)
    rest = values - first.astype(F32)
    second = rest.astype(BF16)
    third = (rest - second.astype(F32)).astype(BF16)
    return first, second, third


def call(kernel, outs, cost, scratch=(), smem=0, limit=40):
    def run(*args):
        in_specs = [pl.BlockSpec(memory_space=pltpu.SMEM)] * smem
        in_specs += [pl.BlockSpec(memory_space=pltpu.VMEM)] * (len(args) - smem)
        return pl.pallas_call(
            kernel,
            out_shape=[jax.ShapeDtypeStruct(s, d) for s, d in outs],
            in_specs=in_specs,
            out_specs=[pl.BlockSpec(memory_space=pltpu.VMEM)] * len(outs),
            scratch_shapes=list(scratch),
            compiler_params=pltpu.CompilerParams(vmem_limit_bytes=limit * 2**20),
            cost_estimate=pl.CostEstimate(
                flops=int(cost * 1e9), bytes_accessed=int(cost * 3e6), transcendentals=0
            ),
        )(*args)

    return run


def project_kernel(x_ref, gain_ref, wq_ref, wk_ref, wv_ref, q_ref, k_ref, v_ref, n_ref):
    normed = rms(x_ref[...], gain_ref[...])
    n_ref[...] = normed
    q_ref[...] = mm(normed, wq_ref[...]).astype(BF16) * jnp.asarray(0.125, BF16)
    k_ref[...] = mm(normed, wk_ref[...]).astype(BF16)
    v_ref[...] = mm(normed, wv_ref[...]).astype(BF16)


def attend_kernel(
    edge_ref, xb_ref, xa_ref, gain_ref, wk_ref, wv_ref, q_ref, k_ref, v_ref, x_ref, wo_ref, wd_ref,
    p_ref, dec_ref, dech_ref, nh_ref, kh, vh, mixed,
):
    gain = gain_ref[...]
    nh_ref[:REACH] = rms(xb_ref[...], gain)
    nh_ref[REACH:] = rms(xa_ref[...], gain)
    halo = nh_ref[...]
    kh[...] = mm(halo, wk_ref[...]).astype(BF16)
    vh[...] = mm(halo, wv_ref[...]).astype(BF16)
    lane = lax.broadcasted_iota(jnp.int32, (REACH, 128), 1)
    low = (lane < 64).astype(F32).astype(BF16)
    high = (lane >= 64).astype(F32).astype(BF16)
    lane_low = lane < 64
    query_o = lax.broadcasted_iota(jnp.int32, (2 * REACH, ROWS), 0) % REACH
    key_o = lax.broadcasted_iota(jnp.int32, (2 * REACH, ROWS), 1)
    query_h = lax.broadcasted_iota(jnp.int32, (2 * REACH, REACH), 0) % REACH
    key_h = lax.broadcasted_iota(jnp.int32, (2 * REACH, REACH), 1)
    for block in range(2):
        if block == 0:
            bias_o = jnp.where(key_o <= query_o + REACH, 0.0, MASKED)
            bias_h = jnp.where((key_h >= query_h) & (edge_ref[0] == 0), 0.0, MASKED)
        else:
            bias_o = jnp.where(key_o >= query_o, 0.0, MASKED)
            bias_h = jnp.where((key_h <= query_h) & (edge_ref[1] == 0), 0.0, MASKED)
        rows = slice(block * REACH, (block + 1) * REACH)
        for pair in range(PAIRS):
            cols = slice(pair * 128, (pair + 1) * 128)
            both = q_ref[rows, cols]
            stacked = jnp.concatenate([both * low, both * high], axis=0)
            so = mm_nt(stacked, k_ref[:, cols]) + bias_o
            sh = mm_nt(stacked, kh[rows, cols]) + bias_h
            top = jnp.maximum(
                jnp.max(so, axis=-1, keepdims=True), jnp.max(sh, axis=-1, keepdims=True)
            )
            eo = jnp.exp(so - top)
            eh = jnp.exp(sh - top)
            inv = 1.0 / (
                jnp.sum(eo, axis=-1, keepdims=True) + jnp.sum(eh, axis=-1, keepdims=True)
            )
            po = (eo * inv).astype(BF16)
            ph = (eh * inv).astype(BF16)
            p_ref[pair, block, :, :ROWS] = po
            p_ref[pair, block, :, ROWS:] = ph
            out = mm(po, v_ref[:, cols]) + mm(ph, vh[rows, cols])
            mixed[rows, cols] = jnp.where(lane_low, out[:REACH], out[REACH:]).astype(BF16)
    projected = mm(mixed[...], wo_ref[...])
    hidden = (x_ref[...].astype(F32) + projected).astype(BF16)
    decoded = mm(hidden, wd_ref[...]).T
    dec_ref[...] = decoded
    dech_ref[...] = decoded.astype(BF16)


def turn_kernel(n_ref, nh_ref, t_ref):
    t_ref[:, :ROWS] = n_ref[...].astype(F32).T.astype(BF16)
    t_ref[:, ROWS:] = nh_ref[...].astype(F32).T.astype(BF16)


def selector(node_ref):
    node = lax.broadcasted_iota(jnp.int32, (ROWS, PTS), 0)
    return (node == node_ref[...]).astype(F32).astype(BF16)


def truth_kernel(dec_ref, node_ref, truth_ref, abs_ref, slope_ref, count_ref):
    select = selector(node_ref)
    parts = thirds(dec_ref[...])
    pred = mm(parts[2], select) + mm(parts[1], select) + mm(parts[0], select)
    error = pred - truth_ref[...]
    square = error * error + 0.25
    inverse = lax.rsqrt(square)
    abs_ref[...] = square * inverse
    slope = error * inverse
    high = slope.astype(BF16)
    rest = (slope - high.astype(F32)).astype(BF16)
    slope_ref[...] = mm_nt(high, select) + mm_nt(rest, select)
    count_ref[...] = mm_nt(jnp.ones((16, PTS), BF16), select)[:8]


def backward_kernel(
    core_ref, dec_ref, o1_ref, oz_ref, oc_ref, slope_ref, count_ref, wd_ref, wo_ref, p_ref,
    keep_ref, send_ref, spread_ref, mg,
):
    own = dec_ref[...]
    spread = jnp.full((CH, ROWS), 0.5, F32)
    total = jnp.zeros((CH, ROWS), F32)
    others = [o1_ref[...]] + [oz_ref[i] for i in range(3)] + [oc_ref[i] for i in range(3)]
    for other in others:
        differ = own - other.astype(F32)
        square = differ * differ + 0.25
        inverse = lax.rsqrt(square)
        spread += square * inverse
        total += differ * inverse
    spread_ref[...] = spread
    node_grad = (slope_ref[...] - count_ref[:1] * total * (1.0 / (MEMBERS - 1))) * (1.0 / MEMBERS)
    high = node_grad.astype(BF16)
    rest = (node_grad - high.astype(F32)).astype(BF16)
    hidden_grad = (mm(wd_ref[...], high) + mm(wd_ref[...], rest)).astype(BF16)
    mg[...] = mm(wo_ref[...], hidden_grad).astype(BF16)
    feature = lax.broadcasted_iota(jnp.int32, (128, REACH), 0)
    low = (feature < 64).astype(F32).astype(BF16)
    high_rows = (feature >= 64).astype(F32).astype(BF16)
    core = core_ref[0]
    for which, out_ref in ((1, send_ref), (0, keep_ref)):
        for z in range(4):
            pair = 2 * z + (core + which) % 2
            grads = mg[pl.ds(pl.multiple_of(pair * 128, 128), 128), :]
            total_own = None
            rows = slice(z * 128, (z + 1) * 128)
            for block in range(2):
                part = grads[:, block * REACH : (block + 1) * REACH]
                split = jnp.concatenate([part * low, part * high_rows], axis=1)
                term = mm(split, p_ref[pair, block, :, :ROWS])
                total_own = term if block == 0 else total_own + term
                out_ref[rows, ROWS + block * REACH : ROWS + (block + 1) * REACH] = mm(
                    split, p_ref[pair, block, :, ROWS:]
                ).astype(BF16)
            out_ref[rows, :ROWS] = total_own.astype(BF16)


def product_kernel(t_ref, u_ref, keep_ref, recv_ref, out_ref):
    out_ref[...] = (
        mm_nt(t_ref[...], keep_ref[...]) + mm_nt(u_ref[...], recv_ref[...])
    ).astype(BF16)


def crps_kernel(abs_ref, spread_ref, node_ref, out_ref):
    select = selector(node_ref)
    parts = thirds(spread_ref[...])
    spread = mm(parts[2], select) + mm(parts[1], select) + mm(parts[0], select)
    out_ref[...] = abs_ref[...] - spread * (1.0 / (2.0 * (MEMBERS - 1)))


def body(inputs, norm_gain, w_query, w_key, w_value, w_out, w_decode, point_node, truth):
    states = inputs[0]
    gain = norm_gain[None]
    band = lax.axis_index(GRID)
    bands = 32
    core = lax.axis_index("core")
    edge = jnp.stack([band == 0, band == bands - 1]).astype(jnp.int32)
    node = (point_node - band * ROWS)[None]
    up = [(i, i + 1) for i in range(bands - 1)]
    down = [(i + 1, i) for i in range(bands - 1)]
    swap = [(0, 1), (1, 0)]
    before = lax.ppermute(states[REACH:], GRID, up)
    after = lax.ppermute(states[:REACH], GRID, down)
    wide = ((ROWS, D), BF16)
    queries, keys, values, normed = call(project_kernel, [wide] * 4, 1.6)(
        states, gain, w_query, w_key, w_value
    )
    probs, decoded, decoded_half, normed_halo = call(
        attend_kernel,
        [((PAIRS, 2, 2 * REACH, ROWS + REACH), BF16), ((CH, ROWS), F32), ((CH, ROWS), BF16), wide],
        4.0,
        [pltpu.VMEM((ROWS, D), BF16)] * 3,
        smem=1,
    )(edge, before, after, gain, w_key, w_value, queries, keys, values, states, w_out, w_decode)
    other = lax.ppermute(decoded_half, "core", swap)
    along = [
        lax.ppermute(decoded_half, "zh", [(i, (i + k) % 4) for i in range(4)]) for k in (2, 1, 3)
    ]
    along = jnp.stack(along)
    across = lax.ppermute(along, "core", swap)
    (turned,) = call(turn_kernel, [((D, 2 * ROWS), BF16)], 1.0)(normed, normed_halo)
    turned_other = lax.ppermute(turned, "core", swap)
    abs_error, slope, count = call(
        truth_kernel, [((CH, PTS), F32), ((CH, ROWS), F32), ((8, ROWS), F32)], 2.0
    )(decoded, node, truth)
    keep, send, spread = call(
        backward_kernel,
        [((512, 512), BF16), ((512, 512), BF16), ((CH, ROWS), F32)],
        3.0,
        [pltpu.VMEM((D, ROWS), BF16)],
        smem=1,
    )(core[None], decoded, other, along, across, slope, count, w_decode, w_out, probs)
    received = lax.ppermute(send, "core", swap)
    (crps_terms,) = call(crps_kernel, [((CH, PTS), F32)], 1.0)(abs_error, spread, node)
    (product,) = call(product_kernel, [((D, 512), BF16)], 1.1)(turned, turned_other, keep, received)
    pieces = lax.all_to_all(product.reshape(32, 32, 512), GRID, 0, 0)
    banded = jnp.sum(pieces.astype(F32), axis=0).astype(BF16)
    columns = jnp.transpose(banded.reshape(32, 4, 128), (1, 0, 2))
    last = lax.all_to_all(columns, "zh", 0, 0)
    grad_value = jnp.sum(last.astype(F32), axis=0)
    return crps_terms[None], grad_value


def solution(mesh):
    parts = Mesh(mesh.devices.reshape(4, 2, 4, 2, 4), ("zh", "core", "y", "zl", "x"))
    member = ("zh", "core")
    return jax.shard_map(
        body,
        mesh=parts,
        in_specs=(
            P(member, GRID, None), P(), P(), P(), P(), P(), P(), P(GRID), P(None, GRID),
        ),
        out_specs=(P(member, None, GRID), P(GRID, member)),
        check_vma=False,
    )
```

time: 366 us -> 93.9 us (0.26)
  the two profiles are of different devices: /device:TPU:64 before, /device:TPU:2 now
where the time goes in v1:
time: 93.9 us; the launch traced here: 93.4 us
  blocking collectives  28.2 us (30%)
  starting transfers between devices  22 us (23%)
  Pallas kernels  18.5 us (20%)
  waiting for transfers between devices  12.2 us (13%)
  local copies, waits for them, and re-layouts  10.7 us (11%)
    all_to_all x1, blocking collectives, body(): pieces = lax.all_to_all(product.reshape(32, 32, 512), GRID, 0, 0)  28.2 us
    pallas_call x7, Pallas kernels, run(): pl.pallas_call(kernel, out_shape=[jax.ShapeDtypeStruct(s, d) for s, d in...  18.5 us
    ppermute x3, starting transfers between devices, body(): lax.ppermute(decoded_half, 'zh', [(i, (i + k) % 4) for i in range(4)])  9.94 us
    unnamed x32, local copies, waits for them, and re-layouts  9.02 us
    all_to_all x1, waiting for transfers between devices, body(): last = lax.all_to_all(columns, 'zh', 0, 0)  6.61 us
    all_to_all x1, starting transfers between devices, body(): last = lax.all_to_all(columns, 'zh', 0, 0)  4.95 us
    ppermute x1, starting transfers between devices, body(): after = lax.ppermute(states[:REACH], GRID, down)  4.18 us
    ppermute x3, waiting for transfers between devices, body(): lax.ppermute(decoded_half, 'zh', [(i, (i + k) % 4) for i in range(4)])  3.76 us
  transfers between devices with their start and end apart: 10, of which 4 were waited for; matrix products, arithmetic and copies ran while one was open for 0% of the time, Pallas kernels for 8%

profile of v1, /device:TPU:2, one launch (start us, length us, event | category | flops | bytes accessed | tf_op | source)
XLA Modules:
  0.0 93.4 jit_solution(11865811755682301092)
XLA Ops:
  0.6 1.1 %slice_bitcast_fusion = (bf16[128,1024]{1,0:T(8,128)(2,1)S(1)}, bf16[128,1024]{1,0:T(8,128)(2,1)S(1)}) fusion(bf16[1,256,1024]{2,1,0:T(8,128)(2,1)} %param.9), kind=kLoop, calls=%fused_computation | loop fusion | bytes 1048576 | tf_op jit(solution)/shard_map/slice | solution.py:216
  1.7 4.2 %collective-permute-start.1 = (bf16[128,1024]{1,0:T(8,128)(2,1)S(1)}, bf16[128,1024]{1,0:T(8,128)(2,1)S(1)}, u32[]{:S(2)}, u32[]{:S(2)}) collective-permute-start(bf16[128,1024]{1,0:T(8,128)(2,1)S(1)} %get-tuple-element.30), channel_id=1, source_target_pairs={{1,0},{2,1},{3,2},{4,3},{5,4},{6,5},{7,6},{8,7},{9,8},{10,9},{11,1... | collective-permute-start | bytes 786440 | tf_op jit(solution)/shard_map/ppermute | solution.py:216
  5.9 1.9 %collective-permute-start = (bf16[128,1024]{1,0:T(8,128)(2,1)S(1)}, bf16[128,1024]{1,0:T(8,128)(2,1)S(1)}, u32[]{:S(2)}, u32[]{:S(2)}) collective-permute-start(bf16[128,1024]{1,0:T(8,128)(2,1)S(1)} %get-tuple-element.31), channel_id=1, source_target_pairs={{0,1},{1,2},{2,3},{3,4},{4,5},{5,6},{6,7},{7,8},{8,9},{9,10},{10,1... | collective-permute-start | bytes 786440 | tf_op jit(solution)/shard_map/ppermute | solution.py:215
  7.8 0.1 add_convert_fusion.edge_ref
  7.9 0.0 copy-start
  7.9 1.6 %copy-done = bf16[1024,1024]{1,0:T(8,128)(2,1)S(1)} copy-done((bf16[1024,1024]{1,0:T(8,128)(2,1)S(1)}, bf16[1024,1024]{1,0:T(8,128)(2,1)}, u32[]{:S(2)}) %copy-start) | copy-done | bytes 2097176
  9.5 0.0 copy-start.1
  9.5 1.6 %copy-done.1 = bf16[1024,1024]{1,0:T(8,128)(2,1)S(1)} copy-done((bf16[1024,1024]{1,0:T(8,128)(2,1)S(1)}, bf16[1024,1024]{1,0:T(8,128)(2,1)}, u32[]{:S(2)}) %copy-start.1) | copy-done | bytes 2097176
  11.1 0.0 copy-start.3
  11.1 1.6 %copy-done.3 = bf16[1024,1024]{1,0:T(8,128)(2,1)S(1)} copy-done((bf16[1024,1024]{1,0:T(8,128)(2,1)S(1)}, bf16[1024,1024]{1,0:T(8,128)(2,1)}, u32[]{:S(2)}) %copy-start.3) | copy-done | bytes 2097176
  12.7 1.0 %copy-done.5 = bf16[1,256,1024]{2,1,0:T(8,128)(2,1)S(1)} copy-done((bf16[1,256,1024]{2,1,0:T(8,128)(2,1)S(1)}, bf16[1,256,1024]{2,1,0:T(8,128)(2,1)}, u32[]{:S(2)}) %copy-start.5) | copy-done | bytes 524312
  13.7 0.0 copy-start.6
  13.7 0.7 copy-done.6
  14.4 0.0 copy-start.2
  14.4 0.0 copy-start.4
  14.4 0.0 copy-start.7
  14.4 0.0 copy-start.10
  14.4 1.9 %shard_map.104 = (bf16[256,1024]{1,0:T(8,128)(2,1)S(1)}, bf16[256,1024]{1,0:T(8,128)(2,1)S(1)}, bf16[256,1024]{1,0:T(8,128)(2,1)S(1)}, bf16[256,1024]{1,0:T(8,128)(2,1)S(1)}) custom-call(bf16[256,1024]{1,0:T(8,128)(2,1)S(1)} %bitcast.17, f32[1,1024]{1,0:T(1,128)S(1)} %bitcast.19, bf16[1024,1024]{1,0:T(8,128)(2,1)S(1)} %copy-done, ...), custom_call_target="tpu_custom_call" | custom-call | flops 1600000000 | bytes 4800000 | tf_op jit(solution)/shard_map/pallas_call | solution.py:49
  16.4 0.0 collective-permute-done.1.xa_ref
  16.4 0.0 collective-permute-done.xb_ref
  16.4 0.0 copy-done.2
  16.4 0.2 copy-done.4
  16.6 0.6 copy-done.7
  17.3 0.0 copy-done.10
  17.3 9.8 %shard_map.105 = (bf16[8,2,256,384]{3,2,1,0:T(8,128)(2,1)S(1)}, f32[128,256]{1,0:T(8,128)S(1)}, bf16[128,256]{1,0:T(8,128)(2,1)S(1)}, bf16[256,1024]{1,0:T(8,128)(2,1)S(1)}) custom-call(s32[2]{0:T(128)S(1)} %add_convert_fusion.edge_ref, bf16[128,1024]{1,0:T(8,128)(2,1)S(1)} %collective-permute-done.xb_ref, ...), custom_call_target="tpu_custom_call" | custom-call | flops 4000000000 | bytes 12000000 | tf_op jit(solution)/shard_map/pallas_call | solution.py:49
  27.1 0.0 copy-start.11
  27.1 0.0 copy-start.15
  27.1 0.0 copy-start.9
  27.1 6.1 %collective-permute-start.5 = (bf16[128,256]{1,0:T(8,128)(2,1)S(1)}, bf16[128,256]{1,0:T(8,128)(2,1)S(1)}, u32[]{:S(2)}, u32[]{:S(2)}) collective-permute-start(bf16[128,256]{1,0:T(8,128)(2,1)S(1)} %get-tuple-element.21), channel_id=1, source_target_pairs={{0,192},{64,0},{128,64},{192,128},{1,193},{65,1},{129,65},{193,129... | collective-permute-start | bytes 196616 | tf_op jit(solution)/shard_map/ppermute | solution.py:230
  33.3 0.0 collective-permute-start.4
  33.3 3.8 %collective-permute-start.3 = (bf16[128,256]{1,0:T(8,128)(2,1)S(1)}, bf16[128,256]{1,0:T(8,128)(2,1)S(1)}, u32[]{:S(2)}, u32[]{:S(2)}) collective-permute-start(bf16[128,256]{1,0:T(8,128)(2,1)S(1)} %get-tuple-element.21), channel_id=1, source_target_pairs={{0,128},{64,192},{128,0},{192,64},{1,129},{65,193},{129,1},{193,65... | collective-permute-start | bytes 196616 | tf_op jit(solution)/shard_map/ppermute | solution.py:230
  37.1 0.3 shard_map.109.t_ref
  37.4 0.3 collective-permute-start.7
  37.7 0.0 collective-permute-done.5
  37.7 3.0 %collective-permute-done.4 = bf16[128,256]{1,0:T(8,128)(2,1)S(1)} collective-permute-done((bf16[128,256]{1,0:T(8,128)(2,1)S(1)}, bf16[128,256]{1,0:T(8,128)(2,1)S(1)}, u32[]{:S(2)}, u32[]{:S(2)}) %collective-permute-start.4) | collective-permute-done | bytes 65568 | tf_op jit(solution)/shard_map/ppermute | solution.py:230
  40.7 0.7 collective-permute-done.3
  41.5 0.0 copy-done.11
  41.5 0.1 collective-permute-start.6
  41.6 0.0 copy-done.15
  41.6 0.5 collective-permute-start.2
  42.1 0.0 copy-done.9
  42.1 0.0 copy-start.8
  42.1 0.0 copy-start.12
  42.1 1.1 %shard_map.106 = (f32[128,1024]{1,0:T(8,128)S(1)}, f32[128,256]{1,0:T(8,128)S(1)}, f32[8,256]{1,0:T(8,128)S(1)}) custom-call(f32[128,256]{1,0:T(8,128)S(1)} %get-tuple-element.19.dec_ref, s32[1,1024]{1,0:T(1,128)S(1)} %bitcast.21, f32[128,1024]{1,0:T(8,128)S(1)} %copy-done.9), custom_call_target="tpu_custom_call" | custom-call | flops 2000000000 | bytes 6000000 | tf_op jit(solution)/shard_map/pallas_call | solution.py:49
  43.2 0.0 copy-start.13
  43.2 0.0 collective-permute-done.2.o1_ref
  43.2 0.0 collective-permute-done.6.oc_ref
  43.2 0.5 copy-done.8
  43.7 1.1 %copy-done.12 = bf16[8,2,256,384]{3,2,1,0:T(8,128)(2,1)S(1)} copy-done((bf16[8,2,256,384]{3,2,1,0:T(8,128)(2,1)S(1)}, bf16[8,2,256,384]{3,2,1,0:T(8,128)(2,1)}, u32[]{:S(2)}) %copy-start.12) | copy-done | bytes 3145752
  44.8 2.8 %shard_map.107 = (bf16[512,512]{1,0:T(8,128)(2,1)S(1)}, bf16[512,512]{1,0:T(8,128)(2,1)S(1)}, f32[128,256]{1,0:T(8,128)S(1)}) custom-call(s32[1]{0:T(128)} %bitcast.7.core_ref, f32[128,256]{1,0:T(8,128)S(1)} %get-tuple-element.19.dec_ref, bf16[128,256]{1,0:T(8,128)(2,1)S(1)} %collective-permute-done.2.o1_ref, ...), custom_call_target="tpu_custom_call" | custom-call | flops 3000000000 | bytes 9000000 | tf_op jit(solution)/shard_map/pallas_call | solution.py:49
  47.7 0.0 copy-done.13
  47.7 0.2 collective-permute-start.8
  47.9 1.8 %collective-permute-done.8.recv_ref = bf16[512,512]{1,0:T(8,128)(2,1)S(1)} collective-permute-done((bf16[512,512]{1,0:T(8,128)(2,1)S(1)}, bf16[512,512]{1,0:T(8,128)(2,1)S(1)}, u32[]{:S(2)}, u32[]{:S(2)}) %collective-permute-start.8) | collective-permute-done | bytes 524320 | tf_op jit(solution)/shard_map/ppermute | solution.py:246
  49.7 0.0 collective-permute-done.7.u_ref
  49.7 1.3 %shard_map.110 = bf16[1024,512]{1,0:T(8,128)(2,1)S(1)} custom-call(bf16[1024,512]{1,0:T(8,128)(2,1)S(1)} %shard_map.109.t_ref, bf16[1024,512]{1,0:T(8,128)(2,1)S(1)} %collective-permute-done.7.u_ref, bf16[512,512]{1,0:T(8,128)(2,1)S(1)} %get-tuple-element.28.keep_ref, bf16[512,512]{1,0:T(8,128)(2,1)S(1)} %collective-permute-done.8.recv_ref), custom_call_target="tpu_custom_call" | custom-call | flops 1100000000 | bytes 3300000 | tf_op jit(solution)/shard_map/pallas_call | solution.py:49
  51.0 0.0 copy-start.14
  51.0 28.2 %all_to_all.10 = bf16[32,32,512]{2,1,0:T(8,128)(2,1)S(1)} all-to-all(bf16[32,32,512]{2,1,0:T(8,128)(2,1)S(1)} %bitcast.16), channel_id=1, replica_groups=mesh['zh'=4,'core'=2,'y'=4,'zl'=2,'x'=4] {'y','zl','x'}, dimensions={0} | all-to-all | bytes 2097152 | tf_op jit(solution)/shard_map/all_to_all | solution.py:249
  79.2 0.2 reduce_sum.21
  79.4 0.6 copy.11
  80.0 5.0 %all-to-all-start.1 = ((bf16[4,32,128]{2,1,0:T(8,128)(2,1)}), bf16[4,32,128]{2,1,0:T(8,128)(2,1)S(1)}, u32[]{:S(2)}, u32[]{:S(2)}) async-start(bf16[4,32,128]{2,1,0:T(8,128)(2,1)} %copy.11), calls=%async_computation.1 | async-start | bytes 65536 | tf_op jit(solution)/shard_map/all_to_all | solution.py:252
  84.9 0.0 copy-done.14
  84.9 1.3 %shard_map.108 = f32[128,1024]{1,0:T(8,128)} custom-call(f32[128,1024]{1,0:T(8,128)S(1)} %copy-done.14, f32[128,256]{1,0:T(8,128)S(1)} %get-tuple-element.25.spread_ref, s32[1,1024]{1,0:T(1,128)S(1)} %bitcast.22), custom_call_target="tpu_custom_call" | custom-call | flops 1000000000 | bytes 3000000 | tf_op jit(solution)/shard_map/pallas_call | solution.py:49
  86.2 6.6 %all-to-all-done.1 = bf16[4,32,128]{2,1,0:T(8,128)(2,1)S(1)} async-done(((bf16[4,32,128]{2,1,0:T(8,128)(2,1)}), bf16[4,32,128]{2,1,0:T(8,128)(2,1)S(1)}, u32[]{:S(2)}, u32[]{:S(2)}) %all-to-all-start.1) | async-done | bytes 32800 | tf_op jit(solution)/shard_map/all_to_all | solution.py:252
  92.8 0.6 convert_reduce_fusion
  (4 shorter events, 0.1 us)
Async XLA Ops:
  1.7 14.7 %collective-permute-start.1 = (bf16[128,1024]{1,0:T(8,128)(2,1)S(1)}, bf16[128,1024]{1,0:T(8,128)(2,1)S(1)}, u32[]{:S(2)}, u32[]{:S(2)}) collective-permute-start(bf16[128,1024]{1,0:T(8,128)(2,1)S(1)} %get-tuple-element.30), channel_id=1, source_target_pairs={{1,0},{2,1},{3,2},{4,3},{5,4},{6,5},{7,6},{8,7},{9,8},{10,9},{11,1... | collective-permute-start | bytes 786440 | tf_op jit(solution)/shard_map/ppermute | solution.py:216
  5.9 10.5 %collective-permute-start = (bf16[128,1024]{1,0:T(8,128)(2,1)S(1)}, bf16[128,1024]{1,0:T(8,128)(2,1)S(1)}, u32[]{:S(2)}, u32[]{:S(2)}) collective-permute-start(bf16[128,1024]{1,0:T(8,128)(2,1)S(1)} %get-tuple-element.31), channel_id=1, source_target_pairs={{0,1},{1,2},{2,3},{3,4},{4,5},{5,6},{6,7},{7,8},{8,9},{9,10},{10,1... | collective-permute-start | bytes 786440 | tf_op jit(solution)/shard_map/ppermute | solution.py:215
  7.9 1.6 %copy-start = (bf16[1024,1024]{1,0:T(8,128)(2,1)S(1)}, bf16[1024,1024]{1,0:T(8,128)(2,1)}, u32[]{:S(2)}) copy-start(bf16[1024,1024]{1,0:T(8,128)(2,1)} %wq_ref.1) | copy-start | bytes 6291460
  9.5 1.6 %copy-start.1 = (bf16[1024,1024]{1,0:T(8,128)(2,1)S(1)}, bf16[1024,1024]{1,0:T(8,128)(2,1)}, u32[]{:S(2)}) copy-start(bf16[1024,1024]{1,0:T(8,128)(2,1)} %wk_ref.3) | copy-start | bytes 6291460
  11.1 1.6 %copy-start.3 = (bf16[1024,1024]{1,0:T(8,128)(2,1)S(1)}, bf16[1024,1024]{1,0:T(8,128)(2,1)}, u32[]{:S(2)}) copy-start(bf16[1024,1024]{1,0:T(8,128)(2,1)} %wv_ref.3) | copy-start | bytes 6291460
  12.7 1.0 %copy-start.5 = (bf16[1,256,1024]{2,1,0:T(8,128)(2,1)S(1)}, bf16[1,256,1024]{2,1,0:T(8,128)(2,1)}, u32[]{:S(2)}) copy-start(bf16[1,256,1024]{2,1,0:T(8,128)(2,1)} %param.9) | copy-start | bytes 1572868
  13.7 0.7 copy-start.6
  14.4 2.0 %copy-start.2 = (bf16[1024,1024]{1,0:T(8,128)(2,1)S(1)}, bf16[1024,1024]{1,0:T(8,128)(2,1)}, u32[]{:S(2)}) copy-start(bf16[1024,1024]{1,0:T(8,128)(2,1)} %wk_ref.3) | copy-start | bytes 6291460
  14.4 2.2 %copy-start.4 = (bf16[1024,1024]{1,0:T(8,128)(2,1)S(1)}, bf16[1024,1024]{1,0:T(8,128)(2,1)}, u32[]{:S(2)}) copy-start(bf16[1024,1024]{1,0:T(8,128)(2,1)} %wv_ref.3) | copy-start | bytes 6291460
  14.4 2.9 %copy-start.7 = (bf16[1024,1024]{1,0:T(8,128)(2,1)S(1)}, bf16[1024,1024]{1,0:T(8,128)(2,1)}, u32[]{:S(2)}) copy-start(bf16[1024,1024]{1,0:T(8,128)(2,1)} %wo_ref.3) | copy-start | bytes 6291460
  14.4 2.9 %copy-start.10 = (bf16[1024,128]{1,0:T(8,128)(2,1)S(1)}, bf16[1024,128]{1,0:T(8,128)(2,1)}, u32[]{:S(2)}) copy-start(bf16[1024,128]{1,0:T(8,128)(2,1)} %wd_ref.3) | copy-start | bytes 786436
  27.1 14.4 %copy-start.11 = (bf16[8,2,256,384]{3,2,1,0:T(8,128)(2,1)}, bf16[8,2,256,384]{3,2,1,0:T(8,128)(2,1)S(1)}, u32[]{:S(2)}) copy-start(bf16[8,2,256,384]{3,2,1,0:T(8,128)(2,1)S(1)} %get-tuple-element.24.p_ref) | copy-start | bytes 9437188
  27.1 14.5 %copy-start.15 = (s32[1024]{0:T(1024)S(1)}, s32[1024]{0:T(1024)}, u32[]{:S(2)}) copy-start(s32[1024]{0:T(1024)} %param.16) | copy-start | bytes 12292
  27.1 15.0 %copy-start.9 = (f32[128,1024]{1,0:T(8,128)S(1)}, f32[128,1024]{1,0:T(8,128)}, u32[]{:S(2)}) copy-start(f32[128,1024]{1,0:T(8,128)} %truth_ref.1) | copy-start | bytes 1572868
  27.1 10.6 %collective-permute-start.5 = (bf16[128,256]{1,0:T(8,128)(2,1)S(1)}, bf16[128,256]{1,0:T(8,128)(2,1)S(1)}, u32[]{:S(2)}, u32[]{:S(2)}) collective-permute-start(bf16[128,256]{1,0:T(8,128)(2,1)S(1)} %get-tuple-element.21), channel_id=1, source_target_pairs={{0,192},{64,0},{128,64},{192,128},{1,193},{65,1},{129,65},{193,129... | collective-permute-start | bytes 196616 | tf_op jit(solution)/shard_map/ppermute | solution.py:230
  33.3 7.5 %collective-permute-start.4 = (bf16[128,256]{1,0:T(8,128)(2,1)S(1)}, bf16[128,256]{1,0:T(8,128)(2,1)S(1)}, u32[]{:S(2)}, u32[]{:S(2)}) collective-permute-start(bf16[128,256]{1,0:T(8,128)(2,1)S(1)} %get-tuple-element.21), channel_id=1, source_target_pairs={{0,64},{64,128},{128,192},{192,0},{1,65},{65,129},{129,193},{193,1... | collective-permute-start | bytes 196616 | tf_op jit(solution)/shard_map/ppermute | solution.py:230
  33.3 8.2 %collective-permute-start.3 = (bf16[128,256]{1,0:T(8,128)(2,1)S(1)}, bf16[128,256]{1,0:T(8,128)(2,1)S(1)}, u32[]{:S(2)}, u32[]{:S(2)}) collective-permute-start(bf16[128,256]{1,0:T(8,128)(2,1)S(1)} %get-tuple-element.21), channel_id=1, source_target_pairs={{0,128},{64,192},{128,0},{192,64},{1,129},{65,193},{129,1},{193,65... | collective-permute-start | bytes 196616 | tf_op jit(solution)/shard_map/ppermute | solution.py:230
  37.4 12.3 %collective-permute-start.7 = (bf16[1024,512]{1,0:T(8,128)(2,1)S(1)}, bf16[1024,512]{1,0:T(8,128)(2,1)S(1)}, u32[]{:S(2)}, u32[]{:S(2)}) collective-permute-start(bf16[1024,512]{1,0:T(8,128)(2,1)S(1)} %shard_map.109.t_ref), channel_id=1, source_target_pairs={{0,32},{32,0},{1,33},{33,1},{2,34},{34,2},{3,35},{35,3},{4,36},{36... | collective-permute-start | bytes 3145736 | tf_op jit(solution)/shard_map/ppermute | solution.py:235
  41.5 1.7 %collective-permute-start.6 = (bf16[3,128,256]{2,1,0:T(8,128)(2,1)S(1)}, bf16[3,128,256]{2,1,0:T(8,128)(2,1)S(1)}, u32[]{:S(2)}, u32[]{:S(2)}) collective-permute-start(bf16[3,128,256]{2,1,0:T(8,128)(2,1)S(1)} %pad_maximum_fusion.oz_ref), channel_id=1, source_target_pairs={{0,32},{32,0},{1,33},{33,1},{2,34},{34,2},{3,35},{35,3},{4,36},{36... | collective-permute-start | bytes 589832 | tf_op jit(solution)/shard_map/ppermute | solution.py:233
  41.6 1.6 %collective-permute-start.2 = (bf16[128,256]{1,0:T(8,128)(2,1)S(1)}, bf16[128,256]{1,0:T(8,128)(2,1)S(1)}, u32[]{:S(2)}, u32[]{:S(2)}) collective-permute-start(bf16[128,256]{1,0:T(8,128)(2,1)S(1)} %get-tuple-element.21), channel_id=1, source_target_pairs={{0,32},{32,0},{1,33},{33,1},{2,34},{34,2},{3,35},{35,3},{4,36},{36... | collective-permute-start | bytes 196616 | tf_op jit(solution)/shard_map/ppermute | solution.py:228
  42.1 1.6 %copy-start.8 = (bf16[1024,1024]{1,0:T(8,128)(2,1)S(1)}, bf16[1024,1024]{1,0:T(8,128)(2,1)}, u32[]{:S(2)}) copy-start(bf16[1024,1024]{1,0:T(8,128)(2,1)} %wo_ref.3) | copy-start | bytes 6291460
  42.1 2.7 %copy-start.12 = (bf16[8,2,256,384]{3,2,1,0:T(8,128)(2,1)S(1)}, bf16[8,2,256,384]{3,2,1,0:T(8,128)(2,1)}, u32[]{:S(2)}) copy-start(bf16[8,2,256,384]{3,2,1,0:T(8,128)(2,1)} %copy-done.11) | copy-start | bytes 9437188
  43.2 4.5 %copy-start.13 = (f32[128,1024]{1,0:T(8,128)}, f32[128,1024]{1,0:T(8,128)S(1)}, u32[]{:S(2)}) copy-start(f32[128,1024]{1,0:T(8,128)S(1)} %get-tuple-element.20.abs_ref) | copy-start | bytes 1572868
  47.7 2.0 %collective-permute-start.8 = (bf16[512,512]{1,0:T(8,128)(2,1)S(1)}, bf16[512,512]{1,0:T(8,128)(2,1)S(1)}, u32[]{:S(2)}, u32[]{:S(2)}) collective-permute-start(bf16[512,512]{1,0:T(8,128)(2,1)S(1)} %get-tuple-element.29), channel_id=1, source_target_pairs={{0,32},{32,0},{1,33},{33,1},{2,34},{34,2},{3,35},{35,3},{4,36},{36... | collective-permute-start | bytes 1572872 | tf_op jit(solution)/shard_map/ppermute | solution.py:246
  51.0 34.0 %copy-start.14 = (f32[128,1024]{1,0:T(8,128)S(1)}, f32[128,1024]{1,0:T(8,128)}, u32[]{:S(2)}) copy-start(f32[128,1024]{1,0:T(8,128)} %copy-done.13) | copy-start | bytes 1572868
  80.0 12.8 %all-to-all-start.1 = ((bf16[4,32,128]{2,1,0:T(8,128)(2,1)}), bf16[4,32,128]{2,1,0:T(8,128)(2,1)S(1)}, u32[]{:S(2)}, u32[]{:S(2)}) async-start(bf16[4,32,128]{2,1,0:T(8,128)(2,1)} %copy.11), calls=%async_computation.1 | async-start | bytes 65536 | tf_op jit(solution)/shard_map/all_to_all | solution.py:252

commit v2 on v1

v2 whole, which is shorter than its diff:
```python
import jax
import jax.numpy as jnp
from jax import lax
from jax.experimental import pallas as pl
from jax.experimental.pallas import tpu as pltpu
from jax.sharding import Mesh, PartitionSpec as P

F32 = jnp.float32
BF16 = jnp.bfloat16
ROWS = 256
REACH = 128
D = 1024
PAIRS = 8
PTS = 1024
CH = 128
MEMBERS = 8
BANDS = 32
MASKED = -1e30
GRID = ("y", "zl", "x")

NT = (((1,), (1,)), ((), ()))


def mm(a, b):
    return jnp.dot(a, b, preferred_element_type=F32)


def mm_nt(a, b):
    return lax.dot_general(a, b, NT, preferred_element_type=F32)


def rms(states, gain):
    floats = states.astype(F32)
    meansq = jnp.mean(floats * floats, axis=-1, keepdims=True) + 1e-05
    return (floats * lax.rsqrt(meansq) * gain).astype(BF16)


def thirds(values):
    first = values.astype(BF16)
    rest = values - first.astype(F32)
    second = rest.astype(BF16)
    third = (rest - second.astype(F32)).astype(BF16)
    return first, second, third


def call(kernel, outs, cost, scratch=(), hbm=0, limit=16, keep=False):
    def run(*args):
        args = [
            pltpu.with_memory_space_constraint(arg, pltpu.HBM) if i < hbm else arg
            for i, arg in enumerate(args)
        ]
        in_specs = [pl.BlockSpec(memory_space=pltpu.HBM)] * hbm
        in_specs += [pl.BlockSpec(memory_space=pltpu.VMEM)] * (len(args) - hbm)
        other = pltpu.VMEM if keep else jax.ShapeDtypeStruct
        return pl.pallas_call(
            kernel,
            out_shape=[other(s, d) for s, d in outs],
            in_specs=in_specs,
            out_specs=[pl.BlockSpec(memory_space=pltpu.VMEM)] * len(outs),
            scratch_shapes=list(scratch),
            compiler_params=pltpu.CompilerParams(vmem_limit_bytes=limit * 2**20),
            cost_estimate=pl.CostEstimate(
                flops=int(cost * 1e9), bytes_accessed=int(cost * 3e6), transcendentals=0
            ),
        )(*args)

    return run


def split_kernel(x_hbm, x_ref, up_ref, down_ref, sems):
    copies = [
        pltpu.make_async_copy(x_hbm.at[REACH:], up_ref, sems.at[0]),
        pltpu.make_async_copy(x_hbm.at[:REACH], down_ref, sems.at[1]),
        pltpu.make_async_copy(x_hbm, x_ref, sems.at[2]),
    ]
    for copy in copies:
        copy.start()
    for copy in copies:
        copy.wait()


def project_kernel(
    wq_hbm, wk_hbm, wv_hbm, wo_hbm, wd_hbm, gain_hbm, x_ref,
    q_ref, k_ref, vt_ref, n_ref, wk_ref, wv_ref, wo_ref, wd_ref, gain_ref, wq, sems,
):
    half = D // 2
    copies = [pltpu.make_async_copy(gain_hbm, gain_ref, sems.at[0])]
    for hbm, vmem in ((wq_hbm, wq), (wk_hbm, wk_ref), (wv_hbm, wv_ref), (wo_hbm, wo_ref)):
        for j in range(2):
            rows = slice(j * half, (j + 1) * half)
            copies.append(
                pltpu.make_async_copy(hbm.at[rows], vmem.at[rows], sems.at[len(copies)])
            )
    copies.append(pltpu.make_async_copy(wd_hbm, wd_ref, sems.at[len(copies)]))
    for copy in copies:
        copy.start()
    copies[0].wait()
    normed = rms(x_ref[...], gain_ref[...])
    n_ref[...] = normed
    copies[1].wait()
    copies[2].wait()
    q_ref[...] = mm(normed, wq[...]).astype(BF16) * jnp.asarray(0.125, BF16)
    copies[3].wait()
    copies[4].wait()
    k_ref[...] = mm(normed, wk_ref[...]).astype(BF16)
    copies[5].wait()
    copies[6].wait()
    vt_ref[...] = mm(normed, wv_ref[...]).T.astype(BF16)
    for copy in copies[7:]:
        copy.wait()


def attend_kernel(
    xb_ref, xa_ref, gain_ref, wk_ref, wv_ref, q_ref, k_ref, vt_ref, x_ref, wo_ref, wd_ref,
    probs, dec_ref, dech_ref, nh_ref, kh, vht, mixed,
):
    band = band_index()
    gain = gain_ref[...]
    nh_ref[:REACH] = rms(xb_ref[...], gain)
    nh_ref[REACH:] = rms(xa_ref[...], gain)
    halo = nh_ref[...]
    kh[...] = mm(halo, wk_ref[...]).astype(BF16)
    vht[...] = mm(halo, wv_ref[...]).T.astype(BF16)
    lane = lax.broadcasted_iota(jnp.int32, (REACH, 128), 1)
    low = (lane < 64).astype(F32).astype(BF16)
    high = (lane >= 64).astype(F32).astype(BF16)
    row_low = lax.broadcasted_iota(jnp.int32, (128, REACH), 0) < 64
    key = lax.broadcasted_iota(jnp.int32, (REACH, 2 * REACH), 0)
    query = lax.broadcasted_iota(jnp.int32, (REACH, 2 * REACH), 1) % REACH
    before = jnp.where(key <= query, 0.0, MASKED)
    after = jnp.where(key >= query, 0.0, MASKED)
    first = jnp.where((key >= query) & (band > 0), 0.0, MASKED)
    last = jnp.where((key <= query) & (band < BANDS - 1), 0.0, MASKED)
    for block in range(2):
        rows = slice(block * REACH, (block + 1) * REACH)
        for pair in range(PAIRS):
            cols = slice(pair * 128, (pair + 1) * 128)
            both = q_ref[rows, cols]
            stacked = jnp.concatenate([both * low, both * high], axis=0)
            s0 = mm_nt(k_ref[:REACH, cols], stacked)
            s1 = mm_nt(k_ref[REACH:, cols], stacked)
            s2 = mm_nt(kh[rows, cols], stacked)
            if block == 0:
                s1 += before
                s2 += first
            else:
                s0 += after
                s2 += last
            top = jnp.max(jnp.maximum(jnp.maximum(s0, s1), s2), axis=0, keepdims=True)
            e0 = jnp.exp(s0 - top)
            e1 = jnp.exp(s1 - top)
            e2 = jnp.exp(s2 - top)
            inv = 1.0 / jnp.sum(e0 + e1 + e2, axis=0, keepdims=True)
            po = jnp.concatenate([(e0 * inv).astype(BF16), (e1 * inv).astype(BF16)], axis=0)
            ph = (e2 * inv).astype(BF16)
            probs[pair, block, :ROWS] = po
            probs[pair, block, ROWS:] = ph
            out = mm(vt_ref[cols, :], po) + mm(vht[cols, rows], ph)
            out = jnp.where(row_low, out[:, :REACH], out[:, REACH:])
            mixed[rows, cols] = out.T.astype(BF16)
    projected = mm(mixed[...], wo_ref[...])
    hidden = (x_ref[...].astype(F32) + projected).astype(BF16)
    decoded = mm(hidden, wd_ref[...]).T
    dec_ref[...] = decoded
    dech_ref[...] = decoded.astype(BF16)


def band_index():
    return (lax.axis_index("y") * 2 + lax.axis_index("zl")) * 4 + lax.axis_index("x")


def selector(node_ref):
    node = lax.broadcasted_iota(jnp.int32, (ROWS, PTS), 0) + band_index() * ROWS
    return (node == node_ref[...]).astype(F32).astype(BF16)


def truth_kernel(
    dec_ref, node_ref, truth_ref, n_ref, nh_ref, abs_ref, slope_ref, count_ref, t_ref, own_ref
):
    t_ref[:, :ROWS] = n_ref[...].astype(F32).T.astype(BF16)
    t_ref[:, ROWS:] = nh_ref[...].astype(F32).T.astype(BF16)
    own_ref[...] = dec_ref[...].astype(BF16)
    select = selector(node_ref)
    parts = thirds(dec_ref[...])
    pred = mm(parts[2], select) + mm(parts[1], select) + mm(parts[0], select)
    error = pred - truth_ref[...]
    square = error * error + 0.25
    inverse = lax.rsqrt(square)
    abs_ref[...] = square * inverse
    slope = error * inverse
    high = slope.astype(BF16)
    rest = (slope - high.astype(F32)).astype(BF16)
    slope_ref[...] = mm_nt(high, select) + mm_nt(rest, select)
    count_ref[...] = mm_nt(jnp.ones((16, PTS), BF16), select)[:8]


def backward_kernel(
    probs, wd, wo, dec_ref, oz_ref, oc_ref, slope_ref, count_ref,
    keep_ref, send_ref, spread_ref, mg,
):
    own = dec_ref[...]
    spread = jnp.full((CH, ROWS), 0.5, F32)
    total = jnp.zeros((CH, ROWS), F32)
    for other in [oz_ref[i] for i in range(3)] + [oc_ref[i] for i in range(4)]:
        differ = own - other.astype(F32)
        square = differ * differ + 0.25
        inverse = lax.rsqrt(square)
        spread += square * inverse
        total += differ * inverse
    spread_ref[...] = spread
    node_grad = (slope_ref[...] - count_ref[:1] * total * (1.0 / (MEMBERS - 1))) * (1.0 / MEMBERS)
    high = node_grad.astype(BF16)
    rest = (node_grad - high.astype(F32)).astype(BF16)
    hidden_grad = (mm(wd[...], high) + mm(wd[...], rest)).astype(BF16)
    mg[...] = mm(wo[...], hidden_grad).astype(BF16)
    feature = lax.broadcasted_iota(jnp.int32, (128, REACH), 0)
    low = (feature < 64).astype(F32).astype(BF16)
    high_rows = (feature >= 64).astype(F32).astype(BF16)
    for which, out_ref in ((1, send_ref), (0, keep_ref)):
        for z in range(4):
            pair = 2 * z + (lax.axis_index("core") + which) % 2
            grads = mg[pl.ds(pl.multiple_of(pair * 128, 128), 128), :]
            rows = slice(z * 128, (z + 1) * 128)
            total = None
            for block in range(2):
                part = grads[:, block * REACH : (block + 1) * REACH]
                both = jnp.concatenate([part * low, part * high_rows], axis=1)
                term = mm_nt(both, probs[pair, block, :ROWS])
                total = term if block == 0 else total + term
                edge = slice(ROWS + block * REACH, ROWS + (block + 1) * REACH)
                out_ref[rows, edge] = mm_nt(both, probs[pair, block, ROWS:]).astype(BF16)
            out_ref[rows, :ROWS] = total.astype(BF16)


def product_kernel(t_ref, u_ref, keep_ref, recv_ref, out_ref):
    out_ref[...] = (
        mm_nt(t_ref[...], keep_ref[...]) + mm_nt(u_ref[...], recv_ref[...])
    ).astype(BF16)


def band_kernel(pieces_ref, *rest):
    outs, total = rest[:4], rest[4]
    both = pieces_ref[0].astype(F32)
    for i in range(1, 32):
        both += pieces_ref[i].astype(F32)
    for i in range(4):
        total[i] = both[:, i * 128 : (i + 1) * 128]
    for k in range(4):
        outs[k][...] = total[(lax.axis_index("zh") + k) % 4].astype(BF16)


def stack_kernel(a_ref, b_ref, c_ref, d_ref, out_ref):
    for i, ref in enumerate((a_ref, b_ref, c_ref, d_ref)):
        out_ref[i] = ref[...]


def last_kernel(a_ref, b_ref, c_ref, d_ref, out_ref):
    out_ref[...] = (a_ref[...].astype(F32) + b_ref[...].astype(F32)) + (
        c_ref[...].astype(F32) + d_ref[...].astype(F32)
    )


def crps_kernel(abs_ref, spread_ref, node_ref, out_ref):
    select = selector(node_ref)
    parts = thirds(spread_ref[...])
    spread = mm(parts[2], select) + mm(parts[1], select) + mm(parts[0], select)
    out_ref[...] = abs_ref[...] - spread * (1.0 / (2.0 * (MEMBERS - 1)))


def ring(chunks, axis):
    return [chunks[0]] + [
        lax.ppermute(chunks[k], axis, [(i, (i + k) % 4) for i in range(4)]) for k in (2, 1, 3)
    ]


def body(inputs, norm_gain, w_query, w_key, w_value, w_out, w_decode, point_node, truth):
    states = inputs[0]
    gain = norm_gain[None]
    node = point_node[None]
    up = [(i, i + 1) for i in range(BANDS - 1)]
    down = [(i + 1, i) for i in range(BANDS - 1)]
    swap = [(0, 1), (1, 0)]
    half = ((REACH, D), BF16)
    wide = ((ROWS, D), BF16)
    matrix = ((D, D), BF16)
    here, upper, lower = call(
        split_kernel, [wide, half, half], 0.2, [pltpu.SemaphoreType.DMA((3,))], hbm=1, keep=True
    )(states)
    before = lax.ppermute(upper, GRID, up)
    after = lax.ppermute(lower, GRID, down)
    queries, keys, values, normed, w_key, w_value, w_out, w_decode, gain = call(
        project_kernel,
        [wide, wide, ((D, ROWS), BF16), wide, matrix, matrix, matrix, ((D, CH), BF16), ((1, D), F32)],
        1.6,
        [pltpu.VMEM((D, D), BF16), pltpu.SemaphoreType.DMA((10,))],
        hbm=6,
        keep=True,
    )(w_query, w_key, w_value, w_out, w_decode, gain, here)
    probs, decoded, decoded_half, normed_halo = call(
        attend_kernel,
        [((PAIRS, 2, ROWS + REACH, 2 * REACH), BF16), ((CH, ROWS), F32), ((CH, ROWS), BF16), wide],
        4.0,
        [pltpu.VMEM((ROWS, D), BF16), pltpu.VMEM((D, ROWS), BF16), pltpu.VMEM((ROWS, D), BF16)],
        limit=20,
        keep=True,
    )(before, after, gain, w_key, w_value, queries, keys, values, here, w_out, w_decode)
    along = ring([None, decoded_half, decoded_half, decoded_half], "zh")[1:]
    abs_error, slope, count, turned, own = call(
        truth_kernel,
        [((CH, PTS), F32), ((CH, ROWS), F32), ((8, ROWS), F32), ((D, 2 * ROWS), BF16)]
        + [((CH, ROWS), BF16)],
        2.0,
    )(decoded, node, truth, normed, normed_halo)
    (along,) = call(stack_kernel, [((4, CH, ROWS), BF16)], 0.1)(*along, own)
    across = lax.ppermute(along, "core", swap)
    turned_other = lax.ppermute(turned, "core", swap)
    square = ((512, 512), BF16)
    keep, send, spread = call(
        backward_kernel, [square, square, ((CH, ROWS), F32)], 3.0, [pltpu.VMEM((D, ROWS), BF16)]
    )(probs, w_decode, w_out, decoded, along, across, slope, count)
    received = lax.ppermute(send, "core", swap)
    (product,) = call(product_kernel, [((D, 512), BF16)], 1.1)(turned, turned_other, keep, received)
    pieces = lax.all_to_all(product.reshape(32, 32, 512), GRID, 0, 0)
    columns = call(
        band_kernel, [((32, 128), BF16)] * 4, 0.1, [pltpu.VMEM((4, 32, 128), F32)]
    )(pieces)
    columns = ring(columns, "zh")
    (crps_terms,) = call(crps_kernel, [((CH, PTS), F32)], 1.0)(abs_error, spread, node)
    (grad_value,) = call(last_kernel, [((32, 128), F32)], 0.1)(*columns)
    return crps_terms[None], grad_value


def solution(mesh):
    parts = Mesh(mesh.devices.reshape(4, 2, 4, 2, 4), ("zh", "core", "y", "zl", "x"))
    member = ("zh", "core")
    return jax.shard_map(
        body,
        mesh=parts,
        in_specs=(
            P(member, GRID, None), P(), P(), P(), P(), P(), P(), P(GRID), P(None, GRID),
        ),
        out_specs=(P(member, None, GRID), P(GRID, member)),
        check_vma=False,
    )
```

time: 93.9 us -> 85 us (0.905)
  local copies, waits for them, and re-layouts: 10.7 us -> 0.01 us
  starting transfers between devices: 22 us -> 25.4 us
  Pallas kernels: 18.5 us -> 20.1 us
  waiting for transfers between devices: 12.2 us -> 11.2 us
    unnamed x32 -> x4, local copies, waits for them, and re-layouts: 9.02 us -> 0.01 us
    ppermute x6 -> x8, starting transfers between devices: 16.5 us -> 24.4 us  [the longest x6 18.6 us: ring(): lax.ppermute(chunks[k], axis, [(i, (i + k) % 4) for i in range(4)])]
    all_to_all x1 -> x0, waiting for transfers between devices: 6.61 us -> none  [body(): last = lax.all_to_all(columns, 'zh', 0, 0)]
    all_to_all x1 -> x0, starting transfers between devices: 4.95 us -> none  [body(): last = lax.all_to_all(columns, 'zh', 0, 0)]
    ppermute x6 -> x8, waiting for transfers between devices: 3.77 us -> 8.42 us  [the longest x6 5.11 us: ring(): lax.ppermute(chunks[k], axis, [(i, (i + k) % 4) for i in range(4)])]
    pallas_call x7 -> x10, Pallas kernels: 18.5 us -> 20.1 us  [run(): pl.pallas_call(kernel, out_shape=[other(s, d) for s, d in outs], in_specs...]
    slice x1 -> x0, local copies, waits for them, and re-layouts: 1.07 us -> none  [body(): after = lax.ppermute(states[:REACH], GRID, down)]
    ppermute x1, waiting for transfers between devices: 0.01 us -> 1.02 us  [body(): across = lax.ppermute(along, 'core', swap)]
  transfers between devices with their start and end apart: 10 -> 11, of which waited for: 4 -> 8; matrix products, arithmetic and copies ran while one was open for 0% -> 0% of each run, Pallas kernels for 8% -> 11%
where the time goes in v2:
time: 85 us; the launch traced here: 84.8 us
  blocking collectives  27.3 us (32%)
  starting transfers between devices  25.4 us (30%)
  Pallas kernels  20.1 us (24%)
  waiting for transfers between devices  11.2 us (13%)
    all_to_all x1, blocking collectives, body(): pieces = lax.all_to_all(product.reshape(32, 32, 512), GRID, 0, 0)  27.3 us
    pallas_call x10, Pallas kernels, run(): pl.pallas_call(kernel, out_shape=[other(s, d) for s, d in outs], in_specs...  20.1 us
    ppermute x6, starting transfers between devices, ring(): lax.ppermute(chunks[k], axis, [(i, (i + k) % 4) for i in range(4)])  18.6 us
    ppermute x6, waiting for transfers between devices, ring(): lax.ppermute(chunks[k], axis, [(i, (i + k) % 4) for i in range(4)])  5.11 us
    ppermute x1, starting transfers between devices, body(): before = lax.ppermute(upper, GRID, up)  3.4 us
    ppermute x1, waiting for transfers between devices, body(): after = lax.ppermute(lower, GRID, down)  3.13 us
    ppermute x1, starting transfers between devices, body(): after = lax.ppermute(lower, GRID, down)  2.45 us
    ppermute x1, waiting for transfers between devices, body(): received = lax.ppermute(send, 'core', swap)  1.77 us
  transfers between devices with their start and end apart: 11, of which 8 were waited for; matrix products, arithmetic and copies ran while one was open for 0% of the time, Pallas kernels for 11%

profile of v2, /device:TPU:2, one launch (start us, length us, event | category | flops | bytes accessed | tf_op | source)
XLA Modules:
  0.0 84.8 jit_solution(15233190770631437254)
XLA Ops:
  0.6 1.2 %shard_map.104 = (bf16[256,1024]{1,0:T(8,128)(2,1)S(1)}, bf16[128,1024]{1,0:T(8,128)(2,1)S(1)}, bf16[128,1024]{1,0:T(8,128)(2,1)S(1)}) custom-call(bf16[256,1024]{1,0:T(8,128)(2,1)} %bitcast.9), custom_call_target="tpu_custom_call" | custom-call | flops 200000000 | bytes 600000 | tf_op jit(solution)/shard_map/pallas_call | solution.py:55
  1.9 3.4 %collective-permute-start = (bf16[128,1024]{1,0:T(8,128)(2,1)S(1)}, bf16[128,1024]{1,0:T(8,128)(2,1)S(1)}, u32[]{:S(2)}, u32[]{:S(2)}) collective-permute-start(bf16[128,1024]{1,0:T(8,128)(2,1)S(1)} %get-tuple-element.30), channel_id=1, source_target_pairs={{0,1},{1,2},{2,3},{3,4},{4,5},{5,6},{6,7},{7,8},{8,9},{9,10},{10,1... | collective-permute-start | bytes 786440 | tf_op jit(solution)/shard_map/ppermute | solution.py:289
  5.3 2.5 %collective-permute-start.1 = (bf16[128,1024]{1,0:T(8,128)(2,1)S(1)}, bf16[128,1024]{1,0:T(8,128)(2,1)S(1)}, u32[]{:S(2)}, u32[]{:S(2)}) collective-permute-start(bf16[128,1024]{1,0:T(8,128)(2,1)S(1)} %get-tuple-element.31), channel_id=1, source_target_pairs={{1,0},{2,1},{3,2},{4,3},{5,4},{6,5},{7,6},{8,7},{9,8},{10,9},{11,1... | collective-permute-start | bytes 786440 | tf_op jit(solution)/shard_map/ppermute | solution.py:290
  7.7 3.9 %shard_map.105 = (bf16[256,1024]{1,0:T(8,128)(2,1)S(1)}, bf16[256,1024]{1,0:T(8,128)(2,1)S(1)}, bf16[1024,256]{1,0:T(8,128)(2,1)S(1)}, bf16[256,1024]{1,0:T(8,12...) custom-call(bf16[1024,1024]{1,0:T(8,128)(2,1)} %wq_hbm.1, ...), custom_call_target="tpu_custom_call" | custom-call | flops 1600000000 | bytes 4800000 | tf_op jit(solution)/shard_map/pallas_call | solution.py:55
  11.6 0.2 collective-permute-done.xb_ref
  11.8 3.1 %collective-permute-done.1.xa_ref = bf16[128,1024]{1,0:T(8,128)(2,1)S(1)} collective-permute-done((bf16[128,1024]{1,0:T(8,128)(2,1)S(1)}, bf16[128,1024]{1,0:T(8,128)(2,1)S(1)}, u32[]{:S(2)}, u32[]{:S(2)}) %collective-permute-start.1) | collective-permute-done | bytes 262176 | tf_op jit(solution)/shard_map/ppermute | solution.py:290
  14.9 0.0 copy-start
  14.9 0.0 copy-start.1
  14.9 7.6 %shard_map.106 = (bf16[8,2,384,256]{3,2,1,0:T(8,128)(2,1)S(1)}, f32[128,256]{1,0:T(8,128)S(1)}, bf16[128,256]{1,0:T(8,128)(2,1)S(1)}, bf16[256,1024]{1,0:T(8,128)(2,1)S(1)}) custom-call(bf16[128,1024]{1,0:T(8,128)(2,1)S(1)} %collective-permute-done.xb_ref, bf16[128,1024]{1,0:T(8,128)(2,1)S(1)} %collective-permute-done.1.xa_ref, ...), custom_call_target="tpu_custom_call" | custom-call | flops 4000000000 | bytes 12000000 | tf_op jit(solution)/shard_map/pallas_call | solution.py:55
  22.6 6.4 %collective-permute-start.4 = (bf16[128,256]{1,0:T(8,128)(2,1)S(1)}, bf16[128,256]{1,0:T(8,128)(2,1)S(1)}, u32[]{:S(2)}, u32[]{:S(2)}) collective-permute-start(bf16[128,256]{1,0:T(8,128)(2,1)S(1)} %get-tuple-element.46), channel_id=1, source_target_pairs={{0,192},{64,0},{128,64},{192,128},{1,193},{65,1},{129,65},{193,129... | collective-permute-start | bytes 196616 | tf_op jit(solution)/shard_map/ppermute | solution.py:272
  28.9 0.0 collective-permute-start.3
  28.9 3.8 %collective-permute-start.2 = (bf16[128,256]{1,0:T(8,128)(2,1)S(1)}, bf16[128,256]{1,0:T(8,128)(2,1)S(1)}, u32[]{:S(2)}, u32[]{:S(2)}) collective-permute-start(bf16[128,256]{1,0:T(8,128)(2,1)S(1)} %get-tuple-element.46), channel_id=1, source_target_pairs={{0,128},{64,192},{128,0},{192,64},{1,129},{65,193},{129,1},{193,65... | collective-permute-start | bytes 196616 | tf_op jit(solution)/shard_map/ppermute | solution.py:272
  32.8 0.0 copy-done
  32.8 0.0 copy-done.1
  32.8 1.0 %shard_map.107 = (f32[128,1024]{1,0:T(8,128)S(1)}, f32[128,256]{1,0:T(8,128)S(1)}, f32[8,256]{1,0:T(8,128)S(1)}, bf16[1024,512]{1,0:T(8,128)(2,1)S(1)}, bf16[128,256]{1,0:T(8,128)(2,1)S(1)}) custom-call(f32[128,256]{1,0:T(8,128)S(1)} %get-tuple-element.41.dec_ref, s32[1,1024]{1,0:T(1,128)S(1)} %bitcast.6, f32[128,1024]{1,0:T(8,128)S(1)} %copy-done, ...), custom_call_target="tpu_custom_call" | custom-call | flops 2000000000 | bytes 6000000 | tf_op jit(solution)/shard_map/pallas_call | solution.py:55
  33.8 0.0 collective-permute-done.4.c_ref
  33.8 2.3 %collective-permute-done.3.b_ref = bf16[128,256]{1,0:T(8,128)(2,1)S(1)} collective-permute-done((bf16[128,256]{1,0:T(8,128)(2,1)S(1)}, bf16[128,256]{1,0:T(8,128)(2,1)S(1)}, u32[]{:S(2)}, u32[]{:S(2)}) %collective-permute-start.3) | collective-permute-done | bytes 65568 | tf_op jit(solution)/shard_map/ppermute | solution.py:272
  36.1 1.2 %collective-permute-done.2.a_ref = bf16[128,256]{1,0:T(8,128)(2,1)S(1)} collective-permute-done((bf16[128,256]{1,0:T(8,128)(2,1)S(1)}, bf16[128,256]{1,0:T(8,128)(2,1)S(1)}, u32[]{:S(2)}, u32[]{:S(2)}) %collective-permute-start.2) | collective-permute-done | bytes 65568 | tf_op jit(solution)/shard_map/ppermute | solution.py:272
  37.3 0.3 collective-permute-start.5
  37.5 0.5 collective-permute-start.6
  38.0 1.0 %collective-permute-done.5.oc_ref = bf16[4,128,256]{2,1,0:T(8,128)(2,1)S(1)} collective-permute-done((bf16[4,128,256]{2,1,0:T(8,128)(2,1)S(1)}, bf16[4,128,256]{2,1,0:T(8,128)(2,1)S(1)}, u32[]{:S(2)}, u32[]{:S(2)}) %collective-permute-start.5) | collective-permute-done | bytes 262176 | tf_op jit(solution)/shard_map/ppermute | solution.py:315
  39.1 3.1 %shard_map.109 = (bf16[512,512]{1,0:T(8,128)(2,1)S(1)}, bf16[512,512]{1,0:T(8,128)(2,1)S(1)}, f32[128,256]{1,0:T(8,128)S(1)}) custom-call(bf16[8,2,384,256]{3,2,1,0:T(8,128)(2,1)S(1)} %get-tuple-element.45.probs, bf16[1024,128]{1,0:T(8,128)(2,1)S(1)} %get-tuple-element.40.wd_ref.wd, bf16[1024,1024]{1,0:T(8,128)(2,1)S(1)} %get-tuple-element.39.wo_ref.wo, ...), custom_call_target="tpu_custom_call" | custom-call | flops 3000000000 | bytes 9000000 | tf_op jit(solution)/shard_map/pallas_call | solution.py:55
  42.2 0.2 collective-permute-start.7
  42.4 1.8 %collective-permute-done.7.recv_ref = bf16[512,512]{1,0:T(8,128)(2,1)S(1)} collective-permute-done((bf16[512,512]{1,0:T(8,128)(2,1)S(1)}, bf16[512,512]{1,0:T(8,128)(2,1)S(1)}, u32[]{:S(2)}, u32[]{:S(2)}) %collective-permute-start.7) | collective-permute-done | bytes 524320 | tf_op jit(solution)/shard_map/ppermute | solution.py:321
  44.2 0.0 collective-permute-done.6.u_ref
  44.2 1.3 %shard_map.111 = bf16[1024,512]{1,0:T(8,128)(2,1)S(1)} custom-call(bf16[1024,512]{1,0:T(8,128)(2,1)S(1)} %get-tuple-element.51.t_ref, bf16[1024,512]{1,0:T(8,128)(2,1)S(1)} %collective-permute-done.6.u_ref, bf16[512,512]{1,0:T(8,128)(2,1)S(1)} %get-tuple-element.52.keep_ref, bf16[512,512]{1,0:T(8,128)(2,1)S(1)} %collective-permute-done.7.recv_ref), custom_call_target="tpu_custom_call" | custom-call | flops 1100000000 | bytes 3300000 | tf_op jit(solution)/shard_map/pallas_call | solution.py:55
  45.5 27.3 %all_to_all.5.pieces_ref = bf16[32,32,512]{2,1,0:T(8,128)(2,1)S(1)} all-to-all(bf16[32,32,512]{2,1,0:T(8,128)(2,1)S(1)} %bitcast.5), channel_id=1, replica_groups=mesh['zh'=4,'core'=2,'y'=4,'zl'=2,'x'=4] {'y','zl','x'}, dimensions={0} | all-to-all | bytes 2097152 | tf_op jit(solution)/shard_map/all_to_all | solution.py:323
  72.8 0.1 shard_map.112
  73.0 4.2 %collective-permute-start.8 = (bf16[32,128]{1,0:T(8,128)(2,1)S(1)}, bf16[32,128]{1,0:T(8,128)(2,1)S(1)}, u32[]{:S(2)}, u32[]{:S(2)}) collective-permute-start(bf16[32,128]{1,0:T(8,128)(2,1)S(1)} %get-tuple-element.55), channel_id=1, source_target_pairs={{0,128},{64,192},{128,0},{192,64},{1,129},{65,193},{129,1},{193,65... | collective-permute-start | bytes 24584 | tf_op jit(solution)/shard_map/ppermute | solution.py:272
  77.2 2.5 %collective-permute-start.9 = (bf16[32,128]{1,0:T(8,128)(2,1)S(1)}, bf16[32,128]{1,0:T(8,128)(2,1)S(1)}, u32[]{:S(2)}, u32[]{:S(2)}) collective-permute-start(bf16[32,128]{1,0:T(8,128)(2,1)S(1)} %get-tuple-element.56), channel_id=1, source_target_pairs={{0,64},{64,128},{128,192},{192,0},{1,65},{65,129},{129,193},{193,1... | collective-permute-start | bytes 24584 | tf_op jit(solution)/shard_map/ppermute | solution.py:272
  79.7 1.7 %collective-permute-start.10 = (bf16[32,128]{1,0:T(8,128)(2,1)S(1)}, bf16[32,128]{1,0:T(8,128)(2,1)S(1)}, u32[]{:S(2)}, u32[]{:S(2)}) collective-permute-start(bf16[32,128]{1,0:T(8,128)(2,1)S(1)} %get-tuple-element.57), channel_id=1, source_target_pairs={{0,192},{64,0},{128,64},{192,128},{1,193},{65,1},{129,65},{193,129... | collective-permute-start | bytes 24584 | tf_op jit(solution)/shard_map/ppermute | solution.py:272
  81.3 1.2 %shard_map.110 = f32[128,1024]{1,0:T(8,128)} custom-call(f32[128,1024]{1,0:T(8,128)S(1)} %get-tuple-element.44.abs_ref, f32[128,256]{1,0:T(8,128)S(1)} %get-tuple-element.50.spread_ref, s32[1,1024]{1,0:T(1,128)S(1)} %bitcast.7), custom_call_target="tpu_custom_call" | custom-call | flops 1000000000 | bytes 3000000 | tf_op jit(solution)/shard_map/pallas_call | solution.py:55
  82.6 0.0 collective-permute-done.8.b_ref
  82.6 0.4 collective-permute-done.9.c_ref
  83.0 1.3 %collective-permute-done.10.d_ref = bf16[32,128]{1,0:T(8,128)(2,1)S(1)} collective-permute-done((bf16[32,128]{1,0:T(8,128)(2,1)S(1)}, bf16[32,128]{1,0:T(8,128)(2,1)S(1)}, u32[]{:S(2)}, u32[]{:S(2)}) %collective-permute-start.10) | collective-permute-done | bytes 8224 | tf_op jit(solution)/shard_map/ppermute | solution.py:272
  84.2 0.6 shard_map.113
  (1 shorter events, 0.0 us)
Async XLA Ops:
  1.9 9.9 %collective-permute-start = (bf16[128,1024]{1,0:T(8,128)(2,1)S(1)}, bf16[128,1024]{1,0:T(8,128)(2,1)S(1)}, u32[]{:S(2)}, u32[]{:S(2)}) collective-permute-start(bf16[128,1024]{1,0:T(8,128)(2,1)S(1)} %get-tuple-element.30), channel_id=1, source_target_pairs={{0,1},{1,2},{2,3},{3,4},{4,5},{5,6},{6,7},{7,8},{8,9},{9,10},{10,1... | collective-permute-start | bytes 786440 | tf_op jit(solution)/shard_map/ppermute | solution.py:289
  5.3 9.7 %collective-permute-start.1 = (bf16[128,1024]{1,0:T(8,128)(2,1)S(1)}, bf16[128,1024]{1,0:T(8,128)(2,1)S(1)}, u32[]{:S(2)}, u32[]{:S(2)}) collective-permute-start(bf16[128,1024]{1,0:T(8,128)(2,1)S(1)} %get-tuple-element.31), channel_id=1, source_target_pairs={{1,0},{2,1},{3,2},{4,3},{5,4},{6,5},{7,6},{8,7},{9,8},{10,9},{11,1... | collective-permute-start | bytes 786440 | tf_op jit(solution)/shard_map/ppermute | solution.py:290
  14.9 17.8 %copy-start = (f32[128,1024]{1,0:T(8,128)S(1)}, f32[128,1024]{1,0:T(8,128)}, u32[]{:S(2)}) copy-start(f32[128,1024]{1,0:T(8,128)} %truth_ref.1) | copy-start | bytes 1572868
  14.9 17.8 %copy-start.1 = (s32[1024]{0:T(1024)S(1)}, s32[1024]{0:T(1024)}, u32[]{:S(2)}) copy-start(s32[1024]{0:T(1024)} %param.16) | copy-start | bytes 12292
  22.6 11.2 %collective-permute-start.4 = (bf16[128,256]{1,0:T(8,128)(2,1)S(1)}, bf16[128,256]{1,0:T(8,128)(2,1)S(1)}, u32[]{:S(2)}, u32[]{:S(2)}) collective-permute-start(bf16[128,256]{1,0:T(8,128)(2,1)S(1)} %get-tuple-element.46), channel_id=1, source_target_pairs={{0,192},{64,0},{128,64},{192,128},{1,193},{65,1},{129,65},{193,129... | collective-permute-start | bytes 196616 | tf_op jit(solution)/shard_map/ppermute | solution.py:272
  28.9 7.1 %collective-permute-start.3 = (bf16[128,256]{1,0:T(8,128)(2,1)S(1)}, bf16[128,256]{1,0:T(8,128)(2,1)S(1)}, u32[]{:S(2)}, u32[]{:S(2)}) collective-permute-start(bf16[128,256]{1,0:T(8,128)(2,1)S(1)} %get-tuple-element.46), channel_id=1, source_target_pairs={{0,64},{64,128},{128,192},{192,0},{1,65},{65,129},{129,193},{193,1... | collective-permute-start | bytes 196616 | tf_op jit(solution)/shard_map/ppermute | solution.py:272
  28.9 8.3 %collective-permute-start.2 = (bf16[128,256]{1,0:T(8,128)(2,1)S(1)}, bf16[128,256]{1,0:T(8,128)(2,1)S(1)}, u32[]{:S(2)}, u32[]{:S(2)}) collective-permute-start(bf16[128,256]{1,0:T(8,128)(2,1)S(1)} %get-tuple-element.46), channel_id=1, source_target_pairs={{0,128},{64,192},{128,0},{192,64},{1,129},{65,193},{129,1},{193,65... | collective-permute-start | bytes 196616 | tf_op jit(solution)/shard_map/ppermute | solution.py:272
  37.3 1.8 %collective-permute-start.5 = (bf16[4,128,256]{2,1,0:T(8,128)(2,1)S(1)}, bf16[4,128,256]{2,1,0:T(8,128)(2,1)S(1)}, u32[]{:S(2)}, u32[]{:S(2)}) collective-permute-start(bf16[4,128,256]{2,1,0:T(8,128)(2,1)S(1)} %shard_map.108.oz_ref), channel_id=1, source_target_pairs={{0,32},{32,0},{1,33},{33,1},{2,34},{34,2},{3,35},{35,3},{4,36},{36... | collective-permute-start | bytes 786440 | tf_op jit(solution)/shard_map/ppermute | solution.py:315
  37.5 6.7 %collective-permute-start.6 = (bf16[1024,512]{1,0:T(8,128)(2,1)S(1)}, bf16[1024,512]{1,0:T(8,128)(2,1)S(1)}, u32[]{:S(2)}, u32[]{:S(2)}) collective-permute-start(bf16[1024,512]{1,0:T(8,128)(2,1)S(1)} %get-tuple-element.51.t_ref), channel_id=1, source_target_pairs={{0,32},{32,0},{1,33},{33,1},{2,34},{34,2},{3,35},{35,3},{4,36},{36... | collective-permute-start | bytes 3145736 | tf_op jit(solution)/shard_map/ppermute | solution.py:316
  42.2 2.0 %collective-permute-start.7 = (bf16[512,512]{1,0:T(8,128)(2,1)S(1)}, bf16[512,512]{1,0:T(8,128)(2,1)S(1)}, u32[]{:S(2)}, u32[]{:S(2)}) collective-permute-start(bf16[512,512]{1,0:T(8,128)(2,1)S(1)} %get-tuple-element.53), channel_id=1, source_target_pairs={{0,32},{32,0},{1,33},{33,1},{2,34},{34,2},{3,35},{35,3},{4,36},{36... | collective-permute-start | bytes 1572872 | tf_op jit(solution)/shard_map/ppermute | solution.py:321
  73.0 9.6 %collective-permute-start.8 = (bf16[32,128]{1,0:T(8,128)(2,1)S(1)}, bf16[32,128]{1,0:T(8,128)(2,1)S(1)}, u32[]{:S(2)}, u32[]{:S(2)}) collective-permute-start(bf16[32,128]{1,0:T(8,128)(2,1)S(1)} %get-tuple-element.55), channel_id=1, source_target_pairs={{0,128},{64,192},{128,0},{192,64},{1,129},{65,193},{129,1},{193,65... | collective-permute-start | bytes 24584 | tf_op jit(solution)/shard_map/ppermute | solution.py:272
  77.2 5.8 %collective-permute-start.9 = (bf16[32,128]{1,0:T(8,128)(2,1)S(1)}, bf16[32,128]{1,0:T(8,128)(2,1)S(1)}, u32[]{:S(2)}, u32[]{:S(2)}) collective-permute-start(bf16[32,128]{1,0:T(8,128)(2,1)S(1)} %get-tuple-element.56), channel_id=1, source_target_pairs={{0,64},{64,128},{128,192},{192,0},{1,65},{65,129},{129,193},{193,1... | collective-permute-start | bytes 24584 | tf_op jit(solution)/shard_map/ppermute | solution.py:272
  79.7 4.5 %collective-permute-start.10 = (bf16[32,128]{1,0:T(8,128)(2,1)S(1)}, bf16[32,128]{1,0:T(8,128)(2,1)S(1)}, u32[]{:S(2)}, u32[]{:S(2)}) collective-permute-start(bf16[32,128]{1,0:T(8,128)(2,1)S(1)} %get-tuple-element.57), channel_id=1, source_target_pairs={{0,192},{64,0},{128,64},{192,128},{1,193},{65,1},{129,65},{193,129... | collective-permute-start | bytes 24584 | tf_op jit(solution)/shard_map/ppermute | solution.py:272

commit v3 on v2

--- a/solution.py
+++ b/solution.py
@@ -67,11 +67,10 @@
     return run
 
 
-def split_kernel(x_hbm, x_ref, up_ref, down_ref, sems):
+def split_kernel(x_hbm, up_ref, down_ref, sems):
     copies = [
         pltpu.make_async_copy(x_hbm.at[REACH:], up_ref, sems.at[0]),
         pltpu.make_async_copy(x_hbm.at[:REACH], down_ref, sems.at[1]),
-        pltpu.make_async_copy(x_hbm, x_ref, sems.at[2]),
     ]
     for copy in copies:
         copy.start()
@@ -79,12 +78,24 @@
         copy.wait()
 
 
+def head_parts():
+    lane = lax.broadcasted_iota(jnp.int32, (REACH, 128), 1)
+    low = (lane < 64).astype(F32).astype(BF16)
+    high = (lane >= 64).astype(F32).astype(BF16)
+    row_low = lax.broadcasted_iota(jnp.int32, (128, REACH), 0) < 64
+    key = lax.broadcasted_iota(jnp.int32, (REACH, 2 * REACH), 0)
+    query = lax.broadcasted_iota(jnp.int32, (REACH, 2 * REACH), 1) % REACH
+    return low, high, row_low, key, query
+
+
 def project_kernel(
-    wq_hbm, wk_hbm, wv_hbm, wo_hbm, wd_hbm, gain_hbm, x_ref,
-    q_ref, k_ref, vt_ref, n_ref, wk_ref, wv_ref, wo_ref, wd_ref, gain_ref, wq, sems,
+    wq_hbm, wk_hbm, wv_hbm, wo_hbm, wd_hbm, gain_hbm, x_hbm,
+    q_ref, n_ref, x_ref, wk_ref, wv_ref, wo_ref, wd_ref, gain_ref, e_ref, out_ref, top_ref, sum_ref,
+    wq, k, vt, sems,
 ):
     half = D // 2
-    copies = [pltpu.make_async_copy(gain_hbm, gain_ref, sems.at[0])]
+    copies = [pltpu.make_async_copy(x_hbm, x_ref, sems.at[0])]
+    copies.append(pltpu.make_async_copy(gain_hbm, gain_ref, sems.at[1]))
     for hbm, vmem in ((wq_hbm, wq), (wk_hbm, wk_ref), (wv_hbm, wv_ref), (wo_hbm, wo_ref)):
         for j in range(2):
             rows = slice(j * half, (j + 1) * half)
@@ -95,24 +106,50 @@
     for copy in copies:
         copy.start()
     copies[0].wait()
+    copies[1].wait()
     normed = rms(x_ref[...], gain_ref[...])
     n_ref[...] = normed
-    copies[1].wait()
     copies[2].wait()
+    copies[3].wait()
     q_ref[...] = mm(normed, wq[...]).astype(BF16) * jnp.asarray(0.125, BF16)
-    copies[3].wait()
     copies[4].wait()
-    k_ref[...] = mm(normed, wk_ref[...]).astype(BF16)
     copies[5].wait()
+    k[...] = mm(normed, wk_ref[...]).astype(BF16)
     copies[6].wait()
-    vt_ref[...] = mm(normed, wv_ref[...]).T.astype(BF16)
-    for copy in copies[7:]:
+    copies[7].wait()
+    vt[...] = mm(normed, wv_ref[...]).T.astype(BF16)
+    low, high, row_low, key, query = head_parts()
+    before = jnp.where(key <= query, 0.0, MASKED)
+    after = jnp.where(key >= query, 0.0, MASKED)
+    for block in range(2):
+        rows = slice(block * REACH, (block + 1) * REACH)
+        for pair in range(PAIRS):
+            cols = slice(pair * 128, (pair + 1) * 128)
+            both = q_ref[rows, cols]
+            stacked = jnp.concatenate([both * low, both * high], axis=0)
+            s0 = mm_nt(k[:REACH, cols], stacked)
+            s1 = mm_nt(k[REACH:, cols], stacked)
+            if block == 0:
+                s1 += before
+            else:
+                s0 += after
+            top = jnp.max(jnp.maximum(s0, s1), axis=0, keepdims=True)
+            e0 = jnp.exp(s0 - top)
+            e1 = jnp.exp(s1 - top)
+            n = pair * 2 + block
+            top_ref[n : n + 1] = top
+            sum_ref[n : n + 1] = jnp.sum(e0 + e1, axis=0, keepdims=True)
+            e = jnp.concatenate([e0.astype(BF16), e1.astype(BF16)], axis=0)
+            e_ref[pair, block] = e
+            out = mm(vt[cols, :], e)
+            out_ref[pair, block] = jnp.where(row_low, out[:, :REACH], out[:, REACH:])
+    for copy in copies[8:]:
         copy.wait()
 
 
 def attend_kernel(
-    xb_ref, xa_ref, gain_ref, wk_ref, wv_ref, q_ref, k_ref, vt_ref, x_ref, wo_ref, wd_ref,
-    probs, dec_ref, dech_ref, nh_ref, kh, vht, mixed,
+    xb_ref, xa_ref, gain_ref, wk_ref, wv_ref, q_ref, out_ref, top_ref, sum_ref, x_ref, wo_ref, wd_ref,
+    e_ref, factor_ref, dec_ref, dech_ref, nh_ref, kh, vht, mixed,
 ):
     band = band_index()
     gain = gain_ref[...]
@@ -121,14 +158,7 @@
     halo = nh_ref[...]
     kh[...] = mm(halo, wk_ref[...]).astype(BF16)
     vht[...] = mm(halo, wv_ref[...]).T.astype(BF16)
-    lane = lax.broadcasted_iota(jnp.int32, (REACH, 128), 1)
-    low = (lane < 64).astype(F32).astype(BF16)
-    high = (lane >= 64).astype(F32).astype(BF16)
-    row_low = lax.broadcasted_iota(jnp.int32, (128, REACH), 0) < 64
-    key = lax.broadcasted_iota(jnp.int32, (REACH, 2 * REACH), 0)
-    query = lax.broadcasted_iota(jnp.int32, (REACH, 2 * REACH), 1) % REACH
-    before = jnp.where(key <= query, 0.0, MASKED)
-    after = jnp.where(key >= query, 0.0, MASKED)
+    low, high, row_low, key, query = head_parts()
     first = jnp.where((key >= query) & (band > 0), 0.0, MASKED)
     last = jnp.where((key <= query) & (band < BANDS - 1), 0.0, MASKED)
     for block in range(2):
@@ -137,26 +167,27 @@
             cols = slice(pair * 128, (pair + 1) * 128)
             both = q_ref[rows, cols]
             stacked = jnp.concatenate([both * low, both * high], axis=0)
-            s0 = mm_nt(k_ref[:REACH, cols], stacked)
-            s1 = mm_nt(k_ref[REACH:, cols], stacked)
-            s2 = mm_nt(kh[rows, cols], stacked)
-            if block == 0:
-                s1 += before
-                s2 += first
-            else:
-                s0 += after
-                s2 += last
-            top = jnp.max(jnp.maximum(jnp.maximum(s0, s1), s2), axis=0, keepdims=True)
-            e0 = jnp.exp(s0 - top)
-            e1 = jnp.exp(s1 - top)
-            e2 = jnp.exp(s2 - top)
-            inv = 1.0 / jnp.sum(e0 + e1 + e2, axis=0, keepdims=True)
-            po = jnp.concatenate([(e0 * inv).astype(BF16), (e1 * inv).astype(BF16)], axis=0)
-            ph = (e2 * inv).astype(BF16)
-            probs[pair, block, :ROWS] = po
-            probs[pair, block, ROWS:] = ph
-            out = mm(vt_ref[cols, :], po) + mm(vht[cols, rows], ph)
+            scores = mm_nt(kh[rows, cols], stacked) + (last if block else first)
+            n = pair * 2 + block
+            top_own = top_ref[n : n + 1]
+            top_halo = jnp.max(scores, axis=0, keepdims=True)
+            e = jnp.exp(scores - top_halo)
+            e_ref[pair, block] = e.astype(BF16)
+            top = jnp.maximum(top_own, top_halo)
+            scale_own = jnp.exp(top_own - top)
+            scale_halo = jnp.exp(top_halo - top)
+            inv = 1.0 / (
+                sum_ref[n : n + 1] * scale_own + jnp.sum(e, axis=0, keepdims=True) * scale_halo
+            )
+            scale_own *= inv
+            scale_halo *= inv
+            factor_ref[pair, 2 * block : 2 * block + 1] = scale_own
+            factor_ref[pair, 2 * block + 1 : 2 * block + 2] = scale_halo
+            out = mm(vht[cols, rows], e.astype(BF16)) * scale_halo
             out = jnp.where(row_low, out[:, :REACH], out[:, REACH:])
+            out += out_ref[pair, block] * jnp.where(
+                row_low, scale_own[:, :REACH], scale_own[:, REACH:]
+            )
             mixed[rows, cols] = out.T.astype(BF16)
     projected = mm(mixed[...], wo_ref[...])
     hidden = (x_ref[...].astype(F32) + projected).astype(BF16)
@@ -195,7 +226,7 @@
 
 
 def backward_kernel(
-    probs, wd, wo, dec_ref, oz_ref, oc_ref, slope_ref, count_ref,
+    eo_ref, eh_ref, factor_ref, wd, wo, dec_ref, oz_ref, oc_ref, slope_ref, count_ref,
     keep_ref, send_ref, spread_ref, mg,
 ):
     own = dec_ref[...]
@@ -213,22 +244,25 @@
     rest = (node_grad - high.astype(F32)).astype(BF16)
     hidden_grad = (mm(wd[...], high) + mm(wd[...], rest)).astype(BF16)
     mg[...] = mm(wo[...], hidden_grad).astype(BF16)
-    feature = lax.broadcasted_iota(jnp.int32, (128, REACH), 0)
-    low = (feature < 64).astype(F32).astype(BF16)
-    high_rows = (feature >= 64).astype(F32).astype(BF16)
+    feature = lax.broadcasted_iota(jnp.int32, (128, 2 * REACH), 0)
+    lane = lax.broadcasted_iota(jnp.int32, (128, 2 * REACH), 1)
+    heads = ((feature < 64) == (lane < REACH)).astype(F32)
     for which, out_ref in ((1, send_ref), (0, keep_ref)):
         for z in range(4):
             pair = 2 * z + (lax.axis_index("core") + which) % 2
-            grads = mg[pl.ds(pl.multiple_of(pair * 128, 128), 128), :]
+            grads = mg[pl.ds(pl.multiple_of(pair * 128, 128), 128), :].astype(F32)
             rows = slice(z * 128, (z + 1) * 128)
             total = None
             for block in range(2):
                 part = grads[:, block * REACH : (block + 1) * REACH]
-                both = jnp.concatenate([part * low, part * high_rows], axis=1)
-                term = mm_nt(both, probs[pair, block, :ROWS])
+                both = jnp.concatenate([part, part], axis=1) * heads
+                factors = factor_ref[pair]
+                own = (both * factors[2 * block : 2 * block + 1]).astype(BF16)
+                halo = (both * factors[2 * block + 1 : 2 * block + 2]).astype(BF16)
+                term = mm_nt(own, eo_ref[pair, block])
                 total = term if block == 0 else total + term
                 edge = slice(ROWS + block * REACH, ROWS + (block + 1) * REACH)
-                out_ref[rows, edge] = mm_nt(both, probs[pair, block, ROWS:]).astype(BF16)
+                out_ref[rows, edge] = mm_nt(halo, eh_ref[pair, block]).astype(BF16)
             out_ref[rows, :ROWS] = total.astype(BF16)
 
 
@@ -283,27 +317,42 @@
     half = ((REACH, D), BF16)
     wide = ((ROWS, D), BF16)
     matrix = ((D, D), BF16)
-    here, upper, lower = call(
-        split_kernel, [wide, half, half], 0.2, [pltpu.SemaphoreType.DMA((3,))], hbm=1, keep=True
+    row = ((2 * PAIRS, 2 * REACH), F32)
+    upper, lower = call(
+        split_kernel, [half, half], 0.2, [pltpu.SemaphoreType.DMA((2,))], hbm=1, keep=True
     )(states)
     before = lax.ppermute(upper, GRID, up)
     after = lax.ppermute(lower, GRID, down)
-    queries, keys, values, normed, w_key, w_value, w_out, w_decode, gain = call(
+    (
+        queries, normed, here, w_key, w_value, w_out, w_decode, gain, exp_own, mixed_own, top_own,
+        sum_own,
+    ) = call(
         project_kernel,
-        [wide, wide, ((D, ROWS), BF16), wide, matrix, matrix, matrix, ((D, CH), BF16), ((1, D), F32)],
-        1.6,
-        [pltpu.VMEM((D, D), BF16), pltpu.SemaphoreType.DMA((10,))],
-        hbm=6,
+        [wide, wide, wide, matrix, matrix, matrix, ((D, CH), BF16), ((1, D), F32)]
+        + [((PAIRS, 2, ROWS, 2 * REACH), BF16), ((PAIRS, 2, 128, REACH), F32), row, row],
+        3.0,
+        [
+            pltpu.VMEM((D, D), BF16),
+            pltpu.VMEM((ROWS, D), BF16),
+            pltpu.VMEM((D, ROWS), BF16),
+            pltpu.SemaphoreType.DMA((11,)),
+        ],
+        hbm=7,
+        limit=20,
         keep=True,
-    )(w_query, w_key, w_value, w_out, w_decode, gain, here)
-    probs, decoded, decoded_half, normed_halo = call(
+    )(w_query, w_key, w_value, w_out, w_decode, gain, states)
+    exp_halo, factors, decoded, decoded_half, normed_halo = call(
         attend_kernel,
-        [((PAIRS, 2, ROWS + REACH, 2 * REACH), BF16), ((CH, ROWS), F32), ((CH, ROWS), BF16), wide],
-        4.0,
+        [((PAIRS, 2, REACH, 2 * REACH), BF16), ((PAIRS, 4, 2 * REACH), F32)]
+        + [((CH, ROWS), F32), ((CH, ROWS), BF16), wide],
+        3.0,
         [pltpu.VMEM((ROWS, D), BF16), pltpu.VMEM((D, ROWS), BF16), pltpu.VMEM((ROWS, D), BF16)],
         limit=20,
         keep=True,
-    )(before, after, gain, w_key, w_value, queries, keys, values, here, w_out, w_decode)
+    )(
+        before, after, gain, w_key, w_value, queries, mixed_own, top_own, sum_own, here, w_out,
+        w_decode,
+    )
     along = ring([None, decoded_half, decoded_half, decoded_half], "zh")[1:]
     abs_error, slope, count, turned, own = call(
         truth_kernel,
@@ -317,7 +366,7 @@
     square = ((512, 512), BF16)
     keep, send, spread = call(
         backward_kernel, [square, square, ((CH, ROWS), F32)], 3.0, [pltpu.VMEM((D, ROWS), BF16)]
-    )(probs, w_decode, w_out, decoded, along, across, slope, count)
+    )(exp_own, exp_halo, factors, w_decode, w_out, decoded, along, across, slope, count)
     received = lax.ppermute(send, "core", swap)
     (product,) = call(product_kernel, [((D, 512), BF16)], 1.1)(turned, turned_other, keep, received)
     pieces = lax.all_to_all(product.reshape(32, 32, 512), GRID, 0, 0)

time: 85 us -> 80.5 us (0.947)
  waiting for transfers between devices: 11.2 us -> 7.85 us
  blocking collectives: 27.3 us -> 26.4 us
    ppermute x1, waiting for transfers between devices: 3.13 us -> 0.01 us  [body(): after = lax.ppermute(lower, GRID, down)]
    all_to_all x1, blocking collectives: 27.3 us -> 26.4 us  [body(): pieces = lax.all_to_all(product.reshape(32, 32, 512), GRID, 0, 0)]
  transfers between devices with their start and end apart: 11 -> 11, of which waited for: 8 -> 6; matrix products, arithmetic and copies ran while one was open for 0% -> 0% of each run, Pallas kernels for 11% -> 17%
where the time goes in v3:
time: 80.5 us; the launch traced here: 80.3 us
  blocking collectives  26.4 us (33%)
  starting transfers between devices  25.2 us (31%)
  Pallas kernels  20 us (25%)
  waiting for transfers between devices  7.85 us (10%)
    all_to_all x1, blocking collectives, body(): pieces = lax.all_to_all(product.reshape(32, 32, 512), GRID, 0, 0)  26.4 us
    pallas_call x10, Pallas kernels, run(): pl.pallas_call(kernel, out_shape=[other(s, d) for s, d in outs], in_specs...  20 us
    ppermute x6, starting transfers between devices, ring(): lax.ppermute(chunks[k], axis, [(i, (i + k) % 4) for i in range(4)])  18.6 us
    ppermute x6, waiting for transfers between devices, ring(): lax.ppermute(chunks[k], axis, [(i, (i + k) % 4) for i in range(4)])  5.04 us
    ppermute x1, starting transfers between devices, body(): before = lax.ppermute(upper, GRID, up)  3.4 us
    ppermute x1, starting transfers between devices, body(): after = lax.ppermute(lower, GRID, down)  2.45 us
    ppermute x1, waiting for transfers between devices, body(): received = lax.ppermute(send, 'core', swap)  1.77 us
  transfers between devices with their start and end apart: 11, of which 6 were waited for; matrix products, arithmetic and copies ran while one was open for 0% of the time, Pallas kernels for 17%

profile of v3, /device:TPU:2, one launch (start us, length us, event | category | flops | bytes accessed | tf_op | source)
XLA Modules:
  0.0 80.3 jit_solution(1739073090935376095)
XLA Ops:
  0.6 1.1 %shard_map.104 = (bf16[128,1024]{1,0:T(8,128)(2,1)S(1)}, bf16[128,1024]{1,0:T(8,128)(2,1)S(1)}) custom-call(bf16[256,1024]{1,0:T(8,128)(2,1)} %bitcast.8), custom_call_target="tpu_custom_call" | custom-call | flops 200000000 | bytes 600000 | tf_op jit(solution)/shard_map/pallas_call | solution.py:55
  1.7 3.4 %collective-permute-start = (bf16[128,1024]{1,0:T(8,128)(2,1)S(1)}, bf16[128,1024]{1,0:T(8,128)(2,1)S(1)}, u32[]{:S(2)}, u32[]{:S(2)}) collective-permute-start(bf16[128,1024]{1,0:T(8,128)(2,1)S(1)} %get-tuple-element.33), channel_id=1, source_target_pairs={{0,1},{1,2},{2,3},{3,4},{4,5},{5,6},{6,7},{7,8},{8,9},{9,10},{10,1... | collective-permute-start | bytes 786440 | tf_op jit(solution)/shard_map/ppermute | solution.py:324
  5.1 2.5 %collective-permute-start.1 = (bf16[128,1024]{1,0:T(8,128)(2,1)S(1)}, bf16[128,1024]{1,0:T(8,128)(2,1)S(1)}, u32[]{:S(2)}, u32[]{:S(2)}) collective-permute-start(bf16[128,1024]{1,0:T(8,128)(2,1)S(1)} %get-tuple-element.34), channel_id=1, source_target_pairs={{1,0},{2,1},{3,2},{4,3},{5,4},{6,5},{7,6},{8,7},{9,8},{10,9},{11,1... | collective-permute-start | bytes 786440 | tf_op jit(solution)/shard_map/ppermute | solution.py:325
  7.6 8.1 %shard_map.105 = (bf16[256,1024]{1,0:T(8,128)(2,1)S(1)}, bf16[256,1024]{1,0:T(8,128)(2,1)S(1)}, bf16[256,1024]{1,0:T(8,128)(2,1)S(1)}, bf16[1024,1024]{1,0:T(8,1...) custom-call(bf16[1024,1024]{1,0:T(8,128)(2,1)} %wq_hbm.1, ...), custom_call_target="tpu_custom_call" | custom-call | flops 3000000000 | bytes 9000000 | tf_op jit(solution)/shard_map/pallas_call | solution.py:55
  15.7 0.0 collective-permute-done.xb_ref
  15.7 0.0 collective-permute-done.1.xa_ref
  15.7 0.0 copy-start
  15.7 0.0 copy-start.1
  15.7 3.4 %shard_map.106 = (bf16[8,2,128,256]{3,2,1,0:T(8,128)(2,1)S(1)}, f32[8,4,256]{2,1,0:T(4,128)S(1)}, f32[128,256]{1,0:T(8,128)S(1)}, bf16[128,256]{1,0:T(8,128)(2,1)S(1)}, bf16[256,1024]{1,0:T(8,128)(2,1)S(1)}) custom-call(bf16[128,1024]{1,0:T(8,128)(2,1)S(1)} %collective-permute-done.xb_ref, bf16[128,1024]{1,0:T(8,128)(2,1)S(1)} %collective-permute-done.1.xa_ref, ...), custom_call_target="tpu_custom_call" | custom-call | flops 3000000000 | bytes 9000000 | tf_op jit(solution)/shard_map/pallas_call | solution.py:55
  19.1 6.4 %collective-permute-start.4 = (bf16[128,256]{1,0:T(8,128)(2,1)S(1)}, bf16[128,256]{1,0:T(8,128)(2,1)S(1)}, u32[]{:S(2)}, u32[]{:S(2)}) collective-permute-start(bf16[128,256]{1,0:T(8,128)(2,1)S(1)} %get-tuple-element.52), channel_id=1, source_target_pairs={{0,192},{64,0},{128,64},{192,128},{1,193},{65,1},{129,65},{193,129... | collective-permute-start | bytes 196616 | tf_op jit(solution)/shard_map/ppermute | solution.py:306
  25.5 0.0 collective-permute-start.3
  25.5 3.8 %collective-permute-start.2 = (bf16[128,256]{1,0:T(8,128)(2,1)S(1)}, bf16[128,256]{1,0:T(8,128)(2,1)S(1)}, u32[]{:S(2)}, u32[]{:S(2)}) collective-permute-start(bf16[128,256]{1,0:T(8,128)(2,1)S(1)} %get-tuple-element.52), channel_id=1, source_target_pairs={{0,128},{64,192},{128,0},{192,64},{1,129},{65,193},{129,1},{193,65... | collective-permute-start | bytes 196616 | tf_op jit(solution)/shard_map/ppermute | solution.py:306
  29.3 0.0 copy-done
  29.3 0.0 copy-done.1
  29.3 1.0 %shard_map.107 = (f32[128,1024]{1,0:T(8,128)S(1)}, f32[128,256]{1,0:T(8,128)S(1)}, f32[8,256]{1,0:T(8,128)S(1)}, bf16[1024,512]{1,0:T(8,128)(2,1)S(1)}, bf16[128,256]{1,0:T(8,128)(2,1)S(1)}) custom-call(f32[128,256]{1,0:T(8,128)S(1)} %get-tuple-element.45.dec_ref, s32[1,1024]{1,0:T(1,128)S(1)} %bitcast.6, f32[128,1024]{1,0:T(8,128)S(1)} %copy-done, ...), custom_call_target="tpu_custom_call" | custom-call | flops 2000000000 | bytes 6000000 | tf_op jit(solution)/shard_map/pallas_call | solution.py:55
  30.3 0.0 collective-permute-done.4.c_ref
  30.4 2.6 %collective-permute-done.3.b_ref = bf16[128,256]{1,0:T(8,128)(2,1)S(1)} collective-permute-done((bf16[128,256]{1,0:T(8,128)(2,1)S(1)}, bf16[128,256]{1,0:T(8,128)(2,1)S(1)}, u32[]{:S(2)}, u32[]{:S(2)}) %collective-permute-start.3) | collective-permute-done | bytes 65568 | tf_op jit(solution)/shard_map/ppermute | solution.py:306
  33.0 0.7 collective-permute-done.2.a_ref
  33.7 0.1 collective-permute-start.5
  33.8 0.5 collective-permute-start.6
  34.3 1.0 %collective-permute-done.5.oc_ref = bf16[4,128,256]{2,1,0:T(8,128)(2,1)S(1)} collective-permute-done((bf16[4,128,256]{2,1,0:T(8,128)(2,1)S(1)}, bf16[4,128,256]{2,1,0:T(8,128)(2,1)S(1)}, u32[]{:S(2)}, u32[]{:S(2)}) %collective-permute-start.5) | collective-permute-done | bytes 262176 | tf_op jit(solution)/shard_map/ppermute | solution.py:364
  35.4 3.2 %shard_map.109 = (bf16[512,512]{1,0:T(8,128)(2,1)S(1)}, bf16[512,512]{1,0:T(8,128)(2,1)S(1)}, f32[128,256]{1,0:T(8,128)S(1)}) custom-call(bf16[8,2,256,256]{3,2,1,0:T(8,128)(2,1)S(1)} %get-tuple-element.49.eo_ref, bf16[8,2,128,256]{3,2,1,0:T(8,128)(2,1)S(1)} %get-tuple-element.50.eh_ref, f32[8,4,256]{2,1,0:T(4,128)S(1)} %get-tuple-element.51.factor_ref, ...), custom_call_target="tpu_custom_call" | custom-call | flops 3000000000 | bytes 9000000 | tf_op jit(solution)/shard_map/pallas_call | solution.py:55
  38.6 0.2 collective-permute-start.7
  38.8 1.8 %collective-permute-done.7.recv_ref = bf16[512,512]{1,0:T(8,128)(2,1)S(1)} collective-permute-done((bf16[512,512]{1,0:T(8,128)(2,1)S(1)}, bf16[512,512]{1,0:T(8,128)(2,1)S(1)}, u32[]{:S(2)}, u32[]{:S(2)}) %collective-permute-start.7) | collective-permute-done | bytes 524320 | tf_op jit(solution)/shard_map/ppermute | solution.py:370
  40.6 0.0 collective-permute-done.6.u_ref
  40.6 1.3 %shard_map.111 = bf16[1024,512]{1,0:T(8,128)(2,1)S(1)} custom-call(bf16[1024,512]{1,0:T(8,128)(2,1)S(1)} %get-tuple-element.57.t_ref, bf16[1024,512]{1,0:T(8,128)(2,1)S(1)} %collective-permute-done.6.u_ref, bf16[512,512]{1,0:T(8,128)(2,1)S(1)} %get-tuple-element.58.keep_ref, bf16[512,512]{1,0:T(8,128)(2,1)S(1)} %collective-permute-done.7.recv_ref), custom_call_target="tpu_custom_call" | custom-call | flops 1100000000 | bytes 3300000 | tf_op jit(solution)/shard_map/pallas_call | solution.py:55
  41.9 26.4 %all_to_all.5.pieces_ref = bf16[32,32,512]{2,1,0:T(8,128)(2,1)S(1)} all-to-all(bf16[32,32,512]{2,1,0:T(8,128)(2,1)S(1)} %bitcast.5), channel_id=1, replica_groups=mesh['zh'=4,'core'=2,'y'=4,'zl'=2,'x'=4] {'y','zl','x'}, dimensions={0} | all-to-all | bytes 2097152 | tf_op jit(solution)/shard_map/all_to_all | solution.py:372
  68.3 0.1 shard_map.112
  68.4 4.2 %collective-permute-start.8 = (bf16[32,128]{1,0:T(8,128)(2,1)S(1)}, bf16[32,128]{1,0:T(8,128)(2,1)S(1)}, u32[]{:S(2)}, u32[]{:S(2)}) collective-permute-start(bf16[32,128]{1,0:T(8,128)(2,1)S(1)} %get-tuple-element.61), channel_id=1, source_target_pairs={{0,128},{64,192},{128,0},{192,64},{1,129},{65,193},{129,1},{193,65... | collective-permute-start | bytes 24584 | tf_op jit(solution)/shard_map/ppermute | solution.py:306
  72.7 2.5 %collective-permute-start.9 = (bf16[32,128]{1,0:T(8,128)(2,1)S(1)}, bf16[32,128]{1,0:T(8,128)(2,1)S(1)}, u32[]{:S(2)}, u32[]{:S(2)}) collective-permute-start(bf16[32,128]{1,0:T(8,128)(2,1)S(1)} %get-tuple-element.62), channel_id=1, source_target_pairs={{0,64},{64,128},{128,192},{192,0},{1,65},{65,129},{129,193},{193,1... | collective-permute-start | bytes 24584 | tf_op jit(solution)/shard_map/ppermute | solution.py:306
  75.1 1.7 %collective-permute-start.10 = (bf16[32,128]{1,0:T(8,128)(2,1)S(1)}, bf16[32,128]{1,0:T(8,128)(2,1)S(1)}, u32[]{:S(2)}, u32[]{:S(2)}) collective-permute-start(bf16[32,128]{1,0:T(8,128)(2,1)S(1)} %get-tuple-element.63), channel_id=1, source_target_pairs={{0,192},{64,0},{128,64},{192,128},{1,193},{65,1},{129,65},{193,129... | collective-permute-start | bytes 24584 | tf_op jit(solution)/shard_map/ppermute | solution.py:306
  76.8 1.2 %shard_map.110 = f32[128,1024]{1,0:T(8,128)} custom-call(f32[128,1024]{1,0:T(8,128)S(1)} %get-tuple-element.48.abs_ref, f32[128,256]{1,0:T(8,128)S(1)} %get-tuple-element.56.spread_ref, s32[1,1024]{1,0:T(1,128)S(1)} %bitcast.7), custom_call_target="tpu_custom_call" | custom-call | flops 1000000000 | bytes 3000000 | tf_op jit(solution)/shard_map/pallas_call | solution.py:55
  78.0 0.0 collective-permute-done.8.b_ref
  78.0 0.4 collective-permute-done.9.c_ref
  78.4 1.3 %collective-permute-done.10.d_ref = bf16[32,128]{1,0:T(8,128)(2,1)S(1)} collective-permute-done((bf16[32,128]{1,0:T(8,128)(2,1)S(1)}, bf16[32,128]{1,0:T(8,128)(2,1)S(1)}, u32[]{:S(2)}, u32[]{:S(2)}) %collective-permute-start.10) | collective-permute-done | bytes 8224 | tf_op jit(solution)/shard_map/ppermute | solution.py:306
  79.7 0.6 shard_map.113
  (1 shorter events, 0.0 us)
Async XLA Ops:
  1.7 14.0 %collective-permute-start = (bf16[128,1024]{1,0:T(8,128)(2,1)S(1)}, bf16[128,1024]{1,0:T(8,128)(2,1)S(1)}, u32[]{:S(2)}, u32[]{:S(2)}) collective-permute-start(bf16[128,1024]{1,0:T(8,128)(2,1)S(1)} %get-tuple-element.33), channel_id=1, source_target_pairs={{0,1},{1,2},{2,3},{3,4},{4,5},{5,6},{6,7},{7,8},{8,9},{9,10},{10,1... | collective-permute-start | bytes 786440 | tf_op jit(solution)/shard_map/ppermute | solution.py:324
  5.1 10.6 %collective-permute-start.1 = (bf16[128,1024]{1,0:T(8,128)(2,1)S(1)}, bf16[128,1024]{1,0:T(8,128)(2,1)S(1)}, u32[]{:S(2)}, u32[]{:S(2)}) collective-permute-start(bf16[128,1024]{1,0:T(8,128)(2,1)S(1)} %get-tuple-element.34), channel_id=1, source_target_pairs={{1,0},{2,1},{3,2},{4,3},{5,4},{6,5},{7,6},{8,7},{9,8},{10,9},{11,1... | collective-permute-start | bytes 786440 | tf_op jit(solution)/shard_map/ppermute | solution.py:325
  15.7 13.6 %copy-start = (f32[128,1024]{1,0:T(8,128)S(1)}, f32[128,1024]{1,0:T(8,128)}, u32[]{:S(2)}) copy-start(f32[128,1024]{1,0:T(8,128)} %truth_ref.1) | copy-start | bytes 1572868
  15.7 13.6 %copy-start.1 = (s32[1024]{0:T(1024)S(1)}, s32[1024]{0:T(1024)}, u32[]{:S(2)}) copy-start(s32[1024]{0:T(1024)} %param.16) | copy-start | bytes 12292
  19.1 11.2 %collective-permute-start.4 = (bf16[128,256]{1,0:T(8,128)(2,1)S(1)}, bf16[128,256]{1,0:T(8,128)(2,1)S(1)}, u32[]{:S(2)}, u32[]{:S(2)}) collective-permute-start(bf16[128,256]{1,0:T(8,128)(2,1)S(1)} %get-tuple-element.52), channel_id=1, source_target_pairs={{0,192},{64,0},{128,64},{192,128},{1,193},{65,1},{129,65},{193,129... | collective-permute-start | bytes 196616 | tf_op jit(solution)/shard_map/ppermute | solution.py:306
  25.5 7.5 %collective-permute-start.3 = (bf16[128,256]{1,0:T(8,128)(2,1)S(1)}, bf16[128,256]{1,0:T(8,128)(2,1)S(1)}, u32[]{:S(2)}, u32[]{:S(2)}) collective-permute-start(bf16[128,256]{1,0:T(8,128)(2,1)S(1)} %get-tuple-element.52), channel_id=1, source_target_pairs={{0,64},{64,128},{128,192},{192,0},{1,65},{65,129},{129,193},{193,1... | collective-permute-start | bytes 196616 | tf_op jit(solution)/shard_map/ppermute | solution.py:306
  25.5 8.2 %collective-permute-start.2 = (bf16[128,256]{1,0:T(8,128)(2,1)S(1)}, bf16[128,256]{1,0:T(8,128)(2,1)S(1)}, u32[]{:S(2)}, u32[]{:S(2)}) collective-permute-start(bf16[128,256]{1,0:T(8,128)(2,1)S(1)} %get-tuple-element.52), channel_id=1, source_target_pairs={{0,128},{64,192},{128,0},{192,64},{1,129},{65,193},{129,1},{193,65... | collective-permute-start | bytes 196616 | tf_op jit(solution)/shard_map/ppermute | solution.py:306
  33.7 1.6 %collective-permute-start.5 = (bf16[4,128,256]{2,1,0:T(8,128)(2,1)S(1)}, bf16[4,128,256]{2,1,0:T(8,128)(2,1)S(1)}, u32[]{:S(2)}, u32[]{:S(2)}) collective-permute-start(bf16[4,128,256]{2,1,0:T(8,128)(2,1)S(1)} %shard_map.108.oz_ref), channel_id=1, source_target_pairs={{0,32},{32,0},{1,33},{33,1},{2,34},{34,2},{3,35},{35,3},{4,36},{36... | collective-permute-start | bytes 786440 | tf_op jit(solution)/shard_map/ppermute | solution.py:364
  33.8 6.7 %collective-permute-start.6 = (bf16[1024,512]{1,0:T(8,128)(2,1)S(1)}, bf16[1024,512]{1,0:T(8,128)(2,1)S(1)}, u32[]{:S(2)}, u32[]{:S(2)}) collective-permute-start(bf16[1024,512]{1,0:T(8,128)(2,1)S(1)} %get-tuple-element.57.t_ref), channel_id=1, source_target_pairs={{0,32},{32,0},{1,33},{33,1},{2,34},{34,2},{3,35},{35,3},{4,36},{36... | collective-permute-start | bytes 3145736 | tf_op jit(solution)/shard_map/ppermute | solution.py:365
  38.6 2.0 %collective-permute-start.7 = (bf16[512,512]{1,0:T(8,128)(2,1)S(1)}, bf16[512,512]{1,0:T(8,128)(2,1)S(1)}, u32[]{:S(2)}, u32[]{:S(2)}) collective-permute-start(bf16[512,512]{1,0:T(8,128)(2,1)S(1)} %get-tuple-element.59), channel_id=1, source_target_pairs={{0,32},{32,0},{1,33},{33,1},{2,34},{34,2},{3,35},{35,3},{4,36},{36... | collective-permute-start | bytes 1572872 | tf_op jit(solution)/shard_map/ppermute | solution.py:370
  68.4 9.6 %collective-permute-start.8 = (bf16[32,128]{1,0:T(8,128)(2,1)S(1)}, bf16[32,128]{1,0:T(8,128)(2,1)S(1)}, u32[]{:S(2)}, u32[]{:S(2)}) collective-permute-start(bf16[32,128]{1,0:T(8,128)(2,1)S(1)} %get-tuple-element.61), channel_id=1, source_target_pairs={{0,128},{64,192},{128,0},{192,64},{1,129},{65,193},{129,1},{193,65... | collective-permute-start | bytes 24584 | tf_op jit(solution)/shard_map/ppermute | solution.py:306
  72.7 5.8 %collective-permute-start.9 = (bf16[32,128]{1,0:T(8,128)(2,1)S(1)}, bf16[32,128]{1,0:T(8,128)(2,1)S(1)}, u32[]{:S(2)}, u32[]{:S(2)}) collective-permute-start(bf16[32,128]{1,0:T(8,128)(2,1)S(1)} %get-tuple-element.62), channel_id=1, source_target_pairs={{0,64},{64,128},{128,192},{192,0},{1,65},{65,129},{129,193},{193,1... | collective-permute-start | bytes 24584 | tf_op jit(solution)/shard_map/ppermute | solution.py:306
  75.1 4.5 %collective-permute-start.10 = (bf16[32,128]{1,0:T(8,128)(2,1)S(1)}, bf16[32,128]{1,0:T(8,128)(2,1)S(1)}, u32[]{:S(2)}, u32[]{:S(2)}) collective-permute-start(bf16[32,128]{1,0:T(8,128)(2,1)S(1)} %get-tuple-element.63), channel_id=1, source_target_pairs={{0,192},{64,0},{128,64},{192,128},{1,193},{65,1},{129,65},{193,129... | collective-permute-start | bytes 24584 | tf_op jit(solution)/shard_map/ppermute | solution.py:306

commit v4 on v3

v4 whole, which is shorter than its diff:
```python
import jax
import jax.numpy as jnp
import numpy as np
from jax import lax
from jax.experimental import pallas as pl
from jax.experimental.pallas import tpu as pltpu
from jax.sharding import Mesh, PartitionSpec as P

F32 = jnp.float32
BF16 = jnp.bfloat16
ROWS = 256
REACH = 128
D = 1024
PAIRS = 8
PTS = 1024
CH = 128
MEMBERS = 8
BANDS = 32
OWN_GAP = 4
HALO_GAP = 4
BACK_GAP = 2
MASKED = -1e30
GRID = ("y", "zl", "x")

NT = (((1,), (1,)), ((), ()))


def mm(a, b):
    return jnp.dot(a, b, preferred_element_type=F32)


def mm_nt(a, b):
    return lax.dot_general(a, b, NT, preferred_element_type=F32)


def rms(states, gain):
    floats = states.astype(F32)
    meansq = jnp.mean(floats * floats, axis=-1, keepdims=True) + 1e-05
    return (floats * lax.rsqrt(meansq) * gain).astype(BF16)


def thirds(values):
    first = values.astype(BF16)
    rest = values - first.astype(F32)
    second = rest.astype(BF16)
    third = (rest - second.astype(F32)).astype(BF16)
    return first, second, third


def call(kernel, outs, cost, scratch=(), hbm=0, limit=16, keep=False):
    def run(*args):
        args = [
            pltpu.with_memory_space_constraint(arg, pltpu.HBM) if i < hbm else arg
            for i, arg in enumerate(args)
        ]
        in_specs = [pl.BlockSpec(memory_space=pltpu.HBM)] * hbm
        in_specs += [pl.BlockSpec(memory_space=pltpu.VMEM)] * (len(args) - hbm)
        other = pltpu.VMEM if keep else jax.ShapeDtypeStruct
        return pl.pallas_call(
            kernel,
            out_shape=[other(s, d) for s, d in outs],
            in_specs=in_specs,
            out_specs=[pl.BlockSpec(memory_space=pltpu.VMEM)] * len(outs),
            scratch_shapes=list(scratch),
            compiler_params=pltpu.CompilerParams(vmem_limit_bytes=limit * 2**20),
            cost_estimate=pl.CostEstimate(
                flops=int(cost * 1e9), bytes_accessed=int(cost * 3e6), transcendentals=0
            ),
        )(*args)

    return run


def split_kernel(x_hbm, first_ref, second_ref, sems):
    core = lax.axis_index("core")
    copies = [
        pltpu.make_async_copy(
            x_hbm.at[pl.ds(pl.multiple_of(start * REACH, REACH), REACH)], ref, sems.at[i]
        )
        for i, (start, ref) in enumerate(((1 - core, first_ref), (core, second_ref)))
    ]
    for copy in copies:
        copy.start()
    for copy in copies:
        copy.wait()


def staged(items, stages, gap):
    kept = [(item,) for item in items]
    for step in range(len(items) + gap * (len(stages) - 1)):
        for s, stage in enumerate(stages):
            i = step - gap * s
            if 0 <= i < len(items):
                kept[i] = (items[i], *stage(*kept[i]))


BLOCKS = [(pair, block) for block in range(2) for pair in range(PAIRS)]


def head_parts():
    lane = lax.broadcasted_iota(jnp.int32, (REACH, 128), 1)
    low = (lane < 64).astype(F32).astype(BF16)
    high = (lane >= 64).astype(F32).astype(BF16)
    row_low = lax.broadcasted_iota(jnp.int32, (128, REACH), 0) < 64
    key = lax.broadcasted_iota(jnp.int32, (REACH, 2 * REACH), 0)
    query = lax.broadcasted_iota(jnp.int32, (REACH, 2 * REACH), 1) % REACH
    return low, high, row_low, key, query


def project_kernel(
    wq_hbm, wk_hbm, wv_hbm, wo_hbm, wd_hbm, gain_hbm, x_hbm,
    q_ref, n_ref, x_ref, wk_ref, wv_ref, wo_ref, wd_ref, gain_ref, e_ref, out_ref, top_ref, sum_ref,
    wq, k, vt, sems,
):
    half = D // 2
    copies = [pltpu.make_async_copy(x_hbm, x_ref, sems.at[0])]
    copies.append(pltpu.make_async_copy(gain_hbm, gain_ref, sems.at[1]))
    for hbm, vmem in ((wq_hbm, wq), (wk_hbm, wk_ref), (wv_hbm, wv_ref), (wo_hbm, wo_ref)):
        for j in range(2):
            rows = slice(j * half, (j + 1) * half)
            copies.append(
                pltpu.make_async_copy(hbm.at[rows], vmem.at[rows], sems.at[len(copies)])
            )
    copies.append(pltpu.make_async_copy(wd_hbm, wd_ref, sems.at[len(copies)]))
    for copy in copies:
        copy.start()
    copies[0].wait()
    copies[1].wait()
    normed = rms(x_ref[...], gain_ref[...])
    n_ref[...] = normed
    copies[2].wait()
    copies[3].wait()
    q_ref[...] = mm(normed, wq[...]).astype(BF16) * jnp.asarray(0.125, BF16)
    copies[4].wait()
    copies[5].wait()
    k[...] = mm(normed, wk_ref[...]).astype(BF16)
    copies[6].wait()
    copies[7].wait()
    vt[...] = mm(normed, wv_ref[...]).T.astype(BF16)
    low, high, row_low, key, query = head_parts()
    before = jnp.where(key <= query, 0.0, MASKED)
    after = jnp.where(key >= query, 0.0, MASKED)

    def scores(item):
        pair, block = item
        cols = slice(pair * 128, (pair + 1) * 128)
        both = q_ref[block * REACH : (block + 1) * REACH, cols]
        stacked = jnp.concatenate([both * low, both * high], axis=0)
        s0 = mm_nt(k[:REACH, cols], stacked)
        s1 = mm_nt(k[REACH:, cols], stacked)
        return (s0, s1 + before) if block == 0 else (s0 + after, s1)

    def softmax(item, s0, s1):
        pair, block = item
        n = pair * 2 + block
        top = jnp.max(jnp.maximum(s0, s1), axis=0, keepdims=True)
        e0 = jnp.exp(s0 - top)
        e1 = jnp.exp(s1 - top)
        top_ref[n : n + 1] = top
        sum_ref[n : n + 1] = jnp.sum(e0 + e1, axis=0, keepdims=True)
        e = jnp.concatenate([e0.astype(BF16), e1.astype(BF16)], axis=0)
        e_ref[pair, block] = e
        return (mm(vt[pair * 128 : (pair + 1) * 128, :], e),)

    def store(item, out):
        out_ref[item] = jnp.where(row_low, out[:, :REACH], out[:, REACH:])
        return ()

    staged(BLOCKS, (scores, softmax, store), OWN_GAP)
    for copy in copies[8:]:
        copy.wait()


def attend_kernel(
    first_ref, second_ref, gain_ref, wk_ref, wv_ref, q_ref, out_ref, top_ref, sum_ref, x_ref, wo_ref, wd_ref,
    e_ref, factor_ref, dec_ref, dech_ref, nh_ref, kh, vht, mixed,
):
    band = band_index()
    gain = gain_ref[...]
    core = lax.axis_index("core")
    for start, ref in ((core, first_ref), (1 - core, second_ref)):
        nh_ref[pl.ds(pl.multiple_of(start * REACH, REACH), REACH)] = rms(ref[...], gain)
    halo = nh_ref[...]
    kh[...] = mm(halo, wk_ref[...]).astype(BF16)
    vht[...] = mm(halo, wv_ref[...]).T.astype(BF16)
    low, high, row_low, key, query = head_parts()
    first = jnp.where((key >= query) & (band > 0), 0.0, MASKED)
    last = jnp.where((key <= query) & (band < BANDS - 1), 0.0, MASKED)

    def scores(item):
        pair, block = item
        rows = slice(block * REACH, (block + 1) * REACH)
        cols = slice(pair * 128, (pair + 1) * 128)
        both = q_ref[rows, cols]
        stacked = jnp.concatenate([both * low, both * high], axis=0)
        return (mm_nt(kh[rows, cols], stacked) + (last if block else first),)

    def softmax(item, scores):
        pair, block = item
        n = pair * 2 + block
        top_own = top_ref[n : n + 1]
        top_halo = jnp.max(scores, axis=0, keepdims=True)
        e = jnp.exp(scores - top_halo)
        e_half = e.astype(BF16)
        e_ref[pair, block] = e_half
        top = jnp.maximum(top_own, top_halo)
        scale_own = jnp.exp(top_own - top)
        scale_halo = jnp.exp(top_halo - top)
        inv = 1.0 / (
            sum_ref[n : n + 1] * scale_own + jnp.sum(e, axis=0, keepdims=True) * scale_halo
        )
        scale_own *= inv
        scale_halo *= inv
        factor_ref[pair, 2 * block : 2 * block + 1] = scale_own
        factor_ref[pair, 2 * block + 1 : 2 * block + 2] = scale_halo
        cols = slice(pair * 128, (pair + 1) * 128)
        out = mm(vht[cols, block * REACH : (block + 1) * REACH], e_half)
        return out, scale_own, scale_halo

    def join(item, out, scale_own, scale_halo):
        pair, block = item
        out *= scale_halo
        out = jnp.where(row_low, out[:, :REACH], out[:, REACH:])
        own = jnp.where(row_low, scale_own[:, :REACH], scale_own[:, REACH:])
        out += out_ref[pair, block] * own
        cols = slice(pair * 128, (pair + 1) * 128)
        mixed[block * REACH : (block + 1) * REACH, cols] = out.T.astype(BF16)
        return ()

    staged(BLOCKS, (scores, softmax, join), HALO_GAP)
    projected = mm(mixed[...], wo_ref[...])
    hidden = (x_ref[...].astype(F32) + projected).astype(BF16)
    decoded = mm(hidden, wd_ref[...]).T
    dec_ref[...] = decoded
    dech_ref[...] = decoded.astype(BF16)


def band_index():
    return (lax.axis_index("y") * 2 + lax.axis_index("zl")) * 4 + lax.axis_index("x")


def selector(node_ref):
    node = lax.broadcasted_iota(jnp.int32, (ROWS, PTS), 0) + band_index() * ROWS
    return (node == node_ref[...]).astype(F32).astype(BF16)


def truth_kernel(
    dec_ref, node_ref, truth_ref, n_ref, nh_ref, eo_ref, eh_ref, factor_ref,
    abs_ref, slope_ref, count_ref, keep_ref, send_ref, own_ref, po_ref, ph_ref,
):
    own_ref[...] = dec_ref[...].astype(BF16)
    select = selector(node_ref)
    parts = thirds(dec_ref[...])
    pred = mm(parts[2], select) + mm(parts[1], select) + mm(parts[0], select)
    error = pred - truth_ref[...]
    square = error * error + 0.25
    inverse = lax.rsqrt(square)
    abs_ref[...] = square * inverse
    slope = error * inverse
    high = slope.astype(BF16)
    rest = (slope - high.astype(F32)).astype(BF16)
    slope_ref[...] = mm_nt(high, select) + mm_nt(rest, select)
    count_ref[...] = mm_nt(jnp.ones((16, PTS), BF16), select)[:8]
    core = lax.axis_index("core")
    for columns, ref in ((slice(0, ROWS), n_ref), (slice(ROWS, 2 * ROWS), nh_ref)):
        for g in range(BANDS):
            rows = ref[:, g * 32 : (g + 1) * 32].astype(F32).T.astype(BF16)
            by_x = g % 4 * 8 + g // 4
            for which, out_ref in ((core, keep_ref), (1 - core, send_ref)):
                start = pl.multiple_of(jnp.where(which == 0, by_x, g) * 32, 32)
                out_ref[pl.ds(start, 32), columns] = rows
    for pair in range(PAIRS):
        for block in range(2):
            factors = factor_ref[pair]
            own = eo_ref[pair, block].astype(F32) * factors[2 * block : 2 * block + 1]
            po_ref[pair, block] = own.astype(BF16)
            halo = eh_ref[pair, block].astype(F32) * factors[2 * block + 1 : 2 * block + 2]
            ph_ref[pair, block] = halo.astype(BF16)


def value_terms(which, hidden_grad, wo_ref, po_ref, ph_ref, out_ref):
    core = lax.axis_index("core")
    pairs = [2 * z + (core + which) % 2 for z in range(4)]
    rows = [wo_ref[pl.ds(pl.multiple_of(pair * 128, 128), 128), :] for pair in pairs]
    mixed_grad = mm(jnp.concatenate(rows, axis=0), hidden_grad).astype(BF16)
    feature = lax.broadcasted_iota(jnp.int32, (128, 2 * REACH), 0)
    lane = lax.broadcasted_iota(jnp.int32, (128, 2 * REACH), 1)
    heads = ((feature < 64) == (lane < REACH)).astype(F32).astype(BF16)

    def products(z):
        grads = mixed_grad[z * 128 : (z + 1) * 128]
        both = [grads[:, i * REACH : (i + 1) * REACH] for i in range(2)]
        both = [jnp.concatenate([part, part], axis=1) * heads for part in both]
        own = mm_nt(both[0], po_ref[pairs[z], 0]) + mm_nt(both[1], po_ref[pairs[z], 1])
        return own, mm_nt(both[0], ph_ref[pairs[z], 0]), mm_nt(both[1], ph_ref[pairs[z], 1])

    def store(z, own, halo0, halo1):
        terms = jnp.concatenate([own, halo0, halo1], axis=1)
        out_ref[z * 128 : (z + 1) * 128] = terms.astype(BF16)
        return ()

    staged(list(range(4)), (products, store), BACK_GAP)


def backward_kernel(
    po_ref, ph_ref, wd, wo_ref, dec_ref, oz_ref, oc_ref, slope_ref, count_ref,
    send_ref, spread_ref, hidden_ref,
):
    own = dec_ref[...]
    spread = jnp.full((CH, ROWS), 0.5, F32)
    total = jnp.zeros((CH, ROWS), F32)
    for other in [oz_ref[i] for i in range(3)] + [oc_ref[i] for i in range(4)]:
        differ = own - other.astype(F32)
        square = differ * differ + 0.25
        inverse = lax.rsqrt(square)
        spread += square * inverse
        total += differ * inverse
    spread_ref[...] = spread
    node_grad = (slope_ref[...] - count_ref[:1] * total * (1.0 / (MEMBERS - 1))) * (1.0 / MEMBERS)
    high = node_grad.astype(BF16)
    rest = (node_grad - high.astype(F32)).astype(BF16)
    hidden_grad = (mm(wd[...], high) + mm(wd[...], rest)).astype(BF16)
    hidden_ref[...] = hidden_grad
    value_terms(1, hidden_grad, wo_ref, po_ref, ph_ref, send_ref)


def own_product_kernel(po_ref, ph_ref, wo_ref, hidden_ref, t_ref, out_ref, terms):
    value_terms(0, hidden_ref[...], wo_ref, po_ref, ph_ref, terms)
    out_ref[...] = mm_nt(t_ref[...], terms[...])


def product_kernel(own_ref, u_ref, recv_ref, out_ref):
    out_ref[...] = (own_ref[...] + mm_nt(u_ref[...], recv_ref[...])).astype(BF16)


def band_kernel(pieces_ref, out_ref):
    for i in range(8):
        rows = slice(i * 32, (i + 1) * 32)
        both = (pieces_ref[0, rows].astype(F32) + pieces_ref[1, rows].astype(F32)) + (
            pieces_ref[2, rows].astype(F32) + pieces_ref[3, rows].astype(F32)
        )
        for zh in range(4):
            out_ref[zh * 8 + i] = both[:, zh * 128 : (zh + 1) * 128].astype(BF16)


def stack_kernel(a_ref, b_ref, c_ref, d_ref, out_ref):
    for i, ref in enumerate((a_ref, b_ref, c_ref, d_ref)):
        out_ref[i] = ref[...]


def last_kernel(pieces_ref, out_ref):
    total = pieces_ref[0].astype(F32)
    for i in range(1, 32):
        total += pieces_ref[i].astype(F32)
    out_ref[...] = total


def crps_kernel(abs_ref, spread_ref, node_ref, out_ref):
    select = selector(node_ref)
    parts = thirds(spread_ref[...])
    spread = mm(parts[2], select) + mm(parts[1], select) + mm(parts[0], select)
    out_ref[...] = abs_ref[...] - spread * (1.0 / (2.0 * (MEMBERS - 1)))


AXES = ("zh", "core", "y", "zl", "x")
SIZES = (4, 2, 4, 2, 4)


def moved(value, move):
    pairs = []
    for i, (zh, core, y, zl, x) in enumerate(np.ndindex(*SIZES)):
        zh, band = move(core, zh, y * 8 + zl * 4 + x)
        if 0 <= band < BANDS:
            to = (zh % 4, core, band // 8, band // 4 % 2, band % 4)
            pairs.append((i, int(np.ravel_multi_index(to, SIZES))))
    return lax.ppermute(value, AXES, pairs)


def grouped(label):
    groups = {}
    for i, place in enumerate(np.ndindex(*SIZES)):
        groups.setdefault(label(*place), []).append(i)
    return list(groups.values())


FIRST = grouped(lambda zh, core, y, zl, x: (zh, core, zl, x if core else y))
SECOND = grouped(lambda zh, core, y, zl, x: (core, y if core else x))


def ring(chunks):
    return [chunks[0]] + [
        moved(chunks[k], lambda core, zh, band: (zh + (4 - k if core else k), band))
        for k in (2, 1, 3)
    ]


def body(inputs, norm_gain, w_query, w_key, w_value, w_out, w_decode, point_node, truth):
    states = inputs[0]
    gain = norm_gain[None]
    node = point_node[None]
    swap = [(0, 1), (1, 0)]
    half = ((REACH, D), BF16)
    wide = ((ROWS, D), BF16)
    matrix = ((D, D), BF16)
    row = ((2 * PAIRS, 2 * REACH), F32)
    first, second = call(
        split_kernel, [half, half], 0.2, [pltpu.SemaphoreType.DMA((2,))], hbm=1, keep=True
    )(states)
    first = moved(first, lambda core, zh, band: (zh, band - 1 if core else band + 1))
    second = moved(second, lambda core, zh, band: (zh, band + 1 if core else band - 1))
    (
        queries, normed, here, w_key, w_value, w_out, w_decode, gain, exp_own, mixed_own, top_own,
        sum_own,
    ) = call(
        project_kernel,
        [wide, wide, wide, matrix, matrix, matrix, ((D, CH), BF16), ((1, D), F32)]
        + [((PAIRS, 2, ROWS, 2 * REACH), BF16), ((PAIRS, 2, 128, REACH), F32), row, row],
        3.0,
        [
            pltpu.VMEM((D, D), BF16),
            pltpu.VMEM((ROWS, D), BF16),
            pltpu.VMEM((D, ROWS), BF16),
            pltpu.SemaphoreType.DMA((11,)),
        ],
        hbm=7,
        limit=20,
        keep=True,
    )(w_query, w_key, w_value, w_out, w_decode, gain, states)
    exp_halo, factors, decoded, decoded_half, normed_halo = call(
        attend_kernel,
        [((PAIRS, 2, REACH, 2 * REACH), BF16), ((PAIRS, 4, 2 * REACH), F32)]
        + [((CH, ROWS), F32), ((CH, ROWS), BF16), wide],
        3.0,
        [pltpu.VMEM((ROWS, D), BF16), pltpu.VMEM((D, ROWS), BF16), pltpu.VMEM((ROWS, D), BF16)],
        limit=20,
        keep=True,
    )(
        first, second, gain, w_key, w_value, queries, mixed_own, top_own, sum_own, here, w_out,
        w_decode,
    )
    along = ring([None, decoded_half, decoded_half, decoded_half])[1:]
    probs = [((PAIRS, 2, ROWS, 2 * REACH), BF16), ((PAIRS, 2, REACH, 2 * REACH), BF16)]
    turned = ((D, 2 * ROWS), BF16)
    abs_error, slope, count, turned, turned_send, own, probs_own, probs_halo = call(
        truth_kernel,
        [((CH, PTS), F32), ((CH, ROWS), F32), ((8, ROWS), F32), turned, turned]
        + [((CH, ROWS), BF16), *probs],
        2.0,
        keep=True,
    )(decoded, node, truth, normed, normed_halo, exp_own, exp_halo, factors)
    (along,) = call(stack_kernel, [((4, CH, ROWS), BF16)], 0.1)(*along, own)
    across = lax.ppermute(along, "core", swap)
    turned_other = lax.ppermute(turned_send, "core", swap)
    send, spread, hidden_grad = call(
        backward_kernel,
        [((512, 512), BF16), ((CH, ROWS), F32), ((D, ROWS), BF16)],
        2.0,
        keep=True,
    )(probs_own, probs_halo, w_decode, w_out, decoded, along, across, slope, count)
    received = lax.ppermute(send, "core", swap)
    (own_product,) = call(
        own_product_kernel, [((D, 512), F32)], 2.0, [pltpu.VMEM((512, 512), BF16)], keep=True
    )(probs_own, probs_halo, w_out, hidden_grad, turned)
    (product,) = call(product_kernel, [((D, 512), BF16)], 1.0)(own_product, turned_other, received)
    product = product.reshape(4, 256, 512)
    pieces = lax.all_to_all(product, AXES, 0, 0, axis_index_groups=FIRST)
    (blocks,) = call(band_kernel, [((32, 32, 128), BF16)], 0.1)(pieces)
    blocks = lax.all_to_all(blocks, AXES, 0, 0, axis_index_groups=SECOND)
    (crps_terms,) = call(crps_kernel, [((CH, PTS), F32)], 1.0)(abs_error, spread, node)
    (grad_value,) = call(last_kernel, [((32, 128), F32)], 0.1)(blocks)
    return crps_terms[None], grad_value


def solution(mesh):
    parts = Mesh(mesh.devices.reshape(4, 2, 4, 2, 4), ("zh", "core", "y", "zl", "x"))
    member = ("zh", "core")
    return jax.shard_map(
        body,
        mesh=parts,
        in_specs=(
            P(member, GRID, None), P(), P(), P(), P(), P(), P(), P(GRID), P(None, GRID),
        ),
        out_specs=(P(member, None, GRID), P(GRID, member)),
        check_vma=False,
    )
```

time: 80.5 us -> 77.7 us (0.965)
  the two profiles are of different devices: /device:TPU:2 before, /device:TPU:1 now
where the time goes in v4:
time: 77.7 us; the launch traced here: 77.4 us
  starting transfers between devices  29.2 us (38%)
  Pallas kernels  19.9 us (26%)
  blocking collectives  15.3 us (20%)
  waiting for transfers between devices  12.3 us (16%)
    pallas_call x11, Pallas kernels, run(): pl.pallas_call(kernel, out_shape=[other(s, d) for s, d in outs], in_specs...  19.9 us
    ppermute x5, starting transfers between devices, moved(): return lax.ppermute(value, AXES, pairs)  16.7 us
    all_to_all x1, blocking collectives, body(): pieces = lax.all_to_all(product, AXES, 0, 0, axis_index_groups=FIRST)  15.3 us
    all_to_all x1, waiting for transfers between devices, body(): blocks = lax.all_to_all(blocks, AXES, 0, 0, axis_index_groups=SECOND)  11.1 us
    all_to_all x1, starting transfers between devices, body(): blocks = lax.all_to_all(blocks, AXES, 0, 0, axis_index_groups=SECOND)  7.58 us
    ppermute x1, starting transfers between devices, body(): across = lax.ppermute(along, 'core', swap)  3.32 us
  transfers between devices with their start and end apart: 9, of which 2 were waited for; matrix products, arithmetic and copies ran while one was open for 0% of the time, Pallas kernels for 17%

profile of v4, /device:TPU:1, one launch (start us, length us, event | category | flops | bytes accessed | tf_op | source)
XLA Modules:
  0.0 77.4 jit_solution(9526825881585277838)
XLA Ops:
  0.6 1.1 %shard_map.104 = (bf16[128,1024]{1,0:T(8,128)(2,1)S(1)}, bf16[128,1024]{1,0:T(8,128)(2,1)S(1)}) custom-call(bf16[256,1024]{1,0:T(8,128)(2,1)} %bitcast.8), custom_call_target="tpu_custom_call" | custom-call | flops 200000000 | bytes 600000 | tf_op jit(solution)/shard_map/pallas_call | solution.py:59
  1.7 1.3 %collective-permute-start = (bf16[128,1024]{1,0:T(8,128)(2,1)S(1)}, bf16[128,1024]{1,0:T(8,128)(2,1)S(1)}, u32[]{:S(2)}, u32[]{:S(2)}) collective-permute-start(bf16[128,1024]{1,0:T(8,128)(2,1)S(1)} %get-tuple-element.32), channel_id=1, source_target_pairs={{0,1},{1,2},{2,3},{3,4},{4,5},{5,6},{6,7},{7,8},{8,9},{9,10},{10,1... | collective-permute-start | bytes 786440 | tf_op jit(solution)/shard_map/ppermute | solution.py:376
  3.0 4.6 %collective-permute-start.1 = (bf16[128,1024]{1,0:T(8,128)(2,1)S(1)}, bf16[128,1024]{1,0:T(8,128)(2,1)S(1)}, u32[]{:S(2)}, u32[]{:S(2)}) collective-permute-start(bf16[128,1024]{1,0:T(8,128)(2,1)S(1)} %get-tuple-element.33), channel_id=1, source_target_pairs={{1,0},{2,1},{3,2},{4,3},{5,4},{6,5},{7,6},{8,7},{9,8},{10,9},{11,1... | collective-permute-start | bytes 786440 | tf_op jit(solution)/shard_map/ppermute | solution.py:376
  7.6 5.6 %shard_map.105 = (bf16[256,1024]{1,0:T(8,128)(2,1)S(1)}, bf16[256,1024]{1,0:T(8,128)(2,1)S(1)}, bf16[256,1024]{1,0:T(8,128)(2,1)S(1)}, bf16[1024,1024]{1,0:T(8,1...) custom-call(bf16[1024,1024]{1,0:T(8,128)(2,1)} %wq_hbm.1, ...), custom_call_target="tpu_custom_call" | custom-call | flops 3000000000 | bytes 9000000 | tf_op jit(solution)/shard_map/pallas_call | solution.py:59
  13.2 0.0 collective-permute-done.first_ref
  13.2 0.0 collective-permute-done.1.second_ref
  13.2 0.0 copy-start
  13.2 0.0 copy-start.1
  13.2 3.5 %shard_map.106 = (bf16[8,2,128,256]{3,2,1,0:T(8,128)(2,1)S(1)}, f32[8,4,256]{2,1,0:T(4,128)S(1)}, f32[128,256]{1,0:T(8,128)S(1)}, bf16[128,256]{1,0:T(8,128)(2,1)S(1)}, bf16[256,1024]{1,0:T(8,128)(2,1)S(1)}) custom-call(bf16[128,1024]{1,0:T(8,128)(2,1)S(1)} %collective-permute-done.first_ref, bf16[128,1024]{1,0:T(8,128)(2,1)S(1)} %collective-permute-done.1.second_ref, ...), custom_call_target="tpu_custom_call" | custom-call | flops 3000000000 | bytes 9000000 | tf_op jit(solution)/shard_map/pallas_call | solution.py:59
  16.7 3.3 %collective-permute-start.4 = (bf16[128,256]{1,0:T(8,128)(2,1)S(1)}, bf16[128,256]{1,0:T(8,128)(2,1)S(1)}, u32[]{:S(2)}, u32[]{:S(2)}) collective-permute-start(bf16[128,256]{1,0:T(8,128)(2,1)S(1)} %get-tuple-element.53), channel_id=1, source_target_pairs={{0,192},{1,193},{2,194},{3,195},{4,196},{5,197},{6,198},{7,199},{8... | collective-permute-start | bytes 196616 | tf_op jit(solution)/shard_map/ppermute | solution.py:376
  20.0 3.1 %collective-permute-start.3 = (bf16[128,256]{1,0:T(8,128)(2,1)S(1)}, bf16[128,256]{1,0:T(8,128)(2,1)S(1)}, u32[]{:S(2)}, u32[]{:S(2)}) collective-permute-start(bf16[128,256]{1,0:T(8,128)(2,1)S(1)} %get-tuple-element.53), channel_id=1, source_target_pairs={{0,64},{1,65},{2,66},{3,67},{4,68},{5,69},{6,70},{7,71},{8,72},{9,... | collective-permute-start | bytes 196616 | tf_op jit(solution)/shard_map/ppermute | solution.py:376
  23.1 4.4 %collective-permute-start.2 = (bf16[128,256]{1,0:T(8,128)(2,1)S(1)}, bf16[128,256]{1,0:T(8,128)(2,1)S(1)}, u32[]{:S(2)}, u32[]{:S(2)}) collective-permute-start(bf16[128,256]{1,0:T(8,128)(2,1)S(1)} %get-tuple-element.53), channel_id=1, source_target_pairs={{0,128},{1,129},{2,130},{3,131},{4,132},{5,133},{6,134},{7,135},{8... | collective-permute-start | bytes 196616 | tf_op jit(solution)/shard_map/ppermute | solution.py:376
  27.5 0.0 copy-done
  27.5 0.0 copy-done.1
  27.5 2.6 %shard_map.107 = (f32[128,1024]{1,0:T(8,128)S(1)}, f32[128,256]{1,0:T(8,128)S(1)}, f32[8,256]{1,0:T(8,128)S(1)}, bf16[1024,512]{1,0:T(8,128)(2,1)S(1)}, bf16[102...) custom-call(f32[128,256]{1,0:T(8,128)S(1)} %get-tuple-element.44.dec, ...), custom_call_target="tpu_custom_call" | custom-call | flops 2000000000 | bytes 6000000 | tf_op jit(solution)/shard_map/pallas_call | solution.py:59
  30.1 1.1 %collective-permute-start.6 = (bf16[1024,512]{1,0:T(8,128)(2,1)S(1)}, bf16[1024,512]{1,0:T(8,128)(2,1)S(1)}, u32[]{:S(2)}, u32[]{:S(2)}) collective-permute-start(bf16[1024,512]{1,0:T(8,128)(2,1)S(1)} %get-tuple-element.60), channel_id=1, source_target_pairs={{0,32},{32,0},{1,33},{33,1},{2,34},{34,2},{3,35},{35,3},{4,36},{36... | collective-permute-start | bytes 3145736 | tf_op jit(solution)/shard_map/ppermute | solution.py:453
  31.3 0.0 collective-permute-done.4.c_ref
  31.3 0.0 collective-permute-done.3.b_ref
  31.3 0.0 collective-permute-done.2.a_ref
  31.3 3.3 %collective-permute-start.5 = (bf16[4,128,256]{2,1,0:T(8,128)(2,1)S(1)}, bf16[4,128,256]{2,1,0:T(8,128)(2,1)S(1)}, u32[]{:S(2)}, u32[]{:S(2)}) collective-permute-start(bf16[4,128,256]{2,1,0:T(8,128)(2,1)S(1)} %shard_map.108.oz_ref), channel_id=1, source_target_pairs={{0,32},{32,0},{1,33},{33,1},{2,34},{34,2},{3,35},{35,3},{4,36},{36... | collective-permute-start | bytes 786440 | tf_op jit(solution)/shard_map/ppermute | solution.py:452
  34.6 1.2 %collective-permute-done.5.oc_ref = bf16[4,128,256]{2,1,0:T(8,128)(2,1)S(1)} collective-permute-done((bf16[4,128,256]{2,1,0:T(8,128)(2,1)S(1)}, bf16[4,128,256]{2,1,0:T(8,128)(2,1)S(1)}, u32[]{:S(2)}, u32[]{:S(2)}) %collective-permute-start.5) | collective-permute-done | bytes 262176 | tf_op jit(solution)/shard_map/ppermute | solution.py:452
  35.8 1.8 %shard_map.109 = (bf16[512,512]{1,0:T(8,128)(2,1)S(1)}, f32[128,256]{1,0:T(8,128)S(1)}, bf16[1024,256]{1,0:T(8,128)(2,1)S(1)}) custom-call(bf16[8,2,256,256]{3,2,1,0:T(8,128)(2,1)S(1)} %get-tuple-element.51.po_ref, bf16[8,2,128,256]{3,2,1,0:T(8,128)(2,1)S(1)} %get-tuple-element.52.ph_ref, bf16[1024,128]{1,0:T(8,128)(2,1)S(1)} %get-tuple-element.43.wd_ref.wd, ...), custom_call_target="tpu_custom_call" | custom-call | flops 2000000000 | bytes 6000000 | tf_op jit(solution)/shard_map/pallas_call | solution.py:59
  37.6 0.5 collective-permute-start.7
  38.1 1.9 %shard_map.111.own_ref = f32[1024,512]{1,0:T(8,128)S(1)} custom-call(bf16[8,2,256,256]{3,2,1,0:T(8,128)(2,1)S(1)} %get-tuple-element.51.po_ref, bf16[8,2,128,256]{3,2,1,0:T(8,128)(2,1)S(1)} %get-tuple-element.52.ph_ref, bf16[1024,1024]{1,0:T(8,128)(2,1)S(1)} %get-tuple-element.42.wo_ref, bf16[1024,256]{1,0:T(8,128)(2,1)S(1)} %get-tuple-element.58.hidden_ref, ...), custom_call_target="tpu_custom_call" | custom-call | flops 2000000000 | bytes 6000000 | tf_op jit(solution)/shard_map/pallas_call | solution.py:59
  40.0 0.0 collective-permute-done.7.recv_ref
  40.0 0.0 collective-permute-done.6.u_ref
  40.0 0.7 shard_map.112
  40.8 15.3 %all_to_all.10.pieces_ref = bf16[4,256,512]{2,1,0:T(8,128)(2,1)S(1)} all-to-all(bf16[4,256,512]{2,1,0:T(8,128)(2,1)S(1)} %bitcast.5), channel_id=1, replica_groups={{0,1,2,3},{4,5,6,7},{8,9,10,11},{12,13,14,15},{16,17,18,19},{20,21,22,2..., dimensions={0} | all-to-all | bytes 2097152 | tf_op jit(solution)/shard_map/all_to_all | solution.py:466
  56.0 0.8 %shard_map.113 = bf16[32,32,128]{2,1,0:T(8,128)(2,1)} custom-call(bf16[4,256,512]{2,1,0:T(8,128)(2,1)S(1)} %all_to_all.10.pieces_ref), custom_call_target="tpu_custom_call" | custom-call | flops 100000000 | bytes 300000 | tf_op jit(solution)/shard_map/pallas_call | solution.py:59
  56.9 7.6 %all-to-all-start.1 = ((bf16[32,32,128]{2,1,0:T(8,128)(2,1)}), bf16[32,32,128]{2,1,0:T(8,128)(2,1)S(1)}, u32[]{:S(2)}, u32[]{:S(2)}) async-start(bf16[32,32,128]{2,1,0:T(8,128)(2,1)} %shard_map.113), calls=%async_computation.1 | async-start | bytes 524288 | tf_op jit(solution)/shard_map/all_to_all | solution.py:468
  64.5 1.2 %shard_map.110 = f32[128,1024]{1,0:T(8,128)} custom-call(f32[128,1024]{1,0:T(8,128)S(1)} %get-tuple-element.50.abs_ref, f32[128,256]{1,0:T(8,128)S(1)} %get-tuple-element.57.spread_ref, s32[1,1024]{1,0:T(1,128)S(1)} %bitcast.7), custom_call_target="tpu_custom_call" | custom-call | flops 1000000000 | bytes 3000000 | tf_op jit(solution)/shard_map/pallas_call | solution.py:59
  65.7 11.1 %all-to-all-done.1.pieces_ref = bf16[32,32,128]{2,1,0:T(8,128)(2,1)S(1)} async-done(((bf16[32,32,128]{2,1,0:T(8,128)(2,1)}), bf16[32,32,128]{2,1,0:T(8,128)(2,1)S(1)}, u32[]{:S(2)}, u32[]{:S(2)}) %all-to-all-start.1) | async-done | bytes 262176 | tf_op jit(solution)/shard_map/all_to_all | solution.py:468
  76.8 0.7 shard_map.114
  (1 shorter events, 0.0 us)
Async XLA Ops:
  1.7 11.5 %collective-permute-start = (bf16[128,1024]{1,0:T(8,128)(2,1)S(1)}, bf16[128,1024]{1,0:T(8,128)(2,1)S(1)}, u32[]{:S(2)}, u32[]{:S(2)}) collective-permute-start(bf16[128,1024]{1,0:T(8,128)(2,1)S(1)} %get-tuple-element.32), channel_id=1, source_target_pairs={{0,1},{1,2},{2,3},{3,4},{4,5},{5,6},{6,7},{7,8},{8,9},{9,10},{10,1... | collective-permute-start | bytes 786440 | tf_op jit(solution)/shard_map/ppermute | solution.py:376
  3.0 10.2 %collective-permute-start.1 = (bf16[128,1024]{1,0:T(8,128)(2,1)S(1)}, bf16[128,1024]{1,0:T(8,128)(2,1)S(1)}, u32[]{:S(2)}, u32[]{:S(2)}) collective-permute-start(bf16[128,1024]{1,0:T(8,128)(2,1)S(1)} %get-tuple-element.33), channel_id=1, source_target_pairs={{1,0},{2,1},{3,2},{4,3},{5,4},{6,5},{7,6},{8,7},{9,8},{10,9},{11,1... | collective-permute-start | bytes 786440 | tf_op jit(solution)/shard_map/ppermute | solution.py:376
  13.2 14.3 %copy-start = (f32[128,1024]{1,0:T(8,128)S(1)}, f32[128,1024]{1,0:T(8,128)}, u32[]{:S(2)}) copy-start(f32[128,1024]{1,0:T(8,128)} %truth_ref.1) | copy-start | bytes 1572868
  13.2 14.3 %copy-start.1 = (s32[1024]{0:T(1024)S(1)}, s32[1024]{0:T(1024)}, u32[]{:S(2)}) copy-start(s32[1024]{0:T(1024)} %param.16) | copy-start | bytes 12292
  16.7 14.6 %collective-permute-start.4 = (bf16[128,256]{1,0:T(8,128)(2,1)S(1)}, bf16[128,256]{1,0:T(8,128)(2,1)S(1)}, u32[]{:S(2)}, u32[]{:S(2)}) collective-permute-start(bf16[128,256]{1,0:T(8,128)(2,1)S(1)} %get-tuple-element.53), channel_id=1, source_target_pairs={{0,192},{1,193},{2,194},{3,195},{4,196},{5,197},{6,198},{7,199},{8... | collective-permute-start | bytes 196616 | tf_op jit(solution)/shard_map/ppermute | solution.py:376
  20.0 11.3 %collective-permute-start.3 = (bf16[128,256]{1,0:T(8,128)(2,1)S(1)}, bf16[128,256]{1,0:T(8,128)(2,1)S(1)}, u32[]{:S(2)}, u32[]{:S(2)}) collective-permute-start(bf16[128,256]{1,0:T(8,128)(2,1)S(1)} %get-tuple-element.53), channel_id=1, source_target_pairs={{0,64},{1,65},{2,66},{3,67},{4,68},{5,69},{6,70},{7,71},{8,72},{9,... | collective-permute-start | bytes 196616 | tf_op jit(solution)/shard_map/ppermute | solution.py:376
  23.1 8.1 %collective-permute-start.2 = (bf16[128,256]{1,0:T(8,128)(2,1)S(1)}, bf16[128,256]{1,0:T(8,128)(2,1)S(1)}, u32[]{:S(2)}, u32[]{:S(2)}) collective-permute-start(bf16[128,256]{1,0:T(8,128)(2,1)S(1)} %get-tuple-element.53), channel_id=1, source_target_pairs={{0,128},{1,129},{2,130},{3,131},{4,132},{5,133},{6,134},{7,135},{8... | collective-permute-start | bytes 196616 | tf_op jit(solution)/shard_map/ppermute | solution.py:376
  30.1 9.9 %collective-permute-start.6 = (bf16[1024,512]{1,0:T(8,128)(2,1)S(1)}, bf16[1024,512]{1,0:T(8,128)(2,1)S(1)}, u32[]{:S(2)}, u32[]{:S(2)}) collective-permute-start(bf16[1024,512]{1,0:T(8,128)(2,1)S(1)} %get-tuple-element.60), channel_id=1, source_target_pairs={{0,32},{32,0},{1,33},{33,1},{2,34},{34,2},{3,35},{35,3},{4,36},{36... | collective-permute-start | bytes 3145736 | tf_op jit(solution)/shard_map/ppermute | solution.py:453
  31.3 4.5 %collective-permute-start.5 = (bf16[4,128,256]{2,1,0:T(8,128)(2,1)S(1)}, bf16[4,128,256]{2,1,0:T(8,128)(2,1)S(1)}, u32[]{:S(2)}, u32[]{:S(2)}) collective-permute-start(bf16[4,128,256]{2,1,0:T(8,128)(2,1)S(1)} %shard_map.108.oz_ref), channel_id=1, source_target_pairs={{0,32},{32,0},{1,33},{33,1},{2,34},{34,2},{3,35},{35,3},{4,36},{36... | collective-permute-start | bytes 786440 | tf_op jit(solution)/shard_map/ppermute | solution.py:452
  37.6 2.4 %collective-permute-start.7 = (bf16[512,512]{1,0:T(8,128)(2,1)S(1)}, bf16[512,512]{1,0:T(8,128)(2,1)S(1)}, u32[]{:S(2)}, u32[]{:S(2)}) collective-permute-start(bf16[512,512]{1,0:T(8,128)(2,1)S(1)} %get-tuple-element.61), channel_id=1, source_target_pairs={{0,32},{32,0},{1,33},{33,1},{2,34},{34,2},{3,35},{35,3},{4,36},{36... | collective-permute-start | bytes 1572872 | tf_op jit(solution)/shard_map/ppermute | solution.py:460
  56.9 19.9 %all-to-all-start.1 = ((bf16[32,32,128]{2,1,0:T(8,128)(2,1)}), bf16[32,32,128]{2,1,0:T(8,128)(2,1)S(1)}, u32[]{:S(2)}, u32[]{:S(2)}) async-start(bf16[32,32,128]{2,1,0:T(8,128)(2,1)} %shard_map.113), calls=%async_computation.1 | async-start | bytes 524288 | tf_op jit(solution)/shard_map/all_to_all | solution.py:468

commit v5 on v4

--- a/solution.py
+++ b/solution.py
@@ -16,6 +16,7 @@
 CH = 128
 MEMBERS = 8
 BANDS = 32
+SPLIT = 8.0
 OWN_GAP = 4
 HALO_GAP = 4
 BACK_GAP = 2
@@ -47,7 +48,7 @@
     return first, second, third
 
 
-def call(kernel, outs, cost, scratch=(), hbm=0, limit=16, keep=False):
+def call(kernel, outs, cost, scratch=(), hbm=0, limit=16, keep=False, out_hbm=0):
     def run(*args):
         args = [
             pltpu.with_memory_space_constraint(arg, pltpu.HBM) if i < hbm else arg
@@ -56,11 +57,15 @@
         in_specs = [pl.BlockSpec(memory_space=pltpu.HBM)] * hbm
         in_specs += [pl.BlockSpec(memory_space=pltpu.VMEM)] * (len(args) - hbm)
         other = pltpu.VMEM if keep else jax.ShapeDtypeStruct
+        near = len(outs) - out_hbm
+        shapes = [other(s, d) for s, d in outs[:near]] + [pltpu.HBM(s, d) for s, d in outs[near:]]
+        out_specs = [pl.BlockSpec(memory_space=pltpu.VMEM)] * near
+        out_specs += [pl.BlockSpec(memory_space=pltpu.HBM)] * out_hbm
         return pl.pallas_call(
             kernel,
-            out_shape=[other(s, d) for s, d in outs],
+            out_shape=shapes,
             in_specs=in_specs,
-            out_specs=[pl.BlockSpec(memory_space=pltpu.VMEM)] * len(outs),
+            out_specs=out_specs,
             scratch_shapes=list(scratch),
             compiler_params=pltpu.CompilerParams(vmem_limit_bytes=limit * 2**20),
             cost_estimate=pl.CostEstimate(
@@ -108,34 +113,12 @@
 
 
 def project_kernel(
-    wq_hbm, wk_hbm, wv_hbm, wo_hbm, wd_hbm, gain_hbm, x_hbm,
-    q_ref, n_ref, x_ref, wk_ref, wv_ref, wo_ref, wd_ref, gain_ref, e_ref, out_ref, top_ref, sum_ref,
-    wq, k, vt, sems,
+    wq_ref, wk_ref, wv_ref, gain_ref, x_ref, q_ref, n_ref, e_ref, out_ref, top_ref, sum_ref, k, vt
 ):
-    half = D // 2
-    copies = [pltpu.make_async_copy(x_hbm, x_ref, sems.at[0])]
-    copies.append(pltpu.make_async_copy(gain_hbm, gain_ref, sems.at[1]))
-    for hbm, vmem in ((wq_hbm, wq), (wk_hbm, wk_ref), (wv_hbm, wv_ref), (wo_hbm, wo_ref)):
-        for j in range(2):
-            rows = slice(j * half, (j + 1) * half)
-            copies.append(
-                pltpu.make_async_copy(hbm.at[rows], vmem.at[rows], sems.at[len(copies)])
-            )
-    copies.append(pltpu.make_async_copy(wd_hbm, wd_ref, sems.at[len(copies)]))
-    for copy in copies:
-        copy.start()
-    copies[0].wait()
-    copies[1].wait()
     normed = rms(x_ref[...], gain_ref[...])
     n_ref[...] = normed
-    copies[2].wait()
-    copies[3].wait()
-    q_ref[...] = mm(normed, wq[...]).astype(BF16) * jnp.asarray(0.125, BF16)
-    copies[4].wait()
-    copies[5].wait()
+    q_ref[...] = mm(normed, wq_ref[...]).astype(BF16) * jnp.asarray(0.125, BF16)
     k[...] = mm(normed, wk_ref[...]).astype(BF16)
-    copies[6].wait()
-    copies[7].wait()
     vt[...] = mm(normed, wv_ref[...]).T.astype(BF16)
     low, high, row_low, key, query = head_parts()
     before = jnp.where(key <= query, 0.0, MASKED)
@@ -167,8 +150,6 @@
         return ()
 
     staged(BLOCKS, (scores, softmax, store), OWN_GAP)
-    for copy in copies[8:]:
-        copy.wait()
 
 
 def attend_kernel(
@@ -324,9 +305,19 @@
     value_terms(1, hidden_grad, wo_ref, po_ref, ph_ref, send_ref)
 
 
-def own_product_kernel(po_ref, ph_ref, wo_ref, hidden_ref, t_ref, out_ref, terms):
+def own_product_kernel(
+    po_ref, ph_ref, wo_ref, hidden_ref, t_ref, abs_ref, spread_ref, node_ref,
+    out_ref, crps_hbm, terms, crps, sem,
+):
+    select = selector(node_ref)
+    parts = thirds(spread_ref[...])
+    spread = mm(parts[2], select) + mm(parts[1], select) + mm(parts[0], select)
+    crps[...] = abs_ref[...] - spread * (1.0 / (2.0 * (MEMBERS - 1)))
+    copy = pltpu.make_async_copy(crps, crps_hbm, sem)
+    copy.start()
     value_terms(0, hidden_ref[...], wo_ref, po_ref, ph_ref, terms)
     out_ref[...] = mm_nt(t_ref[...], terms[...])
+    copy.wait()
 
 
 def product_kernel(own_ref, u_ref, recv_ref, out_ref):
@@ -355,13 +346,6 @@
     out_ref[...] = total
 
 
-def crps_kernel(abs_ref, spread_ref, node_ref, out_ref):
-    select = selector(node_ref)
-    parts = thirds(spread_ref[...])
-    spread = mm(parts[2], select) + mm(parts[1], select) + mm(parts[0], select)
-    out_ref[...] = abs_ref[...] - spread * (1.0 / (2.0 * (MEMBERS - 1)))
-
-
 AXES = ("zh", "core", "y", "zl", "x")
 SIZES = (4, 2, 4, 2, 4)
 
@@ -401,31 +385,20 @@
     swap = [(0, 1), (1, 0)]
     half = ((REACH, D), BF16)
     wide = ((ROWS, D), BF16)
-    matrix = ((D, D), BF16)
     row = ((2 * PAIRS, 2 * REACH), F32)
     first, second = call(
-        split_kernel, [half, half], 0.2, [pltpu.SemaphoreType.DMA((2,))], hbm=1, keep=True
+        split_kernel, [half, half], SPLIT, [pltpu.SemaphoreType.DMA((2,))], hbm=1, keep=True
     )(states)
     first = moved(first, lambda core, zh, band: (zh, band - 1 if core else band + 1))
     second = moved(second, lambda core, zh, band: (zh, band + 1 if core else band - 1))
-    (
-        queries, normed, here, w_key, w_value, w_out, w_decode, gain, exp_own, mixed_own, top_own,
-        sum_own,
-    ) = call(
+    queries, normed, exp_own, mixed_own, top_own, sum_own = call(
         project_kernel,
-        [wide, wide, wide, matrix, matrix, matrix, ((D, CH), BF16), ((1, D), F32)]
-        + [((PAIRS, 2, ROWS, 2 * REACH), BF16), ((PAIRS, 2, 128, REACH), F32), row, row],
+        [wide, wide, ((PAIRS, 2, ROWS, 2 * REACH), BF16), ((PAIRS, 2, 128, REACH), F32), row, row],
         3.0,
-        [
-            pltpu.VMEM((D, D), BF16),
-            pltpu.VMEM((ROWS, D), BF16),
-            pltpu.VMEM((D, ROWS), BF16),
-            pltpu.SemaphoreType.DMA((11,)),
-        ],
-        hbm=7,
+        [pltpu.VMEM((ROWS, D), BF16), pltpu.VMEM((D, ROWS), BF16)],
         limit=20,
         keep=True,
-    )(w_query, w_key, w_value, w_out, w_decode, gain, states)
+    )(w_query, w_key, w_value, gain, states)
     exp_halo, factors, decoded, decoded_half, normed_halo = call(
         attend_kernel,
         [((PAIRS, 2, REACH, 2 * REACH), BF16), ((PAIRS, 4, 2 * REACH), F32)]
@@ -435,7 +408,7 @@
         limit=20,
         keep=True,
     )(
-        first, second, gain, w_key, w_value, queries, mixed_own, top_own, sum_own, here, w_out,
+        first, second, gain, w_key, w_value, queries, mixed_own, top_own, sum_own, states, w_out,
         w_decode,
     )
     along = ring([None, decoded_half, decoded_half, decoded_half])[1:]
@@ -458,15 +431,17 @@
         keep=True,
     )(probs_own, probs_halo, w_decode, w_out, decoded, along, across, slope, count)
     received = lax.ppermute(send, "core", swap)
-    (own_product,) = call(
-        own_product_kernel, [((D, 512), F32)], 2.0, [pltpu.VMEM((512, 512), BF16)], keep=True
-    )(probs_own, probs_halo, w_out, hidden_grad, turned)
+    own_product, crps_terms = call(
+        own_product_kernel, [((D, 512), F32), ((CH, PTS), F32)], 2.0,
+        [pltpu.VMEM((512, 512), BF16), pltpu.VMEM((CH, PTS), F32), pltpu.SemaphoreType.DMA],
+        keep=True,
+        out_hbm=1,
+    )(probs_own, probs_halo, w_out, hidden_grad, turned, abs_error, spread, node)
     (product,) = call(product_kernel, [((D, 512), BF16)], 1.0)(own_product, turned_other, received)
     product = product.reshape(4, 256, 512)
     pieces = lax.all_to_all(product, AXES, 0, 0, axis_index_groups=FIRST)
     (blocks,) = call(band_kernel, [((32, 32, 128), BF16)], 0.1)(pieces)
     blocks = lax.all_to_all(blocks, AXES, 0, 0, axis_index_groups=SECOND)
-    (crps_terms,) = call(crps_kernel, [((CH, PTS), F32)], 1.0)(abs_error, spread, node)
     (grad_value,) = call(last_kernel, [((32, 128), F32)], 0.1)(blocks)
     return crps_terms[None], grad_value
 

time: 77.7 us -> 76.5 us (0.985)
  blocking collectives: 15.3 us -> 34.1 us
  waiting for transfers between devices: 12.3 us -> 2.88 us
  starting transfers between devices: 29.2 us -> 21.9 us
  Pallas kernels: 19.9 us -> 16.4 us
    all_to_all x0 -> x1, blocking collectives: none -> 19.5 us  [body(): blocks = lax.all_to_all(blocks, AXES, 0, 0, axis_index_groups=SECOND)]
    all_to_all x1 -> x0, waiting for transfers between devices: 11.1 us -> none  [body(): blocks = lax.all_to_all(blocks, AXES, 0, 0, axis_index_groups=SECOND)]
    all_to_all x1 -> x0, starting transfers between devices: 7.58 us -> none  [body(): blocks = lax.all_to_all(blocks, AXES, 0, 0, axis_index_groups=SECOND)]
    pallas_call x11 -> x10, Pallas kernels: 19.9 us -> 16.4 us  [run(): pl.pallas_call(kernel, out_shape=shapes, in_specs=in_specs, out_specs=out...]
    ppermute x1, starting transfers between devices: 1.12 us -> 4.13 us  [body(): turned_other = lax.ppermute(turned_send, 'core', swap)]
    ppermute x5, waiting for transfers between devices: 0.01 us -> 1.71 us  [moved(): return lax.ppermute(value, AXES, pairs)]
    ppermute x1, starting transfers between devices: 3.32 us -> 1.85 us  [body(): across = lax.ppermute(along, 'core', swap)]
    ppermute x5, starting transfers between devices: 16.7 us -> 15.5 us  [moved(): return lax.ppermute(value, AXES, pairs)]
  transfers between devices with their start and end apart: 9 -> 8, of which waited for: 2 -> 2; matrix products, arithmetic and copies ran while one was open for 0% -> 0% of each run, Pallas kernels for 17% -> 13%
where the time goes in v5:
time: 76.5 us; the launch traced here: 76.3 us
  blocking collectives  34.1 us (45%)
  starting transfers between devices  21.9 us (29%)
  Pallas kernels  16.4 us (21%)
  waiting for transfers between devices  2.88 us (4%)
  between operations  0.84 us (1%)
    all_to_all x1, blocking collectives, body(): blocks = lax.all_to_all(blocks, AXES, 0, 0, axis_index_groups=SECOND)  19.5 us
    pallas_call x10, Pallas kernels, run(): pl.pallas_call(kernel, out_shape=shapes, in_specs=in_specs, out_specs=out...  16.4 us
    ppermute x5, starting transfers between devices, moved(): return lax.ppermute(value, AXES, pairs)  15.5 us
    all_to_all x1, blocking collectives, body(): pieces = lax.all_to_all(product, AXES, 0, 0, axis_index_groups=FIRST)  14.7 us
    ppermute x1, starting transfers between devices, body(): turned_other = lax.ppermute(turned_send, 'core', swap)  4.13 us
    ppermute x1, starting transfers between devices, body(): across = lax.ppermute(along, 'core', swap)  1.85 us
    ppermute x5, waiting for transfers between devices, moved(): return lax.ppermute(value, AXES, pairs)  1.71 us
  transfers between devices with their start and end apart: 8, of which 2 were waited for; matrix products, arithmetic and copies ran while one was open for 0% of the time, Pallas kernels for 13%

profile of v5, /device:TPU:1, one launch (start us, length us, event | category | flops | bytes accessed | tf_op | source)
XLA Modules:
  0.0 76.3 jit_solution(16714073912017006511)
XLA Ops:
  0.6 0.0 copy-start.2
  0.6 0.0 copy-start.3
  0.7 0.0 copy-start.4
  0.7 0.0 copy-start.5
  0.7 0.0 copy-start.8
  0.7 1.2 %shard_map.104 = (bf16[128,1024]{1,0:T(8,128)(2,1)S(1)}, bf16[128,1024]{1,0:T(8,128)(2,1)S(1)}) custom-call(bf16[256,1024]{1,0:T(8,128)(2,1)} %bitcast.8), custom_call_target="tpu_custom_call" | custom-call | flops 8000000000 | bytes 24000000 | tf_op jit(solution)/shard_map/pallas_call | solution.py:64
  1.9 1.6 %collective-permute-start = (bf16[128,1024]{1,0:T(8,128)(2,1)S(1)}, bf16[128,1024]{1,0:T(8,128)(2,1)S(1)}, u32[]{:S(2)}, u32[]{:S(2)}) collective-permute-start(bf16[128,1024]{1,0:T(8,128)(2,1)S(1)} %get-tuple-element.28), channel_id=1, source_target_pairs={{0,1},{1,2},{2,3},{3,4},{4,5},{5,6},{6,7},{7,8},{8,9},{9,10},{10,1... | collective-permute-start | bytes 786440 | tf_op jit(solution)/shard_map/ppermute | solution.py:360
  3.5 4.6 %collective-permute-start.1 = (bf16[128,1024]{1,0:T(8,128)(2,1)S(1)}, bf16[128,1024]{1,0:T(8,128)(2,1)S(1)}, u32[]{:S(2)}, u32[]{:S(2)}) collective-permute-start(bf16[128,1024]{1,0:T(8,128)(2,1)S(1)} %get-tuple-element.29), channel_id=1, source_target_pairs={{1,0},{2,1},{3,2},{4,3},{5,4},{6,5},{7,6},{8,7},{9,8},{10,9},{11,1... | collective-permute-start | bytes 786440 | tf_op jit(solution)/shard_map/ppermute | solution.py:360
  8.1 0.0 copy-done.2
  8.1 0.0 copy-done.3
  8.1 0.0 copy-done.4
  8.1 0.0 copy-done.5
  8.1 0.0 copy-done.8
  8.1 0.0 copy-start
  8.1 0.0 copy-start.7
  8.1 3.5 %shard_map.105 = (bf16[256,1024]{1,0:T(8,128)(2,1)S(1)}, bf16[256,1024]{1,0:T(8,128)(2,1)S(1)}, bf16[8,2,256,256]{3,2,1,0:T(8,128)(2,1)S(1)}, f32[8,2,128,128]{3...) custom-call(bf16[1024,1024]{1,0:T(8,128)(2,1)S(1)} %copy-done.2, bf16[1024,1024]{1,0:T(8,128)(2,1)S(1)} %copy-done.3, ...), custom_call_target="tpu_custom_call" | custom-call | flops 3000000000 | bytes 9000000 | tf_op jit(solution)/shard_map/pallas_call | solution.py:64
  11.6 0.0 collective-permute-done.first_ref
  11.7 1.7 %collective-permute-done.1.second_ref = bf16[128,1024]{1,0:T(8,128)(2,1)S(1)} collective-permute-done((bf16[128,1024]{1,0:T(8,128)(2,1)S(1)}, bf16[128,1024]{1,0:T(8,128)(2,1)S(1)}, u32[]{:S(2)}, u32[]{:S(2)}) %collective-permute-start.1) | collective-permute-done | bytes 262176 | tf_op jit(solution)/shard_map/ppermute | solution.py:360
  13.4 0.0 copy-done
  13.4 0.0 copy-done.7
  13.4 0.0 copy-start.1
  13.4 0.0 copy-start.6
  13.4 3.5 %shard_map.106 = (bf16[8,2,128,256]{3,2,1,0:T(8,128)(2,1)S(1)}, f32[8,4,256]{2,1,0:T(4,128)S(1)}, f32[128,256]{1,0:T(8,128)S(1)}, bf16[128,256]{1,0:T(8,128)(2,1)S(1)}, bf16[256,1024]{1,0:T(8,128)(2,1)S(1)}) custom-call(bf16[128,1024]{1,0:T(8,128)(2,1)S(1)} %collective-permute-done.first_ref, bf16[128,1024]{1,0:T(8,128)(2,1)S(1)} %collective-permute-done.1.second_ref, ...), custom_call_target="tpu_custom_call" | custom-call | flops 3000000000 | bytes 9000000 | tf_op jit(solution)/shard_map/pallas_call | solution.py:64
  16.9 7.0 %collective-permute-start.2 = (bf16[128,256]{1,0:T(8,128)(2,1)S(1)}, bf16[128,256]{1,0:T(8,128)(2,1)S(1)}, u32[]{:S(2)}, u32[]{:S(2)}) collective-permute-start(bf16[128,256]{1,0:T(8,128)(2,1)S(1)} %get-tuple-element.42), channel_id=1, source_target_pairs={{0,128},{1,129},{2,130},{3,131},{4,132},{5,133},{6,134},{7,135},{8... | collective-permute-start | bytes 196616 | tf_op jit(solution)/shard_map/ppermute | solution.py:360
  23.8 0.0 collective-permute-start.3
  23.9 2.4 %collective-permute-start.4 = (bf16[128,256]{1,0:T(8,128)(2,1)S(1)}, bf16[128,256]{1,0:T(8,128)(2,1)S(1)}, u32[]{:S(2)}, u32[]{:S(2)}) collective-permute-start(bf16[128,256]{1,0:T(8,128)(2,1)S(1)} %get-tuple-element.42), channel_id=1, source_target_pairs={{0,192},{1,193},{2,194},{3,195},{4,196},{5,197},{6,198},{7,199},{8... | collective-permute-start | bytes 196616 | tf_op jit(solution)/shard_map/ppermute | solution.py:360
  26.2 0.0 copy-done.1
  26.2 0.0 copy-done.6
  26.2 2.6 %shard_map.107 = (f32[128,1024]{1,0:T(8,128)S(1)}, f32[128,256]{1,0:T(8,128)S(1)}, f32[8,256]{1,0:T(8,128)S(1)}, bf16[1024,512]{1,0:T(8,128)(2,1)S(1)}, bf16[102...) custom-call(f32[128,256]{1,0:T(8,128)S(1)} %get-tuple-element.34.dec, ...), custom_call_target="tpu_custom_call" | custom-call | flops 2000000000 | bytes 6000000 | tf_op jit(solution)/shard_map/pallas_call | solution.py:64
  28.9 4.1 %collective-permute-start.6 = (bf16[1024,512]{1,0:T(8,128)(2,1)S(1)}, bf16[1024,512]{1,0:T(8,128)(2,1)S(1)}, u32[]{:S(2)}, u32[]{:S(2)}) collective-permute-start(bf16[1024,512]{1,0:T(8,128)(2,1)S(1)} %get-tuple-element.52), channel_id=1, source_target_pairs={{0,32},{32,0},{1,33},{33,1},{2,34},{34,2},{3,35},{35,3},{4,36},{36... | collective-permute-start | bytes 3145736 | tf_op jit(solution)/shard_map/ppermute | solution.py:426
  33.0 0.0 collective-permute-done.2.a_ref
  33.0 0.0 collective-permute-done.3.b_ref
  33.0 0.0 collective-permute-done.4.c_ref
  33.1 1.8 %collective-permute-start.5 = (bf16[4,128,256]{2,1,0:T(8,128)(2,1)S(1)}, bf16[4,128,256]{2,1,0:T(8,128)(2,1)S(1)}, u32[]{:S(2)}, u32[]{:S(2)}) collective-permute-start(bf16[4,128,256]{2,1,0:T(8,128)(2,1)S(1)} %shard_map.108.oz_ref), channel_id=1, source_target_pairs={{0,32},{32,0},{1,33},{33,1},{2,34},{34,2},{3,35},{35,3},{4,36},{36... | collective-permute-start | bytes 786440 | tf_op jit(solution)/shard_map/ppermute | solution.py:425
  34.9 1.2 %collective-permute-done.5.oc_ref = bf16[4,128,256]{2,1,0:T(8,128)(2,1)S(1)} collective-permute-done((bf16[4,128,256]{2,1,0:T(8,128)(2,1)S(1)}, bf16[4,128,256]{2,1,0:T(8,128)(2,1)S(1)}, u32[]{:S(2)}, u32[]{:S(2)}) %collective-permute-start.5) | collective-permute-done | bytes 262176 | tf_op jit(solution)/shard_map/ppermute | solution.py:425
  36.1 1.8 %shard_map.109 = (bf16[512,512]{1,0:T(8,128)(2,1)S(1)}, f32[128,256]{1,0:T(8,128)S(1)}, bf16[1024,256]{1,0:T(8,128)(2,1)S(1)}) custom-call(bf16[8,2,256,256]{3,2,1,0:T(8,128)(2,1)S(1)} %get-tuple-element.40.po_ref, bf16[8,2,128,256]{3,2,1,0:T(8,128)(2,1)S(1)} %get-tuple-element.41.ph_ref, bf16[1024,128]{1,0:T(8,128)(2,1)S(1)} %copy-done.7, ...), custom_call_target="tpu_custom_call" | custom-call | flops 2000000000 | bytes 6000000 | tf_op jit(solution)/shard_map/pallas_call | solution.py:64
  37.9 0.5 collective-permute-start.7
  38.4 2.2 %shard_map.110 = (f32[1024,512]{1,0:T(8,128)S(1)}, f32[128,1024]{1,0:T(8,128)}) custom-call(bf16[8,2,256,256]{3,2,1,0:T(8,128)(2,1)S(1)} %get-tuple-element.40.po_ref, bf16[8,2,128,256]{3,2,1,0:T(8,128)(2,1)S(1)} %get-tuple-element.41.ph_ref, bf16[1024,1024]{1,0:T(8,128)(2,1)S(1)} %copy-done, bf16[1024,256]{1,0:T(8,128)(2,1)S(1)} %get-tuple-element.46.hidden_ref, ...), custom_call_target="tpu_custom_call" | custom-call | flops 2000000000 | bytes 6000000 | tf_op jit(solution)/shard_map/pallas_call | solution.py:64
  40.5 0.0 collective-permute-done.7.recv_ref
  40.5 0.0 collective-permute-done.6.u_ref
  40.6 0.8 shard_map.111
  41.3 14.7 %all_to_all.10.pieces_ref = bf16[4,256,512]{2,1,0:T(8,128)(2,1)S(1)} all-to-all(bf16[4,256,512]{2,1,0:T(8,128)(2,1)S(1)} %bitcast.5), channel_id=1, replica_groups={{0,1,2,3},{4,5,6,7},{8,9,10,11},{12,13,14,15},{16,17,18,19},{20,21,22,2..., dimensions={0} | all-to-all | bytes 2097152 | tf_op jit(solution)/shard_map/all_to_all | solution.py:442
  56.0 0.1 shard_map.112
  56.1 19.5 %all_to_all.11.pieces_ref = bf16[32,32,128]{2,1,0:T(8,128)(2,1)S(1)} all-to-all(bf16[32,32,128]{2,1,0:T(8,128)(2,1)S(1)} %shard_map.112), channel_id=1, replica_groups={{0,4,8,12,16,20,24,28,64,68,72,76,80,84,88,92,128,132,136,140,144,148,1..., dimensions={0} | all-to-all | bytes 524288 | tf_op jit(solution)/shard_map/all_to_all | solution.py:444
  75.6 0.7 shard_map.113
  (1 shorter events, 0.0 us)
Async XLA Ops:
  0.6 7.4 %copy-start.2 = (bf16[1024,1024]{1,0:T(8,128)(2,1)S(1)}, bf16[1024,1024]{1,0:T(8,128)(2,1)}, u32[]{:S(2)}) copy-start(bf16[1024,1024]{1,0:T(8,128)(2,1)} %wq_ref.1) | copy-start | bytes 6291460
  0.6 7.4 %copy-start.3 = (bf16[1024,1024]{1,0:T(8,128)(2,1)S(1)}, bf16[1024,1024]{1,0:T(8,128)(2,1)}, u32[]{:S(2)}) copy-start(bf16[1024,1024]{1,0:T(8,128)(2,1)} %wk_ref.3) | copy-start | bytes 6291460
  0.7 7.4 %copy-start.4 = (bf16[1024,1024]{1,0:T(8,128)(2,1)S(1)}, bf16[1024,1024]{1,0:T(8,128)(2,1)}, u32[]{:S(2)}) copy-start(bf16[1024,1024]{1,0:T(8,128)(2,1)} %wv_ref.3) | copy-start | bytes 6291460
  0.7 7.4 %copy-start.5 = (bf16[1,256,1024]{2,1,0:T(8,128)(2,1)S(1)}, bf16[1,256,1024]{2,1,0:T(8,128)(2,1)}, u32[]{:S(2)}) copy-start(bf16[1,256,1024]{2,1,0:T(8,128)(2,1)} %param.9) | copy-start | bytes 1572868
  0.7 7.4 %copy-start.8 = (f32[1024]{0:T(1024)S(1)}, f32[1024]{0:T(1024)}, u32[]{:S(2)}) copy-start(f32[1024]{0:T(1024)} %param.10) | copy-start | bytes 12292
  1.9 9.8 %collective-permute-start = (bf16[128,1024]{1,0:T(8,128)(2,1)S(1)}, bf16[128,1024]{1,0:T(8,128)(2,1)S(1)}, u32[]{:S(2)}, u32[]{:S(2)}) collective-permute-start(bf16[128,1024]{1,0:T(8,128)(2,1)S(1)} %get-tuple-element.28), channel_id=1, source_target_pairs={{0,1},{1,2},{2,3},{3,4},{4,5},{5,6},{6,7},{7,8},{8,9},{9,10},{10,1... | collective-permute-start | bytes 786440 | tf_op jit(solution)/shard_map/ppermute | solution.py:360
  3.5 9.9 %collective-permute-start.1 = (bf16[128,1024]{1,0:T(8,128)(2,1)S(1)}, bf16[128,1024]{1,0:T(8,128)(2,1)S(1)}, u32[]{:S(2)}, u32[]{:S(2)}) collective-permute-start(bf16[128,1024]{1,0:T(8,128)(2,1)S(1)} %get-tuple-element.29), channel_id=1, source_target_pairs={{1,0},{2,1},{3,2},{4,3},{5,4},{6,5},{7,6},{8,7},{9,8},{10,9},{11,1... | collective-permute-start | bytes 786440 | tf_op jit(solution)/shard_map/ppermute | solution.py:360
  8.1 5.3 %copy-start = (bf16[1024,1024]{1,0:T(8,128)(2,1)S(1)}, bf16[1024,1024]{1,0:T(8,128)(2,1)}, u32[]{:S(2)}) copy-start(bf16[1024,1024]{1,0:T(8,128)(2,1)} %wo_ref.5) | copy-start | bytes 6291460
  8.1 5.2 %copy-start.7 = (bf16[1024,128]{1,0:T(8,128)(2,1)S(1)}, bf16[1024,128]{1,0:T(8,128)(2,1)}, u32[]{:S(2)}) copy-start(bf16[1024,128]{1,0:T(8,128)(2,1)} %wd.1) | copy-start | bytes 786436
  13.4 12.9 %copy-start.1 = (s32[1024]{0:T(1024)S(1)}, s32[1024]{0:T(1024)}, u32[]{:S(2)}) copy-start(s32[1024]{0:T(1024)} %param.16) | copy-start | bytes 12292
  13.4 12.9 %copy-start.6 = (f32[128,1024]{1,0:T(8,128)S(1)}, f32[128,1024]{1,0:T(8,128)}, u32[]{:S(2)}) copy-start(f32[128,1024]{1,0:T(8,128)} %truth_ref.1) | copy-start | bytes 1572868
  16.9 16.2 %collective-permute-start.2 = (bf16[128,256]{1,0:T(8,128)(2,1)S(1)}, bf16[128,256]{1,0:T(8,128)(2,1)S(1)}, u32[]{:S(2)}, u32[]{:S(2)}) collective-permute-start(bf16[128,256]{1,0:T(8,128)(2,1)S(1)} %get-tuple-element.42), channel_id=1, source_target_pairs={{0,128},{1,129},{2,130},{3,131},{4,132},{5,133},{6,134},{7,135},{8... | collective-permute-start | bytes 196616 | tf_op jit(solution)/shard_map/ppermute | solution.py:360
  23.8 9.2 %collective-permute-start.3 = (bf16[128,256]{1,0:T(8,128)(2,1)S(1)}, bf16[128,256]{1,0:T(8,128)(2,1)S(1)}, u32[]{:S(2)}, u32[]{:S(2)}) collective-permute-start(bf16[128,256]{1,0:T(8,128)(2,1)S(1)} %get-tuple-element.42), channel_id=1, source_target_pairs={{0,64},{1,65},{2,66},{3,67},{4,68},{5,69},{6,70},{7,71},{8,72},{9,... | collective-permute-start | bytes 196616 | tf_op jit(solution)/shard_map/ppermute | solution.py:360
  23.9 9.2 %collective-permute-start.4 = (bf16[128,256]{1,0:T(8,128)(2,1)S(1)}, bf16[128,256]{1,0:T(8,128)(2,1)S(1)}, u32[]{:S(2)}, u32[]{:S(2)}) collective-permute-start(bf16[128,256]{1,0:T(8,128)(2,1)S(1)} %get-tuple-element.42), channel_id=1, source_target_pairs={{0,192},{1,193},{2,194},{3,195},{4,196},{5,197},{6,198},{7,199},{8... | collective-permute-start | bytes 196616 | tf_op jit(solution)/shard_map/ppermute | solution.py:360
  28.9 11.7 %collective-permute-start.6 = (bf16[1024,512]{1,0:T(8,128)(2,1)S(1)}, bf16[1024,512]{1,0:T(8,128)(2,1)S(1)}, u32[]{:S(2)}, u32[]{:S(2)}) collective-permute-start(bf16[1024,512]{1,0:T(8,128)(2,1)S(1)} %get-tuple-element.52), channel_id=1, source_target_pairs={{0,32},{32,0},{1,33},{33,1},{2,34},{34,2},{3,35},{35,3},{4,36},{36... | collective-permute-start | bytes 3145736 | tf_op jit(solution)/shard_map/ppermute | solution.py:426
  33.1 3.0 %collective-permute-start.5 = (bf16[4,128,256]{2,1,0:T(8,128)(2,1)S(1)}, bf16[4,128,256]{2,1,0:T(8,128)(2,1)S(1)}, u32[]{:S(2)}, u32[]{:S(2)}) collective-permute-start(bf16[4,128,256]{2,1,0:T(8,128)(2,1)S(1)} %shard_map.108.oz_ref), channel_id=1, source_target_pairs={{0,32},{32,0},{1,33},{33,1},{2,34},{34,2},{3,35},{35,3},{4,36},{36... | collective-permute-start | bytes 786440 | tf_op jit(solution)/shard_map/ppermute | solution.py:425
  37.9 2.6 %collective-permute-start.7 = (bf16[512,512]{1,0:T(8,128)(2,1)S(1)}, bf16[512,512]{1,0:T(8,128)(2,1)S(1)}, u32[]{:S(2)}, u32[]{:S(2)}) collective-permute-start(bf16[512,512]{1,0:T(8,128)(2,1)S(1)} %get-tuple-element.53), channel_id=1, source_target_pairs={{0,32},{32,0},{1,33},{33,1},{2,34},{34,2},{3,35},{35,3},{4,36},{36... | collective-permute-start | bytes 1572872 | tf_op jit(solution)/shard_map/ppermute | solution.py:433

commit v6 on v5

--- a/solution.py
+++ b/solution.py
@@ -244,12 +244,14 @@
     count_ref[...] = mm_nt(jnp.ones((16, PTS), BF16), select)[:8]
     core = lax.axis_index("core")
     for columns, ref in ((slice(0, ROWS), n_ref), (slice(ROWS, 2 * ROWS), nh_ref)):
-        for g in range(BANDS):
-            rows = ref[:, g * 32 : (g + 1) * 32].astype(F32).T.astype(BF16)
-            by_x = g % 4 * 8 + g // 4
-            for which, out_ref in ((core, keep_ref), (1 - core, send_ref)):
-                start = pl.multiple_of(jnp.where(which == 0, by_x, g) * 32, 32)
-                out_ref[pl.ds(start, 32), columns] = rows
+        for k in range(8):
+            block = ref[:, k * 128 : (k + 1) * 128].astype(F32).T.astype(BF16)
+            for g in range(k * 4, k * 4 + 4):
+                rows = block[g % 4 * 32 : (g % 4 + 1) * 32]
+                by_x = g % 4 * 8 + g // 4
+                for which, out_ref in ((core, keep_ref), (1 - core, send_ref)):
+                    start = pl.multiple_of(jnp.where(which == 0, by_x, g) * 32, 32)
+                    out_ref[pl.ds(start, 32), columns] = rows
     for pair in range(PAIRS):
         for block in range(2):
             factors = factor_ref[pair]

time: 76.5 us -> 76.5 us (level)
  starting transfers between devices: 21.9 us -> 23.1 us
  Pallas kernels: 16.4 us -> 15.3 us
    ppermute x1, starting transfers between devices: 1.85 us -> 3 us  [body(): across = lax.ppermute(along, 'core', swap)]
    pallas_call x10, Pallas kernels: 16.4 us -> 15.3 us  [run(): pl.pallas_call(kernel, out_shape=shapes, in_specs=in_specs, out_specs=out...]
  transfers between devices with their start and end apart: 8 -> 8, of which waited for: 2 -> 2; matrix products, arithmetic and copies ran while one was open for 0% -> 0% of each run, Pallas kernels for 13% -> 12%
where the time goes in v6:
time: 76.5 us; the launch traced here: 76.3 us
  blocking collectives  34.1 us (45%)
  starting transfers between devices  23.1 us (30%)
  Pallas kernels  15.3 us (20%)
  waiting for transfers between devices  2.88 us (4%)
  between operations  0.84 us (1%)
    all_to_all x1, blocking collectives, body(): blocks = lax.all_to_all(blocks, AXES, 0, 0, axis_index_groups=SECOND)  19.8 us
    ppermute x5, starting transfers between devices, moved(): return lax.ppermute(value, AXES, pairs)  15.5 us
    pallas_call x10, Pallas kernels, run(): pl.pallas_call(kernel, out_shape=shapes, in_specs=in_specs, out_specs=out...  15.3 us
    all_to_all x1, blocking collectives, body(): pieces = lax.all_to_all(product, AXES, 0, 0, axis_index_groups=FIRST)  14.3 us
    ppermute x1, starting transfers between devices, body(): turned_other = lax.ppermute(turned_send, 'core', swap)  4.13 us
    ppermute x1, starting transfers between devices, body(): across = lax.ppermute(along, 'core', swap)  3 us
    ppermute x5, waiting for transfers between devices, moved(): return lax.ppermute(value, AXES, pairs)  1.71 us
  transfers between devices with their start and end apart: 8, of which 2 were waited for; matrix products, arithmetic and copies ran while one was open for 0% of the time, Pallas kernels for 12%

profile of v6, /device:TPU:1, one launch (start us, length us, event | category | flops | bytes accessed | tf_op | source)
XLA Modules:
  0.0 76.3 jit_solution(11896556991943271287)
XLA Ops:
  0.6 0.0 copy-start.2
  0.6 0.0 copy-start.3
  0.7 0.0 copy-start.4
  0.7 0.0 copy-start.5
  0.7 0.0 copy-start.8
  0.7 1.2 %shard_map.104 = (bf16[128,1024]{1,0:T(8,128)(2,1)S(1)}, bf16[128,1024]{1,0:T(8,128)(2,1)S(1)}) custom-call(bf16[256,1024]{1,0:T(8,128)(2,1)} %bitcast.8), custom_call_target="tpu_custom_call" | custom-call | flops 8000000000 | bytes 24000000 | tf_op jit(solution)/shard_map/pallas_call | solution.py:64
  1.9 1.6 %collective-permute-start = (bf16[128,1024]{1,0:T(8,128)(2,1)S(1)}, bf16[128,1024]{1,0:T(8,128)(2,1)S(1)}, u32[]{:S(2)}, u32[]{:S(2)}) collective-permute-start(bf16[128,1024]{1,0:T(8,128)(2,1)S(1)} %get-tuple-element.28), channel_id=1, source_target_pairs={{0,1},{1,2},{2,3},{3,4},{4,5},{5,6},{6,7},{7,8},{8,9},{9,10},{10,1... | collective-permute-start | bytes 786440 | tf_op jit(solution)/shard_map/ppermute | solution.py:362
  3.5 4.6 %collective-permute-start.1 = (bf16[128,1024]{1,0:T(8,128)(2,1)S(1)}, bf16[128,1024]{1,0:T(8,128)(2,1)S(1)}, u32[]{:S(2)}, u32[]{:S(2)}) collective-permute-start(bf16[128,1024]{1,0:T(8,128)(2,1)S(1)} %get-tuple-element.29), channel_id=1, source_target_pairs={{1,0},{2,1},{3,2},{4,3},{5,4},{6,5},{7,6},{8,7},{9,8},{10,9},{11,1... | collective-permute-start | bytes 786440 | tf_op jit(solution)/shard_map/ppermute | solution.py:362
  8.1 0.0 copy-done.2
  8.1 0.0 copy-done.3
  8.1 0.0 copy-done.4
  8.1 0.0 copy-done.5
  8.1 0.0 copy-done.8
  8.1 0.0 copy-start
  8.1 0.0 copy-start.7
  8.1 3.5 %shard_map.105 = (bf16[256,1024]{1,0:T(8,128)(2,1)S(1)}, bf16[256,1024]{1,0:T(8,128)(2,1)S(1)}, bf16[8,2,256,256]{3,2,1,0:T(8,128)(2,1)S(1)}, f32[8,2,128,128]{3...) custom-call(bf16[1024,1024]{1,0:T(8,128)(2,1)S(1)} %copy-done.2, bf16[1024,1024]{1,0:T(8,128)(2,1)S(1)} %copy-done.3, ...), custom_call_target="tpu_custom_call" | custom-call | flops 3000000000 | bytes 9000000 | tf_op jit(solution)/shard_map/pallas_call | solution.py:64
  11.6 0.0 collective-permute-done.first_ref
  11.7 1.7 %collective-permute-done.1.second_ref = bf16[128,1024]{1,0:T(8,128)(2,1)S(1)} collective-permute-done((bf16[128,1024]{1,0:T(8,128)(2,1)S(1)}, bf16[128,1024]{1,0:T(8,128)(2,1)S(1)}, u32[]{:S(2)}, u32[]{:S(2)}) %collective-permute-start.1) | collective-permute-done | bytes 262176 | tf_op jit(solution)/shard_map/ppermute | solution.py:362
  13.4 0.0 copy-done
  13.4 0.0 copy-done.7
  13.4 0.0 copy-start.1
  13.4 0.0 copy-start.6
  13.4 3.5 %shard_map.106 = (bf16[8,2,128,256]{3,2,1,0:T(8,128)(2,1)S(1)}, f32[8,4,256]{2,1,0:T(4,128)S(1)}, f32[128,256]{1,0:T(8,128)S(1)}, bf16[128,256]{1,0:T(8,128)(2,1)S(1)}, bf16[256,1024]{1,0:T(8,128)(2,1)S(1)}) custom-call(bf16[128,1024]{1,0:T(8,128)(2,1)S(1)} %collective-permute-done.first_ref, bf16[128,1024]{1,0:T(8,128)(2,1)S(1)} %collective-permute-done.1.second_ref, ...), custom_call_target="tpu_custom_call" | custom-call | flops 3000000000 | bytes 9000000 | tf_op jit(solution)/shard_map/pallas_call | solution.py:64
  16.9 7.0 %collective-permute-start.2 = (bf16[128,256]{1,0:T(8,128)(2,1)S(1)}, bf16[128,256]{1,0:T(8,128)(2,1)S(1)}, u32[]{:S(2)}, u32[]{:S(2)}) collective-permute-start(bf16[128,256]{1,0:T(8,128)(2,1)S(1)} %get-tuple-element.42), channel_id=1, source_target_pairs={{0,128},{1,129},{2,130},{3,131},{4,132},{5,133},{6,134},{7,135},{8... | collective-permute-start | bytes 196616 | tf_op jit(solution)/shard_map/ppermute | solution.py:362
  23.8 0.0 collective-permute-start.3
  23.9 2.4 %collective-permute-start.4 = (bf16[128,256]{1,0:T(8,128)(2,1)S(1)}, bf16[128,256]{1,0:T(8,128)(2,1)S(1)}, u32[]{:S(2)}, u32[]{:S(2)}) collective-permute-start(bf16[128,256]{1,0:T(8,128)(2,1)S(1)} %get-tuple-element.42), channel_id=1, source_target_pairs={{0,192},{1,193},{2,194},{3,195},{4,196},{5,197},{6,198},{7,199},{8... | collective-permute-start | bytes 196616 | tf_op jit(solution)/shard_map/ppermute | solution.py:362
  26.2 0.0 copy-done.1
  26.2 0.0 copy-done.6
  26.2 1.5 %shard_map.107 = (f32[128,1024]{1,0:T(8,128)S(1)}, f32[128,256]{1,0:T(8,128)S(1)}, f32[8,256]{1,0:T(8,128)S(1)}, bf16[1024,512]{1,0:T(8,128)(2,1)S(1)}, bf16[102...) custom-call(f32[128,256]{1,0:T(8,128)S(1)} %get-tuple-element.34.dec, ...), custom_call_target="tpu_custom_call" | custom-call | flops 2000000000 | bytes 6000000 | tf_op jit(solution)/shard_map/pallas_call | solution.py:64
  27.7 4.1 %collective-permute-start.6 = (bf16[1024,512]{1,0:T(8,128)(2,1)S(1)}, bf16[1024,512]{1,0:T(8,128)(2,1)S(1)}, u32[]{:S(2)}, u32[]{:S(2)}) collective-permute-start(bf16[1024,512]{1,0:T(8,128)(2,1)S(1)} %get-tuple-element.52), channel_id=1, source_target_pairs={{0,32},{32,0},{1,33},{33,1},{2,34},{34,2},{3,35},{35,3},{4,36},{36... | collective-permute-start | bytes 3145736 | tf_op jit(solution)/shard_map/ppermute | solution.py:428
  31.9 0.0 collective-permute-done.2.a_ref
  31.9 0.0 collective-permute-done.3.b_ref
  31.9 0.0 collective-permute-done.4.c_ref
  31.9 3.0 %collective-permute-start.5 = (bf16[4,128,256]{2,1,0:T(8,128)(2,1)S(1)}, bf16[4,128,256]{2,1,0:T(8,128)(2,1)S(1)}, u32[]{:S(2)}, u32[]{:S(2)}) collective-permute-start(bf16[4,128,256]{2,1,0:T(8,128)(2,1)S(1)} %shard_map.108.oz_ref), channel_id=1, source_target_pairs={{0,32},{32,0},{1,33},{33,1},{2,34},{34,2},{3,35},{35,3},{4,36},{36... | collective-permute-start | bytes 786440 | tf_op jit(solution)/shard_map/ppermute | solution.py:427
  34.9 1.2 %collective-permute-done.5.oc_ref = bf16[4,128,256]{2,1,0:T(8,128)(2,1)S(1)} collective-permute-done((bf16[4,128,256]{2,1,0:T(8,128)(2,1)S(1)}, bf16[4,128,256]{2,1,0:T(8,128)(2,1)S(1)}, u32[]{:S(2)}, u32[]{:S(2)}) %collective-permute-start.5) | collective-permute-done | bytes 262176 | tf_op jit(solution)/shard_map/ppermute | solution.py:427
  36.1 1.8 %shard_map.109 = (bf16[512,512]{1,0:T(8,128)(2,1)S(1)}, f32[128,256]{1,0:T(8,128)S(1)}, bf16[1024,256]{1,0:T(8,128)(2,1)S(1)}) custom-call(bf16[8,2,256,256]{3,2,1,0:T(8,128)(2,1)S(1)} %get-tuple-element.40.po_ref, bf16[8,2,128,256]{3,2,1,0:T(8,128)(2,1)S(1)} %get-tuple-element.41.ph_ref, bf16[1024,128]{1,0:T(8,128)(2,1)S(1)} %copy-done.7, ...), custom_call_target="tpu_custom_call" | custom-call | flops 2000000000 | bytes 6000000 | tf_op jit(solution)/shard_map/pallas_call | solution.py:64
  37.9 0.5 collective-permute-start.7
  38.4 2.2 %shard_map.110 = (f32[1024,512]{1,0:T(8,128)S(1)}, f32[128,1024]{1,0:T(8,128)}) custom-call(bf16[8,2,256,256]{3,2,1,0:T(8,128)(2,1)S(1)} %get-tuple-element.40.po_ref, bf16[8,2,128,256]{3,2,1,0:T(8,128)(2,1)S(1)} %get-tuple-element.41.ph_ref, bf16[1024,1024]{1,0:T(8,128)(2,1)S(1)} %copy-done, bf16[1024,256]{1,0:T(8,128)(2,1)S(1)} %get-tuple-element.46.hidden_ref, ...), custom_call_target="tpu_custom_call" | custom-call | flops 2000000000 | bytes 6000000 | tf_op jit(solution)/shard_map/pallas_call | solution.py:64
  40.5 0.0 collective-permute-done.7.recv_ref
  40.5 0.0 collective-permute-done.6.u_ref
  40.6 0.8 shard_map.111
  41.3 14.3 %all_to_all.10.pieces_ref = bf16[4,256,512]{2,1,0:T(8,128)(2,1)S(1)} all-to-all(bf16[4,256,512]{2,1,0:T(8,128)(2,1)S(1)} %bitcast.5), channel_id=1, replica_groups={{0,1,2,3},{4,5,6,7},{8,9,10,11},{12,13,14,15},{16,17,18,19},{20,21,22,2..., dimensions={0} | all-to-all | bytes 2097152 | tf_op jit(solution)/shard_map/all_to_all | solution.py:444
  55.7 0.1 shard_map.112
  55.8 19.8 %all_to_all.11.pieces_ref = bf16[32,32,128]{2,1,0:T(8,128)(2,1)S(1)} all-to-all(bf16[32,32,128]{2,1,0:T(8,128)(2,1)S(1)} %shard_map.112), channel_id=1, replica_groups={{0,4,8,12,16,20,24,28,64,68,72,76,80,84,88,92,128,132,136,140,144,148,1..., dimensions={0} | all-to-all | bytes 524288 | tf_op jit(solution)/shard_map/all_to_all | solution.py:446
  75.6 0.7 shard_map.113
  (1 shorter events, 0.0 us)
Async XLA Ops:
  0.6 7.4 %copy-start.2 = (bf16[1024,1024]{1,0:T(8,128)(2,1)S(1)}, bf16[1024,1024]{1,0:T(8,128)(2,1)}, u32[]{:S(2)}) copy-start(bf16[1024,1024]{1,0:T(8,128)(2,1)} %wq_ref.1) | copy-start | bytes 6291460
  0.6 7.4 %copy-start.3 = (bf16[1024,1024]{1,0:T(8,128)(2,1)S(1)}, bf16[1024,1024]{1,0:T(8,128)(2,1)}, u32[]{:S(2)}) copy-start(bf16[1024,1024]{1,0:T(8,128)(2,1)} %wk_ref.3) | copy-start | bytes 6291460
  0.7 7.4 %copy-start.4 = (bf16[1024,1024]{1,0:T(8,128)(2,1)S(1)}, bf16[1024,1024]{1,0:T(8,128)(2,1)}, u32[]{:S(2)}) copy-start(bf16[1024,1024]{1,0:T(8,128)(2,1)} %wv_ref.3) | copy-start | bytes 6291460
  0.7 7.4 %copy-start.5 = (bf16[1,256,1024]{2,1,0:T(8,128)(2,1)S(1)}, bf16[1,256,1024]{2,1,0:T(8,128)(2,1)}, u32[]{:S(2)}) copy-start(bf16[1,256,1024]{2,1,0:T(8,128)(2,1)} %param.9) | copy-start | bytes 1572868
  0.7 7.4 %copy-start.8 = (f32[1024]{0:T(1024)S(1)}, f32[1024]{0:T(1024)}, u32[]{:S(2)}) copy-start(f32[1024]{0:T(1024)} %param.10) | copy-start | bytes 12292
  1.9 9.8 %collective-permute-start = (bf16[128,1024]{1,0:T(8,128)(2,1)S(1)}, bf16[128,1024]{1,0:T(8,128)(2,1)S(1)}, u32[]{:S(2)}, u32[]{:S(2)}) collective-permute-start(bf16[128,1024]{1,0:T(8,128)(2,1)S(1)} %get-tuple-element.28), channel_id=1, source_target_pairs={{0,1},{1,2},{2,3},{3,4},{4,5},{5,6},{6,7},{7,8},{8,9},{9,10},{10,1... | collective-permute-start | bytes 786440 | tf_op jit(solution)/shard_map/ppermute | solution.py:362
  3.5 9.9 %collective-permute-start.1 = (bf16[128,1024]{1,0:T(8,128)(2,1)S(1)}, bf16[128,1024]{1,0:T(8,128)(2,1)S(1)}, u32[]{:S(2)}, u32[]{:S(2)}) collective-permute-start(bf16[128,1024]{1,0:T(8,128)(2,1)S(1)} %get-tuple-element.29), channel_id=1, source_target_pairs={{1,0},{2,1},{3,2},{4,3},{5,4},{6,5},{7,6},{8,7},{9,8},{10,9},{11,1... | collective-permute-start | bytes 786440 | tf_op jit(solution)/shard_map/ppermute | solution.py:362
  8.1 5.3 %copy-start = (bf16[1024,1024]{1,0:T(8,128)(2,1)S(1)}, bf16[1024,1024]{1,0:T(8,128)(2,1)}, u32[]{:S(2)}) copy-start(bf16[1024,1024]{1,0:T(8,128)(2,1)} %wo_ref.5) | copy-start | bytes 6291460
  8.1 5.2 %copy-start.7 = (bf16[1024,128]{1,0:T(8,128)(2,1)S(1)}, bf16[1024,128]{1,0:T(8,128)(2,1)}, u32[]{:S(2)}) copy-start(bf16[1024,128]{1,0:T(8,128)(2,1)} %wd.1) | copy-start | bytes 786436
  13.4 12.9 %copy-start.1 = (s32[1024]{0:T(1024)S(1)}, s32[1024]{0:T(1024)}, u32[]{:S(2)}) copy-start(s32[1024]{0:T(1024)} %param.16) | copy-start | bytes 12292
  13.4 12.9 %copy-start.6 = (f32[128,1024]{1,0:T(8,128)S(1)}, f32[128,1024]{1,0:T(8,128)}, u32[]{:S(2)}) copy-start(f32[128,1024]{1,0:T(8,128)} %truth_ref.1) | copy-start | bytes 1572868
  16.9 15.0 %collective-permute-start.2 = (bf16[128,256]{1,0:T(8,128)(2,1)S(1)}, bf16[128,256]{1,0:T(8,128)(2,1)S(1)}, u32[]{:S(2)}, u32[]{:S(2)}) collective-permute-start(bf16[128,256]{1,0:T(8,128)(2,1)S(1)} %get-tuple-element.42), channel_id=1, source_target_pairs={{0,128},{1,129},{2,130},{3,131},{4,132},{5,133},{6,134},{7,135},{8... | collective-permute-start | bytes 196616 | tf_op jit(solution)/shard_map/ppermute | solution.py:362
  23.8 8.0 %collective-permute-start.3 = (bf16[128,256]{1,0:T(8,128)(2,1)S(1)}, bf16[128,256]{1,0:T(8,128)(2,1)S(1)}, u32[]{:S(2)}, u32[]{:S(2)}) collective-permute-start(bf16[128,256]{1,0:T(8,128)(2,1)S(1)} %get-tuple-element.42), channel_id=1, source_target_pairs={{0,64},{1,65},{2,66},{3,67},{4,68},{5,69},{6,70},{7,71},{8,72},{9,... | collective-permute-start | bytes 196616 | tf_op jit(solution)/shard_map/ppermute | solution.py:362
  23.9 8.0 %collective-permute-start.4 = (bf16[128,256]{1,0:T(8,128)(2,1)S(1)}, bf16[128,256]{1,0:T(8,128)(2,1)S(1)}, u32[]{:S(2)}, u32[]{:S(2)}) collective-permute-start(bf16[128,256]{1,0:T(8,128)(2,1)S(1)} %get-tuple-element.42), channel_id=1, source_target_pairs={{0,192},{1,193},{2,194},{3,195},{4,196},{5,197},{6,198},{7,199},{8... | collective-permute-start | bytes 196616 | tf_op jit(solution)/shard_map/ppermute | solution.py:362
  27.7 12.8 %collective-permute-start.6 = (bf16[1024,512]{1,0:T(8,128)(2,1)S(1)}, bf16[1024,512]{1,0:T(8,128)(2,1)S(1)}, u32[]{:S(2)}, u32[]{:S(2)}) collective-permute-start(bf16[1024,512]{1,0:T(8,128)(2,1)S(1)} %get-tuple-element.52), channel_id=1, source_target_pairs={{0,32},{32,0},{1,33},{33,1},{2,34},{34,2},{3,35},{35,3},{4,36},{36... | collective-permute-start | bytes 3145736 | tf_op jit(solution)/shard_map/ppermute | solution.py:428
  31.9 4.2 %collective-permute-start.5 = (bf16[4,128,256]{2,1,0:T(8,128)(2,1)S(1)}, bf16[4,128,256]{2,1,0:T(8,128)(2,1)S(1)}, u32[]{:S(2)}, u32[]{:S(2)}) collective-permute-start(bf16[4,128,256]{2,1,0:T(8,128)(2,1)S(1)} %shard_map.108.oz_ref), channel_id=1, source_target_pairs={{0,32},{32,0},{1,33},{33,1},{2,34},{34,2},{3,35},{35,3},{4,36},{36... | collective-permute-start | bytes 786440 | tf_op jit(solution)/shard_map/ppermute | solution.py:427
  37.9 2.6 %collective-permute-start.7 = (bf16[512,512]{1,0:T(8,128)(2,1)S(1)}, bf16[512,512]{1,0:T(8,128)(2,1)S(1)}, u32[]{:S(2)}, u32[]{:S(2)}) collective-permute-start(bf16[512,512]{1,0:T(8,128)(2,1)S(1)} %get-tuple-element.53), channel_id=1, source_target_pairs={{0,32},{32,0},{1,33},{33,1},{2,34},{34,2},{3,35},{35,3},{4,36},{36... | collective-permute-start | bytes 1572872 | tf_op jit(solution)/shard_map/ppermute | solution.py:435

commit v7 on v5

--- a/solution.py
+++ b/solution.py
@@ -298,9 +298,7 @@
         total += differ * inverse
     spread_ref[...] = spread
     node_grad = (slope_ref[...] - count_ref[:1] * total * (1.0 / (MEMBERS - 1))) * (1.0 / MEMBERS)
-    high = node_grad.astype(BF16)
-    rest = (node_grad - high.astype(F32)).astype(BF16)
-    hidden_grad = (mm(wd[...], high) + mm(wd[...], rest)).astype(BF16)
+    hidden_grad = mm(wd[...], node_grad.astype(BF16)).astype(BF16)
     hidden_ref[...] = hidden_grad
     value_terms(1, hidden_grad, wo_ref, po_ref, ph_ref, send_ref)
 

time: 76.5 us -> 76.3 us (level)
  no operation moved by 1% of the time
where the time goes in v7:
time: 76.3 us; the launch traced here: 76.1 us
  blocking collectives  34.2 us (45%)
  starting transfers between devices  21.9 us (29%)
  Pallas kernels  16.2 us (21%)
  waiting for transfers between devices  2.88 us (4%)
  between operations  0.84 us (1%)
    all_to_all x1, blocking collectives, body(): blocks = lax.all_to_all(blocks, AXES, 0, 0, axis_index_groups=SECOND)  19.5 us
    pallas_call x10, Pallas kernels, run(): pl.pallas_call(kernel, out_shape=shapes, in_specs=in_specs, out_specs=out...  16.2 us
    ppermute x5, starting transfers between devices, moved(): return lax.ppermute(value, AXES, pairs)  15.5 us
    all_to_all x1, blocking collectives, body(): pieces = lax.all_to_all(product, AXES, 0, 0, axis_index_groups=FIRST)  14.7 us
    ppermute x1, starting transfers between devices, body(): turned_other = lax.ppermute(turned_send, 'core', swap)  4.13 us
    ppermute x1, starting transfers between devices, body(): across = lax.ppermute(along, 'core', swap)  1.85 us
    ppermute x5, waiting for transfers between devices, moved(): return lax.ppermute(value, AXES, pairs)  1.71 us
  transfers between devices with their start and end apart: 8, of which 2 were waited for; matrix products, arithmetic and copies ran while one was open for 0% of the time, Pallas kernels for 13%

profile of v7, /device:TPU:1, one launch (start us, length us, event | category | flops | bytes accessed | tf_op | source)
XLA Modules:
  0.0 76.1 jit_solution(6174872770838101190)
XLA Ops:
  0.6 0.0 copy-start.2
  0.6 0.0 copy-start.3
  0.7 0.0 copy-start.4
  0.7 0.0 copy-start.5
  0.7 0.0 copy-start.8
  0.7 1.2 %shard_map.104 = (bf16[128,1024]{1,0:T(8,128)(2,1)S(1)}, bf16[128,1024]{1,0:T(8,128)(2,1)S(1)}) custom-call(bf16[256,1024]{1,0:T(8,128)(2,1)} %bitcast.8), custom_call_target="tpu_custom_call" | custom-call | flops 8000000000 | bytes 24000000 | tf_op jit(solution)/shard_map/pallas_call | solution.py:64
  1.9 1.6 %collective-permute-start = (bf16[128,1024]{1,0:T(8,128)(2,1)S(1)}, bf16[128,1024]{1,0:T(8,128)(2,1)S(1)}, u32[]{:S(2)}, u32[]{:S(2)}) collective-permute-start(bf16[128,1024]{1,0:T(8,128)(2,1)S(1)} %get-tuple-element.28), channel_id=1, source_target_pairs={{0,1},{1,2},{2,3},{3,4},{4,5},{5,6},{6,7},{7,8},{8,9},{9,10},{10,1... | collective-permute-start | bytes 786440 | tf_op jit(solution)/shard_map/ppermute | solution.py:358
  3.5 4.6 %collective-permute-start.1 = (bf16[128,1024]{1,0:T(8,128)(2,1)S(1)}, bf16[128,1024]{1,0:T(8,128)(2,1)S(1)}, u32[]{:S(2)}, u32[]{:S(2)}) collective-permute-start(bf16[128,1024]{1,0:T(8,128)(2,1)S(1)} %get-tuple-element.29), channel_id=1, source_target_pairs={{1,0},{2,1},{3,2},{4,3},{5,4},{6,5},{7,6},{8,7},{9,8},{10,9},{11,1... | collective-permute-start | bytes 786440 | tf_op jit(solution)/shard_map/ppermute | solution.py:358
  8.1 0.0 copy-done.2
  8.1 0.0 copy-done.3
  8.1 0.0 copy-done.4
  8.1 0.0 copy-done.5
  8.1 0.0 copy-done.8
  8.1 0.0 copy-start
  8.1 0.0 copy-start.7
  8.1 3.5 %shard_map.105 = (bf16[256,1024]{1,0:T(8,128)(2,1)S(1)}, bf16[256,1024]{1,0:T(8,128)(2,1)S(1)}, bf16[8,2,256,256]{3,2,1,0:T(8,128)(2,1)S(1)}, f32[8,2,128,128]{3...) custom-call(bf16[1024,1024]{1,0:T(8,128)(2,1)S(1)} %copy-done.2, bf16[1024,1024]{1,0:T(8,128)(2,1)S(1)} %copy-done.3, ...), custom_call_target="tpu_custom_call" | custom-call | flops 3000000000 | bytes 9000000 | tf_op jit(solution)/shard_map/pallas_call | solution.py:64
  11.6 0.0 collective-permute-done.first_ref
  11.7 1.7 %collective-permute-done.1.second_ref = bf16[128,1024]{1,0:T(8,128)(2,1)S(1)} collective-permute-done((bf16[128,1024]{1,0:T(8,128)(2,1)S(1)}, bf16[128,1024]{1,0:T(8,128)(2,1)S(1)}, u32[]{:S(2)}, u32[]{:S(2)}) %collective-permute-start.1) | collective-permute-done | bytes 262176 | tf_op jit(solution)/shard_map/ppermute | solution.py:358
  13.4 0.0 copy-done
  13.4 0.0 copy-done.7
  13.4 0.0 copy-start.1
  13.4 0.0 copy-start.6
  13.4 3.5 %shard_map.106 = (bf16[8,2,128,256]{3,2,1,0:T(8,128)(2,1)S(1)}, f32[8,4,256]{2,1,0:T(4,128)S(1)}, f32[128,256]{1,0:T(8,128)S(1)}, bf16[128,256]{1,0:T(8,128)(2,1)S(1)}, bf16[256,1024]{1,0:T(8,128)(2,1)S(1)}) custom-call(bf16[128,1024]{1,0:T(8,128)(2,1)S(1)} %collective-permute-done.first_ref, bf16[128,1024]{1,0:T(8,128)(2,1)S(1)} %collective-permute-done.1.second_ref, ...), custom_call_target="tpu_custom_call" | custom-call | flops 3000000000 | bytes 9000000 | tf_op jit(solution)/shard_map/pallas_call | solution.py:64
  16.9 7.0 %collective-permute-start.2 = (bf16[128,256]{1,0:T(8,128)(2,1)S(1)}, bf16[128,256]{1,0:T(8,128)(2,1)S(1)}, u32[]{:S(2)}, u32[]{:S(2)}) collective-permute-start(bf16[128,256]{1,0:T(8,128)(2,1)S(1)} %get-tuple-element.42), channel_id=1, source_target_pairs={{0,128},{1,129},{2,130},{3,131},{4,132},{5,133},{6,134},{7,135},{8... | collective-permute-start | bytes 196616 | tf_op jit(solution)/shard_map/ppermute | solution.py:358
  23.8 0.0 collective-permute-start.3
  23.9 2.4 %collective-permute-start.4 = (bf16[128,256]{1,0:T(8,128)(2,1)S(1)}, bf16[128,256]{1,0:T(8,128)(2,1)S(1)}, u32[]{:S(2)}, u32[]{:S(2)}) collective-permute-start(bf16[128,256]{1,0:T(8,128)(2,1)S(1)} %get-tuple-element.42), channel_id=1, source_target_pairs={{0,192},{1,193},{2,194},{3,195},{4,196},{5,197},{6,198},{7,199},{8... | collective-permute-start | bytes 196616 | tf_op jit(solution)/shard_map/ppermute | solution.py:358
  26.2 0.0 copy-done.1
  26.2 0.0 copy-done.6
  26.2 2.6 %shard_map.107 = (f32[128,1024]{1,0:T(8,128)S(1)}, f32[128,256]{1,0:T(8,128)S(1)}, f32[8,256]{1,0:T(8,128)S(1)}, bf16[1024,512]{1,0:T(8,128)(2,1)S(1)}, bf16[102...) custom-call(f32[128,256]{1,0:T(8,128)S(1)} %get-tuple-element.34.dec, ...), custom_call_target="tpu_custom_call" | custom-call | flops 2000000000 | bytes 6000000 | tf_op jit(solution)/shard_map/pallas_call | solution.py:64
  28.9 4.1 %collective-permute-start.6 = (bf16[1024,512]{1,0:T(8,128)(2,1)S(1)}, bf16[1024,512]{1,0:T(8,128)(2,1)S(1)}, u32[]{:S(2)}, u32[]{:S(2)}) collective-permute-start(bf16[1024,512]{1,0:T(8,128)(2,1)S(1)} %get-tuple-element.52), channel_id=1, source_target_pairs={{0,32},{32,0},{1,33},{33,1},{2,34},{34,2},{3,35},{35,3},{4,36},{36... | collective-permute-start | bytes 3145736 | tf_op jit(solution)/shard_map/ppermute | solution.py:424
  33.0 0.0 collective-permute-done.2.a_ref
  33.0 0.0 collective-permute-done.3.b_ref
  33.0 0.0 collective-permute-done.4.c_ref
  33.1 1.8 %collective-permute-start.5 = (bf16[4,128,256]{2,1,0:T(8,128)(2,1)S(1)}, bf16[4,128,256]{2,1,0:T(8,128)(2,1)S(1)}, u32[]{:S(2)}, u32[]{:S(2)}) collective-permute-start(bf16[4,128,256]{2,1,0:T(8,128)(2,1)S(1)} %shard_map.108.oz_ref), channel_id=1, source_target_pairs={{0,32},{32,0},{1,33},{33,1},{2,34},{34,2},{3,35},{35,3},{4,36},{36... | collective-permute-start | bytes 786440 | tf_op jit(solution)/shard_map/ppermute | solution.py:423
  34.9 1.2 %collective-permute-done.5.oc_ref = bf16[4,128,256]{2,1,0:T(8,128)(2,1)S(1)} collective-permute-done((bf16[4,128,256]{2,1,0:T(8,128)(2,1)S(1)}, bf16[4,128,256]{2,1,0:T(8,128)(2,1)S(1)}, u32[]{:S(2)}, u32[]{:S(2)}) %collective-permute-start.5) | collective-permute-done | bytes 262176 | tf_op jit(solution)/shard_map/ppermute | solution.py:423
  36.1 1.7 %shard_map.109 = (bf16[512,512]{1,0:T(8,128)(2,1)S(1)}, f32[128,256]{1,0:T(8,128)S(1)}, bf16[1024,256]{1,0:T(8,128)(2,1)S(1)}) custom-call(bf16[8,2,256,256]{3,2,1,0:T(8,128)(2,1)S(1)} %get-tuple-element.40.po_ref, bf16[8,2,128,256]{3,2,1,0:T(8,128)(2,1)S(1)} %get-tuple-element.41.ph_ref, bf16[1024,128]{1,0:T(8,128)(2,1)S(1)} %copy-done.7, ...), custom_call_target="tpu_custom_call" | custom-call | flops 2000000000 | bytes 6000000 | tf_op jit(solution)/shard_map/pallas_call | solution.py:64
  37.7 0.5 collective-permute-start.7
  38.2 2.2 %shard_map.110 = (f32[1024,512]{1,0:T(8,128)S(1)}, f32[128,1024]{1,0:T(8,128)}) custom-call(bf16[8,2,256,256]{3,2,1,0:T(8,128)(2,1)S(1)} %get-tuple-element.40.po_ref, bf16[8,2,128,256]{3,2,1,0:T(8,128)(2,1)S(1)} %get-tuple-element.41.ph_ref, bf16[1024,1024]{1,0:T(8,128)(2,1)S(1)} %copy-done, bf16[1024,256]{1,0:T(8,128)(2,1)S(1)} %get-tuple-element.46.hidden_ref, ...), custom_call_target="tpu_custom_call" | custom-call | flops 2000000000 | bytes 6000000 | tf_op jit(solution)/shard_map/pallas_call | solution.py:64
  40.4 0.0 collective-permute-done.7.recv_ref
  40.4 0.0 collective-permute-done.6.u_ref
  40.4 0.8 shard_map.111
  41.2 14.7 %all_to_all.10.pieces_ref = bf16[4,256,512]{2,1,0:T(8,128)(2,1)S(1)} all-to-all(bf16[4,256,512]{2,1,0:T(8,128)(2,1)S(1)} %bitcast.5), channel_id=1, replica_groups={{0,1,2,3},{4,5,6,7},{8,9,10,11},{12,13,14,15},{16,17,18,19},{20,21,22,2..., dimensions={0} | all-to-all | bytes 2097152 | tf_op jit(solution)/shard_map/all_to_all | solution.py:440
  55.8 0.1 shard_map.112
  56.0 19.5 %all_to_all.11.pieces_ref = bf16[32,32,128]{2,1,0:T(8,128)(2,1)S(1)} all-to-all(bf16[32,32,128]{2,1,0:T(8,128)(2,1)S(1)} %shard_map.112), channel_id=1, replica_groups={{0,4,8,12,16,20,24,28,64,68,72,76,80,84,88,92,128,132,136,140,144,148,1..., dimensions={0} | all-to-all | bytes 524288 | tf_op jit(solution)/shard_map/all_to_all | solution.py:442
  75.5 0.7 shard_map.113
  (1 shorter events, 0.0 us)
Async XLA Ops:
  0.6 7.4 %copy-start.2 = (bf16[1024,1024]{1,0:T(8,128)(2,1)S(1)}, bf16[1024,1024]{1,0:T(8,128)(2,1)}, u32[]{:S(2)}) copy-start(bf16[1024,1024]{1,0:T(8,128)(2,1)} %wq_ref.1) | copy-start | bytes 6291460
  0.6 7.4 %copy-start.3 = (bf16[1024,1024]{1,0:T(8,128)(2,1)S(1)}, bf16[1024,1024]{1,0:T(8,128)(2,1)}, u32[]{:S(2)}) copy-start(bf16[1024,1024]{1,0:T(8,128)(2,1)} %wk_ref.3) | copy-start | bytes 6291460
  0.7 7.4 %copy-start.4 = (bf16[1024,1024]{1,0:T(8,128)(2,1)S(1)}, bf16[1024,1024]{1,0:T(8,128)(2,1)}, u32[]{:S(2)}) copy-start(bf16[1024,1024]{1,0:T(8,128)(2,1)} %wv_ref.3) | copy-start | bytes 6291460
  0.7 7.4 %copy-start.5 = (bf16[1,256,1024]{2,1,0:T(8,128)(2,1)S(1)}, bf16[1,256,1024]{2,1,0:T(8,128)(2,1)}, u32[]{:S(2)}) copy-start(bf16[1,256,1024]{2,1,0:T(8,128)(2,1)} %param.9) | copy-start | bytes 1572868
  0.7 7.4 %copy-start.8 = (f32[1024]{0:T(1024)S(1)}, f32[1024]{0:T(1024)}, u32[]{:S(2)}) copy-start(f32[1024]{0:T(1024)} %param.10) | copy-start | bytes 12292
  1.9 9.8 %collective-permute-start = (bf16[128,1024]{1,0:T(8,128)(2,1)S(1)}, bf16[128,1024]{1,0:T(8,128)(2,1)S(1)}, u32[]{:S(2)}, u32[]{:S(2)}) collective-permute-start(bf16[128,1024]{1,0:T(8,128)(2,1)S(1)} %get-tuple-element.28), channel_id=1, source_target_pairs={{0,1},{1,2},{2,3},{3,4},{4,5},{5,6},{6,7},{7,8},{8,9},{9,10},{10,1... | collective-permute-start | bytes 786440 | tf_op jit(solution)/shard_map/ppermute | solution.py:358
  3.5 9.9 %collective-permute-start.1 = (bf16[128,1024]{1,0:T(8,128)(2,1)S(1)}, bf16[128,1024]{1,0:T(8,128)(2,1)S(1)}, u32[]{:S(2)}, u32[]{:S(2)}) collective-permute-start(bf16[128,1024]{1,0:T(8,128)(2,1)S(1)} %get-tuple-element.29), channel_id=1, source_target_pairs={{1,0},{2,1},{3,2},{4,3},{5,4},{6,5},{7,6},{8,7},{9,8},{10,9},{11,1... | collective-permute-start | bytes 786440 | tf_op jit(solution)/shard_map/ppermute | solution.py:358
  8.1 5.3 %copy-start = (bf16[1024,1024]{1,0:T(8,128)(2,1)S(1)}, bf16[1024,1024]{1,0:T(8,128)(2,1)}, u32[]{:S(2)}) copy-start(bf16[1024,1024]{1,0:T(8,128)(2,1)} %wo_ref.5) | copy-start | bytes 6291460
  8.1 5.2 %copy-start.7 = (bf16[1024,128]{1,0:T(8,128)(2,1)S(1)}, bf16[1024,128]{1,0:T(8,128)(2,1)}, u32[]{:S(2)}) copy-start(bf16[1024,128]{1,0:T(8,128)(2,1)} %wd.1) | copy-start | bytes 786436
  13.4 12.9 %copy-start.1 = (s32[1024]{0:T(1024)S(1)}, s32[1024]{0:T(1024)}, u32[]{:S(2)}) copy-start(s32[1024]{0:T(1024)} %param.16) | copy-start | bytes 12292
  13.4 12.9 %copy-start.6 = (f32[128,1024]{1,0:T(8,128)S(1)}, f32[128,1024]{1,0:T(8,128)}, u32[]{:S(2)}) copy-start(f32[128,1024]{1,0:T(8,128)} %truth_ref.1) | copy-start | bytes 1572868
  16.9 16.2 %collective-permute-start.2 = (bf16[128,256]{1,0:T(8,128)(2,1)S(1)}, bf16[128,256]{1,0:T(8,128)(2,1)S(1)}, u32[]{:S(2)}, u32[]{:S(2)}) collective-permute-start(bf16[128,256]{1,0:T(8,128)(2,1)S(1)} %get-tuple-element.42), channel_id=1, source_target_pairs={{0,128},{1,129},{2,130},{3,131},{4,132},{5,133},{6,134},{7,135},{8... | collective-permute-start | bytes 196616 | tf_op jit(solution)/shard_map/ppermute | solution.py:358
  23.8 9.2 %collective-permute-start.3 = (bf16[128,256]{1,0:T(8,128)(2,1)S(1)}, bf16[128,256]{1,0:T(8,128)(2,1)S(1)}, u32[]{:S(2)}, u32[]{:S(2)}) collective-permute-start(bf16[128,256]{1,0:T(8,128)(2,1)S(1)} %get-tuple-element.42), channel_id=1, source_target_pairs={{0,64},{1,65},{2,66},{3,67},{4,68},{5,69},{6,70},{7,71},{8,72},{9,... | collective-permute-start | bytes 196616 | tf_op jit(solution)/shard_map/ppermute | solution.py:358
  23.9 9.2 %collective-permute-start.4 = (bf16[128,256]{1,0:T(8,128)(2,1)S(1)}, bf16[128,256]{1,0:T(8,128)(2,1)S(1)}, u32[]{:S(2)}, u32[]{:S(2)}) collective-permute-start(bf16[128,256]{1,0:T(8,128)(2,1)S(1)} %get-tuple-element.42), channel_id=1, source_target_pairs={{0,192},{1,193},{2,194},{3,195},{4,196},{5,197},{6,198},{7,199},{8... | collective-permute-start | bytes 196616 | tf_op jit(solution)/shard_map/ppermute | solution.py:358
  28.9 11.5 %collective-permute-start.6 = (bf16[1024,512]{1,0:T(8,128)(2,1)S(1)}, bf16[1024,512]{1,0:T(8,128)(2,1)S(1)}, u32[]{:S(2)}, u32[]{:S(2)}) collective-permute-start(bf16[1024,512]{1,0:T(8,128)(2,1)S(1)} %get-tuple-element.52), channel_id=1, source_target_pairs={{0,32},{32,0},{1,33},{33,1},{2,34},{34,2},{3,35},{35,3},{4,36},{36... | collective-permute-start | bytes 3145736 | tf_op jit(solution)/shard_map/ppermute | solution.py:424
  33.1 3.0 %collective-permute-start.5 = (bf16[4,128,256]{2,1,0:T(8,128)(2,1)S(1)}, bf16[4,128,256]{2,1,0:T(8,128)(2,1)S(1)}, u32[]{:S(2)}, u32[]{:S(2)}) collective-permute-start(bf16[4,128,256]{2,1,0:T(8,128)(2,1)S(1)} %shard_map.108.oz_ref), channel_id=1, source_target_pairs={{0,32},{32,0},{1,33},{33,1},{2,34},{34,2},{3,35},{35,3},{4,36},{36... | collective-permute-start | bytes 786440 | tf_op jit(solution)/shard_map/ppermute | solution.py:423
  37.7 2.6 %collective-permute-start.7 = (bf16[512,512]{1,0:T(8,128)(2,1)S(1)}, bf16[512,512]{1,0:T(8,128)(2,1)S(1)}, u32[]{:S(2)}, u32[]{:S(2)}) collective-permute-start(bf16[512,512]{1,0:T(8,128)(2,1)S(1)} %get-tuple-element.53), channel_id=1, source_target_pairs={{0,32},{32,0},{1,33},{33,1},{2,34},{34,2},{3,35},{35,3},{4,36},{36... | collective-permute-start | bytes 1572872 | tf_op jit(solution)/shard_map/ppermute | solution.py:431
